TPU v7x, 512 devices: a whole 4x8x8 slice. The times are simulated.
512 devices in a mesh: row: 64 (over y_hi, z, x), col: 8 (over y_lo, core).
Axes of the slice: x: 4, y: 8 (y_hi: 2, y_lo: 4; y = y_hi * 4 + y_lo), z: 8, core: 2. Of those that a mesh axis runs over, the one named last changes fastest.
Arguments:
- pair_field: bfloat16 [384, 384, 128], P('row', 'col'), may hold values from -6 to 6
- proj_weight: bfloat16 [2, 128, 640], replicated, may hold values from -0.5 to 0.5
- out_weight: bfloat16 [2, 128, 128], replicated, may hold values from -0.5 to 0.5
- in_gain: float32 [2, 128], replicated, may hold values from 0.1 to 1.9
- out_gain: float32 [2, 128], replicated, may hold values from 0.1 to 1.9
Outputs:
- updated_pair: bfloat16 [384, 384, 128], P('row', 'col')
All inputs are finite; a program needn't handle non-finite values.
Results may differ from a plain program's by a relative error of at most 0.022.
Values may be sent and summed in bfloat16 or wider, within the bound.
No kernel may reach another device: no remote copies, remote signals or barrier semaphores. Data moves between devices by JAX's collectives and lax.ppermute only.
A program may use at most 64 MiB of HBM per device.

v0:
```python
import jax
import jax.numpy as jnp
from jax import lax
from jax.sharding import PartitionSpec as P

HIDDEN_SIZE = 128


def normalize(values, gain):
    mean = jnp.mean(values, axis=-1, keepdims=True)
    centred = values - mean
    spread = jnp.mean(centred * centred, axis=-1, keepdims=True)
    return centred * lax.rsqrt(spread + 1e-05) * gain


def prepare(field, weight, gain):
    widened = field.astype(jnp.float32)
    normed = normalize(widened, gain).astype(jnp.bfloat16)
    projected = jnp.einsum("ijc,cd->ijd", normed, weight, preferred_element_type=jnp.float32)
    left_side = (
        jax.nn.sigmoid(projected[..., HIDDEN_SIZE : 2 * HIDDEN_SIZE]) * projected[..., :HIDDEN_SIZE]
    ).astype(jnp.bfloat16)
    right_side = (
        jax.nn.sigmoid(projected[..., 3 * HIDDEN_SIZE : 4 * HIDDEN_SIZE])
        * projected[..., 2 * HIDDEN_SIZE : 3 * HIDDEN_SIZE]
    ).astype(jnp.bfloat16)
    gating = jax.nn.sigmoid(projected[..., 4 * HIDDEN_SIZE :])
    return (widened, left_side, right_side, gating)


def finish(widened, summed, gating, weight, gain):
    mixed = normalize(summed, gain).astype(jnp.bfloat16)
    update = gating * jnp.einsum("ijh,hc->ijc", mixed, weight, preferred_element_type=jnp.float32)
    return (widened + update).astype(jnp.bfloat16)


def shards(pair_field, proj_weight, out_weight, in_gain, out_gain):
    widened, left_side, right_side, gating = prepare(pair_field, proj_weight[0], in_gain[0])
    partial_rows = jnp.einsum(
        "ikh,jkh->ijh",
        left_side,
        lax.all_gather(right_side, "row", axis=0, tiled=True),
        preferred_element_type=jnp.float32,
    )
    summed = lax.psum_scatter(
        partial_rows.astype(jnp.bfloat16), "col", scatter_dimension=1, tiled=True
    ).astype(jnp.float32)
    first_pair = finish(widened, summed, gating, out_weight[0], out_gain[0])
    widened, left_side, right_side, gating = prepare(first_pair, proj_weight[1], in_gain[1])
    col_width = left_side.shape[1]
    left_whole, right_whole = (
        lax.all_gather(left_side, "col", axis=1, tiled=True),
        lax.all_gather(right_side, "col", axis=1, tiled=True),
    )
    left_turned, right_turned = (
        lax.all_to_all(left_whole, "row", split_axis=1, concat_axis=0, tiled=True),
        lax.all_to_all(right_whole, "row", split_axis=1, concat_axis=0, tiled=True),
    )
    offset = lax.axis_index("col") * col_width
    left_rows = jnp.transpose(
        lax.dynamic_slice_in_dim(left_turned, offset, col_width, 0), (1, 0, 2)
    )
    right_rows = jnp.transpose(
        lax.dynamic_slice_in_dim(right_turned, offset, col_width, 0), (1, 0, 2)
    )
    partial_rows = jnp.einsum(
        "ikh,jkh->ijh",
        left_rows,
        lax.all_gather(right_rows, "row", axis=0, tiled=True),
        preferred_element_type=jnp.float32,
    )
    summed = lax.psum_scatter(
        partial_rows.astype(jnp.bfloat16), "col", scatter_dimension=1, tiled=True
    ).astype(jnp.float32)
    return finish(widened, summed, gating, out_weight[1], out_gain[1])


def solution(mesh):
    placed = (P("row", "col", None), P(), P(), P(), P())
    return jax.shard_map(
        shards, mesh=mesh, in_specs=placed, out_specs=P("row", "col", None), check_vma=False
    )
```

profile of v0, /device:TPU:1, one launch (start us, length us, event | category | flops | bytes accessed | tf_op | source)
XLA Modules:
  0.0 531.9 jit_solution(6058046149555919809)
XLA Ops:
  6.5 1.0 convert_reduce_fusion.2
  7.5 1.1 fusion.25
  8.6 0.8 slice_bitcast_fusion.1
  9.4 1.3 fusion.21
  10.7 0.7 fusion.39
  11.4 0.2 copy.57
  11.7 159.4 %all-gather.3.cloned.1.call-done = bf16[384,48,128]{2,1,0:T(8,128)(2,1)} async-done(((bf16[6,48,128]{2,1,0:T(8,128)(2,1)}), bf16[384,48,128]{2,1,0:T(8,128)(2,1)}) %all-gather.3.cloned.1.call-update) | async-done | bytes 4718608 | tf_op jit(solution)/shard_map/all_gather | solution.py:42
  171.1 17.9 %copy.56 = bf16[384,48,128]{1,0,2:T(8,128)(2,1)} copy(bf16[384,48,128]{2,1,0:T(8,128)(2,1)} %all-gather.3.cloned.1.call-done) | data formatting | bytes 9437184 | tf_op jit(solution)/shard_map/all_gather | solution.py:42
  189.0 9.1 %fusion = bf16[6,384,128]{1,0,2:T(8,128)(2,1)S(1)} fusion(bf16[384,48,128]{1,0,2:T(8,128)(2,1)} %copy.56, bf16[6,48,128]{1,0,2:T(8,128)(2,1)S(1)} %copy.57), kind=kOutput, calls=%fused_computation.2 | convolution fusion | flops 28606464 | bytes 5382144 | tf_op jit(solution)/shard_map/ikh,jkh->ijh/dot_general | solution.py:39
  198.0 1.6 copy.58
  199.7 36.6 %reduce-scatter.3.cloned.1.call-done = bf16[6,48,128]{2,0,1:T(8,128)(2,1)} async-done(((bf16[6,384,128]{2,0,1:T(8,128)(2,1)}), bf16[6,48,128]{2,0,1:T(8,128)(2,1)}) %reduce-scatter.3.cloned.1.call-update) | async-done | bytes 73744 | tf_op jit(solution)/shard_map/reduce_scatter | solution.py:45
  236.3 1.0 convert_reduce_fusion.1
  237.3 0.1 copy.59
  237.4 0.1 copy.60
  237.5 1.1 fusion.14
  238.6 0.1 copy.61
  238.7 0.1 copy.62
  238.8 1.1 fusion.16
  239.9 0.3 fusion.63
  240.2 0.2 multiply_reduce_fusion
  240.4 0.3 fusion.19
  240.7 0.1 fusion.28
  240.8 17.8 %all_gather.13 = bf16[6,384,128]{2,1,0:T(8,128)(2,1)S(1)} all-gather(bf16[6,48,128]{2,1,0:T(8,128)(2,1)S(1)} %get-tuple-element.6), channel_id=1, replica_groups=mesh['row'=64,'col'=8] {'col'}, dimensions={1}, use_global_device_ids=true | all-gather | bytes 663552 | tf_op jit(solution)/shard_map/all_gather | solution.py:53
  258.6 1.3 copy.64
  259.9 12.7 %all-to-all-start = ((bf16[6,384,128]{2,0,1:T(8,128)(2,1)}), bf16[6,384,128]{2,0,1:T(8,128)(2,1)S(1)}, u32[]{:S(2)}, u32[]{:S(2)}) async-start(bf16[6,384,128]{2,0,1:T(8,128)(2,1)} %copy.64), calls=%async_computation.1 | async-start | bytes 1572864 | tf_op jit(solution)/shard_map/all_to_all | solution.py:57
  272.6 22.5 %all-to-all-done = bf16[6,384,128]{2,0,1:T(8,128)(2,1)S(1)} async-done(((bf16[6,384,128]{2,0,1:T(8,128)(2,1)}), bf16[6,384,128]{2,0,1:T(8,128)(2,1)S(1)}, u32[]{:S(2)}, u32[]{:S(2)}) %all-to-all-start) | async-done | bytes 589856 | tf_op jit(solution)/shard_map/all_to_all | solution.py:57
  295.1 0.1 copy.66
  295.2 0.2 all_to_all.29
  295.5 0.6 dynamic-slice_bitcast_fusion
  296.2 19.7 %all_gather.15 = bf16[6,384,128]{2,1,0:T(8,128)(2,1)S(1)} all-gather(bf16[6,48,128]{2,1,0:T(8,128)(2,1)S(1)} %get-tuple-element.5), channel_id=1, replica_groups=mesh['row'=64,'col'=8] {'col'}, dimensions={1}, use_global_device_ids=true | all-gather | bytes 663552 | tf_op jit(solution)/shard_map/all_gather | solution.py:52
  315.9 0.4 copy.67
  316.3 29.3 %all_to_all.36 = bf16[6,384,128]{2,0,1:T(8,128)(2,1)S(1)} all-to-all(bf16[6,384,128]{2,0,1:T(8,128)(2,1)S(1)} %copy.67), channel_id=1, replica_groups=mesh['row'=64,'col'=8] {'row'}, dimensions={1} | all-to-all | bytes 1179648 | tf_op jit(solution)/shard_map/all_to_all | solution.py:56
  345.6 0.1 copy.69
  345.7 0.2 all_to_all.33
  346.0 0.2 copy.82
  346.2 109.5 %all-gather.5.cloned.1.call-done = bf16[384,48,128]{2,1,0:T(8,128)(2,1)} async-done(((bf16[6,48,128]{2,1,0:T(8,128)(2,1)}), bf16[384,48,128]{2,1,0:T(8,128)(2,1)}) %all-gather.5.cloned.1.call-update) | async-done | bytes 4718608 | tf_op jit(solution)/shard_map/all_gather | solution.py:69
  455.7 17.9 %copy.71 = bf16[384,48,128]{1,0,2:T(8,128)(2,1)} copy(bf16[384,48,128]{2,1,0:T(8,128)(2,1)} %all-gather.5.cloned.1.call-done) | data formatting | bytes 9437184 | tf_op jit(solution)/shard_map/all_gather | solution.py:69
  473.6 9.0 %fusion.1 = bf16[6,384,128]{1,0,2:T(8,128)(2,1)S(1)} fusion(bf16[384,48,128]{1,0,2:T(8,128)(2,1)} %copy.71, bf16[48,6,128]{0,1,2:T(8,128)(2,1)S(1)} %copy.82), kind=kOutput, calls=%fused_computation.3 | convolution fusion | flops 28606464 | bytes 5382144 | tf_op jit(solution)/shard_map/ikh,jkh->ijh/dot_general | solution.py:66
  482.6 1.6 copy.72
  484.2 36.9 %reduce-scatter.5.cloned.1.call-done = bf16[6,48,128]{2,0,1:T(8,128)(2,1)} async-done(((bf16[6,384,128]{2,0,1:T(8,128)(2,1)}), bf16[6,48,128]{2,0,1:T(8,128)(2,1)}) %reduce-scatter.5.cloned.1.call-update) | async-done | bytes 73744 | tf_op jit(solution)/shard_map/reduce_scatter | solution.py:72
  521.1 1.0 convert_reduce_fusion
  522.1 0.1 copy.73
  522.2 0.1 copy.74
  522.3 1.1 fusion.11
  523.4 0.1 copy.75
  523.4 0.1 copy.76
  523.5 1.1 fusion.13
  524.6 0.8 fusion.5
  (26 shorter events, 0.3 us)
Async XLA Ops:
  6.5 164.5 %all-gather.3.cloned.1.call-start = ((), (), s32[]{:S(2)}) async-start(), calls=%async_computation.4 | async-start | bytes 4792320 | tf_op jit(solution)/shard_map/all_gather | solution.py:42
  11.4 224.9 %reduce-scatter.3.cloned.1.call-start = ((), (), s32[]{:S(2)}) async-start(), calls=%async_computation.5 | async-start | bytes 884736 | tf_op jit(solution)/shard_map/reduce_scatter | solution.py:45
  11.6 188.0 %copy-start.2 = (f32[2,128]{1,0:T(2,128)S(1)}, f32[2,128]{1,0:T(2,128)}, u32[]{:S(2)}) copy-start(f32[2,128]{1,0:T(2,128)} %param.9) | copy-start | bytes 3076
  189.0 50.9 %copy-start = (bf16[6,48,128]{2,1,0:T(8,128)(2,1)S(1)}, bf16[6,48,128]{2,1,0:T(8,128)(2,1)}, u32[]{:S(2)}) copy-start(bf16[6,48,128]{2,1,0:T(8,128)(2,1)} %param.5) | copy-start | bytes 221188
  189.0 50.9 %copy-start.3 = (bf16[2,128,128]{2,1,0:T(8,128)(2,1)S(1)}, bf16[2,128,128]{2,1,0:T(8,128)(2,1)}, u32[]{:S(2)}) copy-start(bf16[2,128,128]{2,1,0:T(8,128)(2,1)} %param.7) | copy-start | bytes 196612
  189.0 51.4 %copy-start.1 = (bf16[2,128,640]{2,1,0:T(8,128)(2,1)S(1)}, bf16[2,128,640]{2,1,0:T(8,128)(2,1)}, u32[]{:S(2)}) copy-start(bf16[2,128,640]{2,1,0:T(8,128)(2,1)} %param.6) | copy-start | bytes 983044
  259.9 35.2 %all-to-all-start = ((bf16[6,384,128]{2,0,1:T(8,128)(2,1)}), bf16[6,384,128]{2,0,1:T(8,128)(2,1)S(1)}, u32[]{:S(2)}, u32[]{:S(2)}) async-start(bf16[6,384,128]{2,0,1:T(8,128)(2,1)} %copy.64), calls=%async_computation.1 | async-start | bytes 1572864 | tf_op jit(solution)/shard_map/all_to_all | solution.py:57
  272.5 183.2 %all-gather.5.cloned.1.call-start = ((), (), s32[]{:S(2)}) async-start(), calls=%async_computation.6 | async-start | bytes 4792320 | tf_op jit(solution)/shard_map/all_gather | solution.py:69
  296.1 224.9 %reduce-scatter.5.cloned.1.call-start = ((), (), s32[]{:S(2)}) async-start(), calls=%async_computation.7 | async-start | bytes 884736 | tf_op jit(solution)/shard_map/reduce_scatter | solution.py:72
Sparse Core Ops, SparseCore 0:
  11.9 159.0 all-gather.2
  199.8 36.5 reduce-scatter.2
  296.3 159.3 all-gather.4
  484.3 36.6 reduce-scatter.4
where the time goes:
time: 534 us; the launch traced here: 532 us
  waiting for transfers between devices  365 us (68%)
  blocking collectives  66.8 us (13%)
  local copies, waits for them, and re-layouts  43.9 us (8%)
  matrix products  20.7 us (4%)
  between operations  13.4 us (3%)
  starting transfers between devices  12.8 us (2%)
  other arithmetic  9.45 us (2%)
    all_gather x1, waiting for transfers between devices, shards(): lax.all_gather(right_side, 'row', axis=0, tiled=True)  159 us
    all_gather x1, waiting for transfers between devices, shards(): lax.all_gather(right_rows, 'row', axis=0, tiled=True)  110 us
    reduce_scatter x2, waiting for transfers between devices, shards(): lax.psum_scatter(partial_rows.astype(jnp.bfloat16), 'col', scatter_dimens...  73.5 us
    all_to_all x1, blocking collectives, shards(): lax.all_to_all(left_whole, 'row', split_axis=1, concat_axis=0, tiled=True)  29.3 us
    all_to_all x1, waiting for transfers between devices, shards(): lax.all_to_all(right_whole, 'row', split_axis=1, concat_axis=0, tiled=True)  22.5 us
    all_gather x1, blocking collectives, shards(): lax.all_gather(left_side, 'col', axis=1, tiled=True)  19.7 us
    all_gather x1, local copies, waits for them, and re-layouts, shards(): lax.all_gather(right_side, 'row', axis=0, tiled=True)  17.9 us
    all_gather x1, local copies, waits for them, and re-layouts, shards(): lax.all_gather(right_rows, 'row', axis=0, tiled=True)  17.9 us
  transfers between devices with their start and end apart: 5, of which 5 were waited for; matrix products, arithmetic and copies ran while one was open for 0% of the time, Pallas kernels for 0%

commit v1 on v0

v1 whole, which is shorter than its diff:
```python
import functools

import jax
import jax.numpy as jnp
import numpy as np
from jax import lax
from jax.experimental import pallas as pl
from jax.experimental.pallas import tpu as pltpu
from jax.sharding import Mesh
from jax.sharding import PartitionSpec as P

H = 128
HALF = 64
SPREAD = ("yl", "core", "yh", "x")
F32 = jnp.float32
BF16 = jnp.bfloat16


def normalize(values, gain, axis):
    mean = jnp.mean(values, axis=axis, keepdims=True)
    centred = values - mean
    spread = jnp.mean(centred * centred, axis=axis, keepdims=True)
    return centred * lax.rsqrt(spread + 1e-05) * gain


def swap(tile):
    return pltpu.roll(tile, HALF, 1)


def lower(shape):
    return lax.broadcasted_iota(jnp.int32, shape, 1) < HALF


def halves(top, bottom):
    low = lower(top.shape)
    return jnp.where(low, top, swap(bottom)), jnp.where(low, swap(top), bottom)


def widen_groups(values, scratch):
    rows = values.shape[0]
    scratch[0:rows, :] = values
    keep = lax.broadcasted_iota(jnp.int32, (8, H), 0) < 6
    return jnp.concatenate(
        [jnp.where(keep, scratch[6 * n : 6 * n + 8, :], 0.0) for n in range(rows // 6)], axis=0
    )


def spread_sides(normed, weight):
    projected = lax.dot_general(
        weight[:, : 4 * H], normed, (((0,), (1,)), ((), ())), preferred_element_type=F32
    )
    rows = []
    for side in range(2):
        value = projected[2 * side * H : (2 * side + 1) * H]
        gate = projected[(2 * side + 1) * H : (2 * side + 2) * H]
        turned = jax.nn.sigmoid(gate) * value
        for t in range(3):
            tile = turned[:, t * H : (t + 1) * H]
            rows.extend(halves(tile[:HALF], tile[HALF:]))
        rows.extend([jnp.zeros((HALF, H), F32)] * 2)
    return jnp.swapaxes(jnp.stack(rows, axis=0), 0, 1).astype(BF16)


def gate_of(normed, weight):
    return jax.nn.sigmoid(jnp.dot(normed, weight[:, 4 * H :], preferred_element_type=F32))


def finish(arrived, field, gating, weight, gain):
    by_row = jnp.swapaxes(arrived.astype(F32), 0, 1)
    tiles = []
    for t in range(3):
        tiles.append(jnp.concatenate(halves(by_row[2 * t], by_row[2 * t + 1]), axis=0))
    summed = jnp.concatenate(tiles, axis=1)
    mixed = normalize(summed, gain, 0).astype(BF16)
    update = lax.dot_general(
        mixed, weight, (((0,), (0,)), ((), ())), preferred_element_type=F32
    )
    return field + gating * update


def send_back(product, out_ref):
    for u in range(4):
        tile = product[:, u * H : (u + 1) * H]
        for e, part in enumerate(halves(tile[:HALF], tile[HALF:])):
            c = 2 * u + e
            out_ref[c * 8 : (c + 1) * 8] = part.reshape(8, 8, H).astype(BF16)


def start_kernel(pair_ref, weight_ref, gain_ref, out_ref, field_ref, gate_ref, scratch):
    field = widen_groups(pair_ref[...].reshape(288, H).astype(F32), scratch)
    normed = normalize(field, gain_ref[...], 1).astype(BF16)
    weight = weight_ref[...]
    out_ref[...] = spread_sides(normed, weight)
    field_ref[...] = field
    gate_ref[...] = gate_of(normed, weight)


def outgoing_kernel(own_ref, right_ref, out_ref):
    left = own_ref[:, 0:8, :].astype(F32).reshape(8, HALF, H)
    low = lower((HALF, H))
    left_all, right_all = [], []
    for c in range(8):
        part = left[c]
        left_all.append(
            jnp.concatenate([jnp.where(low, part, 0.0), jnp.where(low, 0.0, part)], axis=0).astype(BF16)
        )
        right = right_ref[:, c * 8 : (c + 1) * 8].astype(F32)
        right_all.append(
            jnp.concatenate([right[:, :4].reshape(256, H), right[:, 4:].reshape(256, H)], axis=0).astype(BF16)
        )
    product = lax.dot_general(
        jnp.concatenate(left_all, axis=1),
        jnp.concatenate(right_all, axis=1),
        (((1,), (1,)), ((), ())),
        preferred_element_type=F32,
    )
    send_back(product, out_ref)


def middle_kernel(
    arrived_ref, field_ref, gate_ref, out_weight_ref, out_gain_ref, weight_ref, gain_ref, out_ref, first_ref, next_gate_ref
):
    first = finish(
        arrived_ref[...], field_ref[...], gate_ref[...], out_weight_ref[...], out_gain_ref[...]
    ).astype(BF16).astype(F32)
    normed = normalize(first, gain_ref[...], 1).astype(BF16)
    weight = weight_ref[...]
    out_ref[...] = spread_sides(normed, weight)
    first_ref[...] = first
    next_gate_ref[...] = gate_of(normed, weight)


def incoming_kernel(own_ref, squeeze_ref, out_ref):
    sides = []
    for side in range(2):
        part = own_ref[:, side * 8 : side * 8 + 8, :].astype(F32).reshape(8, HALF, H)
        tiles = [halves(part[2 * u], part[2 * u + 1]) for u in range(4)]
        for channel in range(2):
            sides.append(jnp.concatenate([tile[channel] for tile in tiles], axis=1))
    packed = jnp.dot(
        jnp.concatenate(sides, axis=0).astype(BF16), squeeze_ref[...], preferred_element_type=F32
    ).astype(BF16)
    for channel in range(2):
        left = packed[channel * HALF : (channel + 1) * HALF]
        right = packed[(2 + channel) * HALF : (3 + channel) * HALF]
        product = lax.dot_general(
            left, right, (((0,), (0,)), ((), ())), preferred_element_type=F32
        )
        out_ref[:, channel] = product.reshape(8, 48, 384).astype(BF16)


def sum_kernel(parts_ref, stretch_ref, out_ref, scratch):
    products = []
    for channel in range(2):
        total = parts_ref[0, channel].astype(F32)
        for z in range(1, 8):
            total = total + parts_ref[z, channel].astype(F32)
        wide = jnp.concatenate(
            [widen_groups(total[:, t * H : (t + 1) * H], scratch.at[3 * channel + t]) for t in range(3)], axis=1
        )
        products.append(wide.astype(BF16))
    send_back(
        jnp.dot(jnp.concatenate(products, axis=0), stretch_ref[...], preferred_element_type=F32), out_ref
    )


def end_kernel(arrived_ref, field_ref, gate_ref, out_weight_ref, out_gain_ref, out_ref, scratch):
    final = finish(
        arrived_ref[...], field_ref[...], gate_ref[...], out_weight_ref[...], out_gain_ref[...]
    )
    for n in range(48):
        scratch[6 * n : 6 * n + 8, :] = final[8 * n : 8 * n + 8]
    out_ref[...] = scratch[0:288, :].reshape(6, 48, H).astype(BF16)


def squeeze_matrix():
    places = np.arange(512).reshape(2, 8, 4, 8)[..., :6].transpose(1, 0, 2, 3).reshape(-1)
    return (np.arange(512)[:, None] == places[None, :]).astype(jnp.bfloat16)


def call(kernel, outs, scratch=(), cost=20_000_000):
    return pl.pallas_call(
        kernel,
        out_shape=[jax.ShapeDtypeStruct(shape, dtype) for shape, dtype in outs],
        scratch_shapes=list(scratch),
        compiler_params=pltpu.CompilerParams(vmem_limit_bytes=48 * 1024 * 1024),
        cost_estimate=pl.CostEstimate(flops=cost, bytes_accessed=1_000_000, transcendentals=100_000),
    )


def shards(pair_field, proj_weight, out_weight, in_gain, out_gain):
    exchange = functools.partial(lax.all_to_all, split_axis=0, concat_axis=0, tiled=True)
    squeeze = squeeze_matrix()
    wide, narrow = (384, H), (64, 8, H)

    sides, field, gating = call(
        start_kernel, [((64, 16, H), BF16), (wide, F32), (wide, F32)], [pltpu.VMEM((296, H), F32)]
    )(pair_field, proj_weight[0], in_gain[0][None])
    own = exchange(sides, SPREAD)
    right = lax.all_gather(own[:, 8:], "z", axis=0, tiled=False)
    [back] = call(outgoing_kernel, [(narrow, BF16)])(own, right)
    arrived = exchange(back, SPREAD)

    sides, field, gating = call(
        middle_kernel, [((64, 16, H), BF16), (wide, F32), (wide, F32)]
    )(arrived, field, gating, out_weight[0], out_gain[0][:, None], proj_weight[1], in_gain[1][None])
    own = exchange(sides, SPREAD)
    [parts] = call(incoming_kernel, [((8, 2, 48, 384), BF16)])(own, jnp.asarray(squeeze))
    parts = exchange(parts, "z")
    [back] = call(sum_kernel, [(narrow, BF16)], [pltpu.VMEM((6, 56, H), F32)])(
        parts, jnp.asarray(squeeze.T)
    )
    arrived = exchange(back, SPREAD)
    [out] = call(end_kernel, [((6, 48, H), BF16)], [pltpu.VMEM((296, H), F32)])(
        arrived, field, gating, out_weight[1], out_gain[1][:, None]
    )
    return out


def solution(mesh):
    fine = Mesh(mesh.devices.reshape(2, 8, 4, 4, 2), ("yh", "z", "x", "yl", "core"))
    row, col = ("yh", "z", "x"), ("yl", "core")
    return jax.shard_map(
        shards,
        mesh=fine,
        in_specs=(P(row, col, None), P(), P(), P(), P()),
        out_specs=P(row, col, None),
        check_vma=False,
    )
```

time: 534 us -> 164 us (0.31)
  waiting for transfers between devices: 365 us -> 56.4 us
  local copies, waits for them, and re-layouts: 43.9 us -> 3.92 us
  matrix products: 20.7 us -> 0 us
  starting transfers between devices: 12.8 us -> 24 us
  other arithmetic: 9.45 us -> 0 us
  blocking collectives: 66.8 us -> 60.7 us
  Pallas kernels: 0 us -> 5.49 us
    all_gather x2 -> x1, waiting for transfers between devices: 269 us -> 37.2 us  [shards(): right = lax.all_gather(own[:, 8:], 'z', axis=0, tiled=False)]
    reduce_scatter x2 -> x0, waiting for transfers between devices: 73.5 us -> none  [shards(): lax.psum_scatter(partial_rows.astype(jnp.bfloat16), 'col', scatter_dimens...]
    all_gather x4 -> x0, local copies, waits for them, and re-layouts: 37.5 us -> none  [the longest x1 17.9 us: shards(): lax.all_gather(right_side, 'row', axis=0, tiled=True)]
    all_gather x2 -> x0, blocking collectives: 37.5 us -> none  [the longest x1 19.7 us: shards(): lax.all_gather(left_side, 'col', axis=1, tiled=True)]
    all_to_all x1 -> x3, blocking collectives: 29.3 us -> 60.7 us  [the longest x2 41.2 us: shards(): own = exchange(sides, SPREAD)]
    dot_general x6 -> x0, matrix products: 20.7 us -> none  [the longest x1 9.06 us: shards(): jnp.einsum('ikh,jkh->ijh', left_side, lax.all_gather(right_side, 'row', a...]
    all_to_all x1 -> x2, starting transfers between devices: 12.7 us -> 24 us  [shards(): arrived = exchange(back, SPREAD)]
    reduce_sum x7 -> x0, other arithmetic: 6.45 us -> none  [the longest x4 3.43 us: normalize(): spread = jnp.mean(centred * centred, axis=-1, keepdims=True)]
  transfers between devices with their start and end apart: 5 -> 3, of which waited for: 5 -> 3; matrix products, arithmetic and copies ran while one was open for 0% -> 0% of each run, Pallas kernels for 0% -> 0%
where the time goes in v1:
time: 164 us
  blocking collectives  60.7 us (37%)
  waiting for transfers between devices  56.4 us (34%)
  starting transfers between devices  24 us (15%)
  between operations  13.5 us (8%)
  Pallas kernels  5.49 us (3%)
  local copies, waits for them, and re-layouts  3.92 us (2%)
    all_to_all x2, blocking collectives, shards(): own = exchange(sides, SPREAD)  41.2 us
    all_gather x1, waiting for transfers between devices, shards(): right = lax.all_gather(own[:, 8:], 'z', axis=0, tiled=False)  37.2 us
    all_to_all x2, starting transfers between devices, shards(): arrived = exchange(back, SPREAD)  24 us
    all_to_all x1, blocking collectives, shards(): parts = exchange(parts, 'z')  19.5 us
    all_to_all x2, waiting for transfers between devices, shards(): arrived = exchange(back, SPREAD)  19.2 us
  transfers between devices with their start and end apart: 3, of which 3 were waited for; matrix products, arithmetic and copies ran while one was open for 0% of the time, Pallas kernels for 0%

profile of v1, /device:TPU:1, one launch (start us, length us, event | category | flops | bytes accessed | tf_op | source)
XLA Modules:
  0.0 164.0 jit_solution(14172234749092494140)
XLA Ops:
  6.5 0.0 copy-start.5
  6.5 0.0 copy-start.3
  6.5 0.0 all-gather.3.cloned.1.call-start
  6.5 1.1 slice_bitcast_fusion
  7.6 0.0 copy-done.5
  7.6 0.0 copy-done.3
  7.6 0.6 shard_map.73
  8.2 23.8 %all_to_all.25.own_ref = bf16[64,16,128]{2,1,0:T(8,128)(2,1)S(1)} all-to-all(bf16[64,16,128]{2,1,0:T(8,128)(2,1)S(1)} %get-tuple-element.11), channel_id=1, replica_groups=mesh['yh'=2,'z'=8,'x'=4,'yl'=4,'core'=2] {'yl','core','yh','x'}, dimensions={0} | all-to-all | bytes 524288 | tf_op jit(solution)/shard_map/all_to_all | solution.py:199
  32.1 0.7 slice.36
  32.7 0.0 all-gather.3.cloned.1.call-update
  32.8 37.2 %all-gather.3.cloned.1.call-done = bf16[512,8,128]{2,1,0:T(8,128)(2,1)} async-done(((bf16[64,8,128]{2,1,0:T(8,128)(2,1)}), bf16[512,8,128]{2,1,0:T(8,128)(2,1)}) %all-gather.3.cloned.1.call-update) | async-done | bytes 1048592 | tf_op jit(solution)/shard_map/all_gather | solution.py:200
  69.9 0.0 copy-start
  70.0 1.2 copy-done
  71.2 1.2 shard_map.74
  72.4 0.0 copy-start.6
  72.4 15.1 %all-to-all-start.1 = ((bf16[64,8,128]{2,1,0:T(8,128)(2,1)}), bf16[64,8,128]{2,1,0:T(8,128)(2,1)S(1)}, u32[]{:S(2)}, u32[]{:S(2)}) async-start(bf16[64,8,128]{2,1,0:T(8,128)(2,1)} %shard_map.74), calls=%async_computation.1 | async-start | bytes 262144 | tf_op jit(solution)/shard_map/all_to_all | solution.py:202
  87.5 0.0 copy-done.6
  87.5 0.0 copy-start.4
  87.5 0.1 copy.10.out_gain_ref
  87.6 0.7 copy-done.4
  88.3 9.2 %all-to-all-done.1.arrived_ref = bf16[64,8,128]{2,1,0:T(8,128)(2,1)S(1)} async-done(((bf16[64,8,128]{2,1,0:T(8,128)(2,1)}), bf16[64,8,128]{2,1,0:T(8,128)(2,1)S(1)}, u32[]{:S(2)}, u32[]{:S(2)}) %all-to-all-start.1) | async-done | bytes 131104 | tf_op jit(solution)/shard_map/all_to_all | solution.py:202
  97.5 1.0 shard_map.75
  98.6 0.0 copy-start.1
  98.6 17.4 %all_to_all.26.own_ref = bf16[64,16,128]{2,1,0:T(8,128)(2,1)S(1)} all-to-all(bf16[64,16,128]{2,1,0:T(8,128)(2,1)S(1)} %get-tuple-element.14), channel_id=1, replica_groups=mesh['yh'=2,'z'=8,'x'=4,'yl'=4,'core'=2] {'yl','core','yh','x'}, dimensions={0} | all-to-all | bytes 524288 | tf_op jit(solution)/shard_map/all_to_all | solution.py:207
  116.0 0.0 copy-done.1
  116.0 0.6 shard_map.76
  116.6 0.0 copy-start.2
  116.6 19.5 %all_to_all.27.parts_ref = bf16[8,2,48,384]{3,2,1,0:T(8,128)(2,1)S(1)} all-to-all(bf16[8,2,48,384]{3,2,1,0:T(8,128)(2,1)S(1)} %shard_map.76), channel_id=1, replica_groups=mesh['yh'=2,'z'=8,'x'=4,'yl'=4,'core'=2] {'z'}, dimensions={0} | all-to-all | bytes 1179648 | tf_op jit(solution)/shard_map/all_to_all | solution.py:209
  136.1 0.0 copy-done.2
  136.1 1.0 shard_map.77
  137.1 8.9 %all-to-all-start.4 = ((bf16[64,8,128]{2,1,0:T(8,128)(2,1)}), bf16[64,8,128]{2,1,0:T(8,128)(2,1)S(1)}, u32[]{:S(2)}, u32[]{:S(2)}) async-start(bf16[64,8,128]{2,1,0:T(8,128)(2,1)} %shard_map.77), calls=%async_computation.4 | async-start | bytes 262144 | tf_op jit(solution)/shard_map/all_to_all | solution.py:213
  146.0 0.1 copy.11.out_gain_ref
  146.2 10.0 %all-to-all-done.4.arrived_ref = bf16[64,8,128]{2,1,0:T(8,128)(2,1)S(1)} async-done(((bf16[64,8,128]{2,1,0:T(8,128)(2,1)}), bf16[64,8,128]{2,1,0:T(8,128)(2,1)S(1)}, u32[]{:S(2)}, u32[]{:S(2)}) %all-to-all-start.4) | async-done | bytes 131104 | tf_op jit(solution)/shard_map/all_to_all | solution.py:213
  156.1 1.0 shard_map.78
  (3 shorter events, 0.0 us)
Async XLA Ops:
  6.5 1.1 copy-start.5
  6.5 1.1 copy-start.3
  6.5 63.4 %all-gather.3.cloned.1.call-start = ((), (), s32[]{:S(2)}) async-start(), calls=%async_computation.5 | async-start | bytes 1179648 | tf_op jit(solution)/shard_map/all_gather | solution.py:200
  69.9 1.2 copy-start
  72.4 15.1 %copy-start.6 = (f32[2,128]{1,0:T(2,128)S(1)}, f32[2,128]{1,0:T(2,128)}, u32[]{:S(2)}) copy-start(f32[2,128]{1,0:T(2,128)} %param.11) | copy-start | bytes 3076
  72.4 25.2 %all-to-all-start.1 = ((bf16[64,8,128]{2,1,0:T(8,128)(2,1)}), bf16[64,8,128]{2,1,0:T(8,128)(2,1)S(1)}, u32[]{:S(2)}, u32[]{:S(2)}) async-start(bf16[64,8,128]{2,1,0:T(8,128)(2,1)} %shard_map.74), calls=%async_computation.1 | async-start | bytes 262144 | tf_op jit(solution)/shard_map/all_to_all | solution.py:202
  87.5 0.8 copy-start.4
  98.6 17.4 %copy-start.1 = (bf16[512,384]{1,0:T(8,128)(2,1)S(1)}, bf16[512,384]{1,0:T(8,128)(2,1)}, u32[]{:S(2)}) copy-start(bf16[512,384]{1,0:T(8,128)(2,1)} %constant.4.clone.squeeze_ref) | copy-start | bytes 1179652
  116.6 19.5 %copy-start.2 = (bf16[384,512]{1,0:T(8,128)(2,1)S(1)}, bf16[384,512]{1,0:T(8,128)(2,1)}, u32[]{:S(2)}) copy-start(bf16[384,512]{1,0:T(8,128)(2,1)} %constant.5.clone.stretch_ref) | copy-start | bytes 1179652
  137.1 19.0 %all-to-all-start.4 = ((bf16[64,8,128]{2,1,0:T(8,128)(2,1)}), bf16[64,8,128]{2,1,0:T(8,128)(2,1)S(1)}, u32[]{:S(2)}, u32[]{:S(2)}) async-start(bf16[64,8,128]{2,1,0:T(8,128)(2,1)} %shard_map.77), calls=%async_computation.4 | async-start | bytes 262144 | tf_op jit(solution)/shard_map/all_to_all | solution.py:213
Sparse Core Ops, SparseCore 0:
  32.9 37.0 all-gather.2

commit v2 on v1

v2 whole, which is shorter than its diff:
```python
import functools

import jax
import jax.numpy as jnp
import numpy as np
from jax import lax
from jax.experimental import pallas as pl
from jax.experimental.pallas import tpu as pltpu
from jax.sharding import Mesh
from jax.sharding import PartitionSpec as P

H = 128
HALF = 64
SPREAD = ("yl", "core", "yh", "z")
F32 = jnp.float32
BF16 = jnp.bfloat16


def normalize(values, gain, axis):
    mean = jnp.mean(values, axis=axis, keepdims=True)
    centred = values - mean
    spread = jnp.mean(centred * centred, axis=axis, keepdims=True)
    return centred * lax.rsqrt(spread + 1e-05) * gain


def halves(top, bottom):
    low = lax.broadcasted_iota(jnp.int32, top.shape, 1) < HALF
    return jnp.where(low, top, pltpu.roll(bottom, HALF, 1)), jnp.where(low, pltpu.roll(top, HALF, 1), bottom)


def by_device(rows):
    return jnp.swapaxes(jnp.stack(rows, axis=0), 0, 1).astype(BF16)


def widen_groups(values, scratch):
    scratch[0:288, :] = values
    keep = lax.broadcasted_iota(jnp.int32, (8, H), 0) < 6
    return jnp.concatenate(
        [jnp.where(keep, scratch[6 * n : 6 * n + 8, :], 0.0) for n in range(48)], axis=0
    )


def spread_sides(normed, weight):
    projected = lax.dot_general(
        weight[:, : 4 * H], normed, (((0,), (1,)), ((), ())), preferred_element_type=F32
    )
    rows = []
    for side in range(2):
        value = projected[2 * side * H : (2 * side + 1) * H]
        gate = projected[(2 * side + 1) * H : (2 * side + 2) * H]
        turned = jax.nn.sigmoid(gate) * value
        rows.extend(turned[:, t * H : (t + 1) * H] for t in range(3))
        rows.append(jnp.zeros((H, H), F32))
    return by_device(rows)


def gate_of(normed, weight):
    return jax.nn.sigmoid(jnp.dot(normed, weight[:, 4 * H :], preferred_element_type=F32))


def finish(arrived, field, gating, weight, gain):
    by_row = jnp.swapaxes(arrived.astype(F32), 0, 1)
    summed = jnp.concatenate([by_row[t] for t in range(3)], axis=1)
    column = jnp.swapaxes(jnp.broadcast_to(gain, (8, H)), 0, 1)[:, :1]
    mixed = normalize(summed, column, 0).astype(BF16)
    update = lax.dot_general(
        mixed, weight, (((0,), (0,)), ((), ())), preferred_element_type=F32
    )
    return field + gating * update


def matrices(own, squeeze):
    by_row = jnp.swapaxes(own.astype(F32), 0, 1)
    rows = []
    for side in range(2):
        for t in range(3):
            part = by_row[4 * side + t]
            tiles = [
                halves(part[32 * u : 32 * u + 16], part[32 * u + 16 : 32 * u + 32]) for u in range(4)
            ]
            for e in range(2):
                rows.append(jnp.concatenate([tile[e] for tile in tiles], axis=1))
    packed = jnp.dot(
        jnp.concatenate(rows, axis=0).astype(BF16), squeeze, preferred_element_type=F32
    ).astype(BF16)
    return packed[:96], packed[96:]


def send_back(product, stretch):
    wide = jnp.dot(product.astype(BF16), stretch, preferred_element_type=F32)
    rows = []
    for t in range(3):
        parts = []
        for u in range(4):
            tile = wide[32 * t : 32 * t + 32, u * H : (u + 1) * H]
            parts.extend(halves(tile[:16], tile[16:]))
        rows.append(jnp.concatenate(parts, axis=0))
    rows.append(jnp.zeros((H, H), F32))
    return by_device(rows)


def start_kernel(pair_ref, weight_ref, gain_ref, out_ref, field_ref, gate_ref, scratch):
    field = widen_groups(pair_ref[...].reshape(288, H).astype(F32), scratch)
    normed = normalize(field, gain_ref[0:1, :], 1).astype(BF16)
    weight = weight_ref[0]
    out_ref[...] = spread_sides(normed, weight)
    field_ref[...] = field
    gate_ref[...] = gate_of(normed, weight)


def pack_kernel(own_ref, squeeze_ref, left_ref, right_ref):
    left, right = matrices(own_ref[...], squeeze_ref[...])
    left_ref[...] = left
    for x in range(4):
        right_ref[x] = right


def outgoing_kernel(left_ref, right_ref, stretch_ref, out_ref):
    product = lax.dot_general(
        left_ref[...],
        right_ref[...].reshape(384, 384),
        (((1,), (1,)), ((), ())),
        preferred_element_type=F32,
    )
    out_ref[...] = send_back(product, stretch_ref[...])


def middle_kernel(
    arrived_ref, field_ref, gate_ref, out_weight_ref, out_gain_ref, weight_ref, gain_ref, out_ref, first_ref, next_gate_ref
):
    first = finish(
        arrived_ref[...], field_ref[...], gate_ref[...], out_weight_ref[0], out_gain_ref[0:1, :]
    ).astype(BF16).astype(F32)
    normed = normalize(first, gain_ref[1:2, :], 1).astype(BF16)
    weight = weight_ref[1]
    out_ref[...] = spread_sides(normed, weight)
    first_ref[...] = first
    next_gate_ref[...] = gate_of(normed, weight)


def incoming_kernel(own_ref, squeeze_ref, out_ref):
    left, right = matrices(own_ref[...], squeeze_ref[...])
    product = lax.dot_general(
        left, right, (((0,), (0,)), ((), ())), preferred_element_type=F32
    )
    out_ref[...] = product.reshape(4, 96, 384).astype(BF16)


def sum_kernel(parts_ref, stretch_ref, out_ref):
    total = parts_ref[0].astype(F32)
    for x in range(1, 4):
        total = total + parts_ref[x].astype(F32)
    out_ref[...] = send_back(total, stretch_ref[...])


def end_kernel(arrived_ref, field_ref, gate_ref, out_weight_ref, out_gain_ref, out_ref, scratch):
    final = finish(
        arrived_ref[...], field_ref[...], gate_ref[...], out_weight_ref[1], out_gain_ref[1:2, :]
    )
    for n in range(48):
        scratch[6 * n : 6 * n + 8, :] = final[8 * n : 8 * n + 8]
    out_ref[...] = scratch[0:288, :].reshape(6, 48, H).astype(BF16)


def squeeze_matrix():
    places = np.arange(512).reshape(2, 8, 4, 8)[..., :6].transpose(2, 3, 0, 1).reshape(-1)
    return (np.arange(512)[:, None] == places[None, :]).astype(jnp.bfloat16)


def call(kernel, outs, scratch=(), cost=20_000_000):
    return pl.pallas_call(
        kernel,
        out_shape=[jax.ShapeDtypeStruct(shape, dtype) for shape, dtype in outs],
        scratch_shapes=list(scratch),
        compiler_params=pltpu.CompilerParams(vmem_limit_bytes=48 * 1024 * 1024),
        cost_estimate=pl.CostEstimate(flops=cost, bytes_accessed=1_000_000, transcendentals=100_000),
    )


def shards(pair_field, proj_weight, out_weight, in_gain, out_gain):
    exchange = functools.partial(lax.all_to_all, split_axis=0, concat_axis=0, tiled=True)
    squeeze, stretch = jnp.asarray(squeeze_matrix()), jnp.asarray(squeeze_matrix().T)
    pairs = ((384, H), F32)
    sides, results = ((H, 8, H), BF16), ((H, 4, H), BF16)
    block, blocks = ((96, 384), BF16), ((4, 96, 384), BF16)
    padded = pltpu.VMEM((296, H), F32)

    sent, field, gating = call(start_kernel, [sides, pairs, pairs], [padded])(
        pair_field, proj_weight, in_gain
    )
    own = exchange(sent, SPREAD)
    left, right = call(pack_kernel, [block, blocks])(own, squeeze)
    right = exchange(right, "x")
    [back] = call(outgoing_kernel, [results])(left, right, stretch)
    arrived = exchange(back, SPREAD)

    sent, field, gating = call(middle_kernel, [sides, pairs, pairs])(
        arrived, field, gating, out_weight, out_gain, proj_weight, in_gain
    )
    own = exchange(sent, SPREAD)
    [parts] = call(incoming_kernel, [blocks])(own, squeeze)
    parts = exchange(parts, "x")
    [back] = call(sum_kernel, [results])(parts, stretch)
    arrived = exchange(back, SPREAD)
    [out] = call(end_kernel, [((6, 48, H), BF16)], [padded])(
        arrived, field, gating, out_weight, out_gain
    )
    return out


def solution(mesh):
    fine = Mesh(mesh.devices.reshape(2, 8, 4, 4, 2), ("yh", "z", "x", "yl", "core"))
    row, col = ("yh", "z", "x"), ("yl", "core")
    return jax.shard_map(
        shards,
        mesh=fine,
        in_specs=(P(row, col, None), P(), P(), P(), P()),
        out_specs=P(row, col, None),
        check_vma=False,
    )
```

time: 164 us -> 119 us (0.73)
  waiting for transfers between devices: 56.4 us -> 0 us
  blocking collectives: 60.7 us -> 111 us
  starting transfers between devices: 24 us -> 0 us
  between operations: 13.5 us -> 0.08 us
    all_to_all x3 -> x6, blocking collectives: 60.7 us -> 111 us  [the longest x2 53.8 us: shards(): own = exchange(sent, SPREAD)]
    all_gather x1 -> x0, waiting for transfers between devices: 37.2 us -> none  [shards(): right = lax.all_gather(own[:, 8:], 'z', axis=0, tiled=False)]
    all_to_all x2 -> x0, starting transfers between devices: 24 us -> none  [shards(): arrived = exchange(back, SPREAD)]
    all_to_all x2 -> x0, waiting for transfers between devices: 19.2 us -> none  [shards(): arrived = exchange(back, SPREAD)]
    unnamed x14 -> x18, local copies, waits for them, and re-layouts: 1.96 us -> 3.28 us
    pallas_call x6 -> x7, Pallas kernels: 5.49 us -> 4.46 us  [the longest x1 1.05 us: shards(): call(end_kernel, [((6, 48, H), BF16)], [padded])]
  transfers between devices with their start and end apart: 3 -> 0, of which waited for: 3 -> 0; matrix products, arithmetic and copies ran while one was open for 0% -> 0% of each run, Pallas kernels for 0% -> 0%
where the time goes in v2:
time: 119 us
  blocking collectives  111 us (93%)
  Pallas kernels  4.46 us (4%)
  local copies, waits for them, and re-layouts  3.28 us (3%)
    all_to_all x2, blocking collectives, shards(): own = exchange(sent, SPREAD)  53.8 us
    all_to_all x2, blocking collectives, shards(): arrived = exchange(back, SPREAD)  37.7 us
    all_to_all x1, blocking collectives, shards(): right = exchange(right, 'x')  10.6 us
    all_to_all x1, blocking collectives, shards(): parts = exchange(parts, 'x')  9.02 us
    unnamed x18, local copies, waits for them, and re-layouts  3.28 us

profile of v2, /device:TPU:1, one launch (start us, length us, event | category | flops | bytes accessed | tf_op | source)
XLA Modules:
  0.0 119.0 jit_solution(1714384756319917498)
XLA Ops:
  0.0 0.0 copy-start.1
  0.0 0.0 copy-start.2
  0.0 1.0 copy-done.2
  1.0 0.0 copy-start.5
  1.0 0.9 copy-done.5
  1.9 0.0 copy-start.6
  1.9 0.7 copy-done.6
  2.6 0.6 shard_map.73
  3.2 33.6 %all_to_all.30.own_ref = bf16[128,8,128]{2,1,0:T(8,128)(2,1)S(1)} all-to-all(bf16[128,8,128]{2,1,0:T(8,128)(2,1)S(1)} %get-tuple-element.13), channel_id=1, replica_groups=mesh['yh'=2,'z'=8,'x'=4,'yl'=4,'core'=2] {'yl','core','yh','z'}, dimensions={0} | all-to-all | bytes 524288 | tf_op jit(solution)/shard_map/all_to_all | solution.py:191
  36.7 0.0 copy-done.1
  36.7 0.4 shard_map.74
  37.1 0.0 copy-start
  37.1 10.6 %all_to_all.31.right_ref = bf16[4,96,384]{2,1,0:T(8,128)(2,1)S(1)} all-to-all(bf16[4,96,384]{2,1,0:T(8,128)(2,1)S(1)} %get-tuple-element.15), channel_id=1, replica_groups=mesh['yh'=2,'z'=8,'x'=4,'yl'=4,'core'=2] {'x'}, dimensions={0} | all-to-all | bytes 589824 | tf_op jit(solution)/shard_map/all_to_all | solution.py:193
  47.7 0.0 copy-done
  47.7 0.0 copy-start.3
  47.7 0.5 shard_map.75
  48.3 0.0 copy-start.4
  48.3 0.0 copy-start.8
  48.3 18.9 %all_to_all.32.arrived_ref = bf16[128,4,128]{2,1,0:T(4,128)(2,1)S(1)} all-to-all(bf16[128,4,128]{2,1,0:T(4,128)(2,1)S(1)} %shard_map.75), channel_id=1, replica_groups=mesh['yh'=2,'z'=8,'x'=4,'yl'=4,'core'=2] {'yl','core','yh','z'}, dimensions={0} | all-to-all | bytes 262144 | tf_op jit(solution)/shard_map/all_to_all | solution.py:195
  67.2 0.0 copy-start.7
  67.2 0.0 copy-done.3
  67.2 0.0 copy-done.4
  67.2 0.0 copy-done.8
  67.2 0.7 copy-done.7
  67.9 1.0 shard_map.76
  68.9 20.3 %all_to_all.33.own_ref = bf16[128,8,128]{2,1,0:T(8,128)(2,1)S(1)} all-to-all(bf16[128,8,128]{2,1,0:T(8,128)(2,1)S(1)} %get-tuple-element.18), channel_id=1, replica_groups=mesh['yh'=2,'z'=8,'x'=4,'yl'=4,'core'=2] {'yl','core','yh','z'}, dimensions={0} | all-to-all | bytes 524288 | tf_op jit(solution)/shard_map/all_to_all | solution.py:200
  89.2 0.6 shard_map.77
  89.8 9.0 %all_to_all.34.parts_ref = bf16[4,96,384]{2,1,0:T(8,128)(2,1)S(1)} all-to-all(bf16[4,96,384]{2,1,0:T(8,128)(2,1)S(1)} %shard_map.77), channel_id=1, replica_groups=mesh['yh'=2,'z'=8,'x'=4,'yl'=4,'core'=2] {'x'}, dimensions={0} | all-to-all | bytes 589824 | tf_op jit(solution)/shard_map/all_to_all | solution.py:202
  98.8 0.4 shard_map.78
  99.2 18.8 %all_to_all.35.arrived_ref = bf16[128,4,128]{2,1,0:T(4,128)(2,1)S(1)} all-to-all(bf16[128,4,128]{2,1,0:T(4,128)(2,1)S(1)} %shard_map.78), channel_id=1, replica_groups=mesh['yh'=2,'z'=8,'x'=4,'yl'=4,'core'=2] {'yl','core','yh','z'}, dimensions={0} | all-to-all | bytes 262144 | tf_op jit(solution)/shard_map/all_to_all | solution.py:204
  118.0 1.1 shard_map.79
Async XLA Ops:
  0.0 36.7 %copy-start.1 = (bf16[512,384]{1,0:T(8,128)(2,1)S(1)}, bf16[512,384]{1,0:T(8,128)(2,1)}, u32[]{:S(2)}) copy-start(bf16[512,384]{1,0:T(8,128)(2,1)} %constant.4.clone.squeeze_ref) | copy-start | bytes 1179652
  0.0 1.0 copy-start.2
  1.0 0.9 copy-start.5
  1.9 0.7 copy-start.6
  37.1 10.6 %copy-start = (bf16[384,512]{1,0:T(8,128)(2,1)S(1)}, bf16[384,512]{1,0:T(8,128)(2,1)}, u32[]{:S(2)}) copy-start(bf16[384,512]{1,0:T(8,128)(2,1)} %constant.5.clone.stretch_ref) | copy-start | bytes 1179652
  47.7 19.5 %copy-start.3 = (bf16[2,128,640]{2,1,0:T(8,128)(2,1)S(1)}, bf16[2,128,640]{2,1,0:T(8,128)(2,1)}, u32[]{:S(2)}) copy-start(bf16[2,128,640]{2,1,0:T(8,128)(2,1)} %weight_ref.3) | copy-start | bytes 983044
  48.3 19.0 %copy-start.4 = (bf16[2,128,128]{2,1,0:T(8,128)(2,1)S(1)}, bf16[2,128,128]{2,1,0:T(8,128)(2,1)}, u32[]{:S(2)}) copy-start(bf16[2,128,128]{2,1,0:T(8,128)(2,1)} %out_weight_ref.3) | copy-start | bytes 196612
  48.3 19.0 %copy-start.8 = (f32[2,128]{1,0:T(2,128)S(1)}, f32[2,128]{1,0:T(2,128)}, u32[]{:S(2)}) copy-start(f32[2,128]{1,0:T(2,128)} %out_gain_ref.3) | copy-start | bytes 3076
  67.2 0.7 copy-start.7

commit v3 on v2

--- a/solution.py
+++ b/solution.py
@@ -12,6 +12,7 @@
 H = 128
 HALF = 64
 SPREAD = ("yl", "core", "yh", "z")
+START_ROOM = 60 * 1024
 F32 = jnp.float32
 BF16 = jnp.bfloat16
 
@@ -29,7 +30,7 @@
 
 
 def by_device(rows):
-    return jnp.swapaxes(jnp.stack(rows, axis=0), 0, 1).astype(BF16)
+    return jnp.swapaxes(jnp.stack(rows, axis=0), 0, 1)
 
 
 def widen_groups(values, scratch):
@@ -50,8 +51,7 @@
         gate = projected[(2 * side + 1) * H : (2 * side + 2) * H]
         turned = jax.nn.sigmoid(gate) * value
         rows.extend(turned[:, t * H : (t + 1) * H] for t in range(3))
-        rows.append(jnp.zeros((H, H), F32))
-    return by_device(rows)
+    return by_device(rows).reshape(H, 3, 2, H).astype(BF16)
 
 
 def gate_of(normed, weight):
@@ -66,15 +66,15 @@
     update = lax.dot_general(
         mixed, weight, (((0,), (0,)), ((), ())), preferred_element_type=F32
     )
-    return field + gating * update
+    return field.astype(F32) + gating * update
 
 
 def matrices(own, squeeze):
-    by_row = jnp.swapaxes(own.astype(F32), 0, 1)
+    by_row = jnp.swapaxes(own.astype(F32).reshape(H, 6, H), 0, 1)
     rows = []
     for side in range(2):
         for t in range(3):
-            part = by_row[4 * side + t]
+            part = by_row[3 * side + t]
             tiles = [
                 halves(part[32 * u : 32 * u + 16], part[32 * u + 16 : 32 * u + 32]) for u in range(4)
             ]
@@ -96,16 +96,34 @@
             parts.extend(halves(tile[:16], tile[16:]))
         rows.append(jnp.concatenate(parts, axis=0))
     rows.append(jnp.zeros((H, H), F32))
-    return by_device(rows)
-
-
-def start_kernel(pair_ref, weight_ref, gain_ref, out_ref, field_ref, gate_ref, scratch):
+    return by_device(rows).astype(BF16)
+
+
+def start_kernel(
+    pair_hbm, weight_hbm, gain_hbm, out_gain_hbm,
+    out_ref, field_ref, gate_ref,
+    scratch, pair_ref, weight_ref, gain_ref, out_gain_ref, sems,
+):
+    moves = [
+        (pair_hbm, pair_ref),
+        (gain_hbm, gain_ref),
+        (weight_hbm.at[0], weight_ref),
+        (out_gain_hbm, out_gain_ref),
+    ]
+    copies = [pltpu.make_async_copy(source, target, sems.at[n]) for n, (source, target) in enumerate(moves)]
+    for copy in copies:
+        copy.start()
+    copies[0].wait()
     field = widen_groups(pair_ref[...].reshape(288, H).astype(F32), scratch)
+    field_ref[...] = field.astype(BF16)
+    copies[1].wait()
     normed = normalize(field, gain_ref[0:1, :], 1).astype(BF16)
-    weight = weight_ref[0]
+    copies[2].wait()
+    weight = weight_ref[...]
     out_ref[...] = spread_sides(normed, weight)
-    field_ref[...] = field
-    gate_ref[...] = gate_of(normed, weight)
+    gate_ref[:384] = gate_of(normed, weight)
+    copies[3].wait()
+    gate_ref[384:392] = jnp.concatenate([gain_ref[...], out_gain_ref[...], jnp.zeros((4, H), F32)], axis=0)
 
 
 def pack_kernel(own_ref, squeeze_ref, left_ref, right_ref):
@@ -126,12 +144,12 @@
 
 
 def middle_kernel(
-    arrived_ref, field_ref, gate_ref, out_weight_ref, out_gain_ref, weight_ref, gain_ref, out_ref, first_ref, next_gate_ref
+    arrived_ref, field_ref, gate_ref, out_weight_ref, weight_ref, out_ref, first_ref, next_gate_ref
 ):
     first = finish(
-        arrived_ref[...], field_ref[...], gate_ref[...], out_weight_ref[0], out_gain_ref[0:1, :]
-    ).astype(BF16).astype(F32)
-    normed = normalize(first, gain_ref[1:2, :], 1).astype(BF16)
+        arrived_ref[...], field_ref[...], gate_ref[:384], out_weight_ref[0], gate_ref[386:387]
+    ).astype(BF16)
+    normed = normalize(first.astype(F32), gate_ref[385:386], 1).astype(BF16)
     weight = weight_ref[1]
     out_ref[...] = spread_sides(normed, weight)
     first_ref[...] = first
@@ -153,9 +171,9 @@
     out_ref[...] = send_back(total, stretch_ref[...])
 
 
-def end_kernel(arrived_ref, field_ref, gate_ref, out_weight_ref, out_gain_ref, out_ref, scratch):
+def end_kernel(arrived_ref, field_ref, gate_ref, out_weight_ref, gains_ref, out_ref, scratch):
     final = finish(
-        arrived_ref[...], field_ref[...], gate_ref[...], out_weight_ref[1], out_gain_ref[1:2, :]
+        arrived_ref[...], field_ref[...], gate_ref[...], out_weight_ref[1], gains_ref[387:388]
     )
     for n in range(48):
         scratch[6 * n : 6 * n + 8, :] = final[8 * n : 8 * n + 8]
@@ -167,35 +185,47 @@
     return (np.arange(512)[:, None] == places[None, :]).astype(jnp.bfloat16)
 
 
-def call(kernel, outs, scratch=(), cost=20_000_000):
+def call(kernel, outs, scratch=(), room=48 * 1024, **specs):
     return pl.pallas_call(
         kernel,
         out_shape=[jax.ShapeDtypeStruct(shape, dtype) for shape, dtype in outs],
         scratch_shapes=list(scratch),
-        compiler_params=pltpu.CompilerParams(vmem_limit_bytes=48 * 1024 * 1024),
-        cost_estimate=pl.CostEstimate(flops=cost, bytes_accessed=1_000_000, transcendentals=100_000),
+        compiler_params=pltpu.CompilerParams(vmem_limit_bytes=room * 1024),
+        cost_estimate=pl.CostEstimate(flops=20_000_000, bytes_accessed=1_000_000, transcendentals=100_000),
+        **specs,
     )
 
 
 def shards(pair_field, proj_weight, out_weight, in_gain, out_gain):
     exchange = functools.partial(lax.all_to_all, split_axis=0, concat_axis=0, tiled=True)
     squeeze, stretch = jnp.asarray(squeeze_matrix()), jnp.asarray(squeeze_matrix().T)
-    pairs = ((384, H), F32)
-    sides, results = ((H, 8, H), BF16), ((H, 4, H), BF16)
+    pairs = ((384, H), BF16)
+    sides, results = ((H, 3, 2, H), BF16), ((H, 4, H), BF16)
     block, blocks = ((96, 384), BF16), ((4, 96, 384), BF16)
     padded = pltpu.VMEM((296, H), F32)
 
-    sent, field, gating = call(start_kernel, [sides, pairs, pairs], [padded])(
-        pair_field, proj_weight, in_gain
-    )
+    sent, field, gating = call(
+        start_kernel,
+        [sides, pairs, ((392, H), F32)],
+        [
+            padded,
+            pltpu.VMEM((6, 48, H), BF16),
+            pltpu.VMEM((H, 5 * H), BF16),
+            pltpu.VMEM((2, H), F32),
+            pltpu.VMEM((2, H), F32),
+            pltpu.SemaphoreType.DMA((4,)),
+        ],
+        START_ROOM,
+        in_specs=[pl.BlockSpec(memory_space=pltpu.HBM)] * 4,
+    )(pair_field, proj_weight, in_gain, out_gain)
     own = exchange(sent, SPREAD)
     left, right = call(pack_kernel, [block, blocks])(own, squeeze)
     right = exchange(right, "x")
     [back] = call(outgoing_kernel, [results])(left, right, stretch)
     arrived = exchange(back, SPREAD)
 
-    sent, field, gating = call(middle_kernel, [sides, pairs, pairs])(
-        arrived, field, gating, out_weight, out_gain, proj_weight, in_gain
+    sent, field, next_gating = call(middle_kernel, [sides, pairs, ((384, H), F32)])(
+        arrived, field, gating, out_weight, proj_weight
     )
     own = exchange(sent, SPREAD)
     [parts] = call(incoming_kernel, [blocks])(own, squeeze)
@@ -203,7 +233,7 @@
     [back] = call(sum_kernel, [results])(parts, stretch)
     arrived = exchange(back, SPREAD)
     [out] = call(end_kernel, [((6, 48, H), BF16)], [padded])(
-        arrived, field, gating, out_weight, out_gain
+        arrived, field, next_gating, out_weight, gating
     )
     return out
 

time: 119 us -> 116 us (0.975)
  local copies, waits for them, and re-layouts: 3.28 us -> 0.03 us
  Pallas kernels: 4.46 us -> 6.64 us
  blocking collectives: 111 us -> 109 us
    unnamed x18 -> x12, local copies, waits for them, and re-layouts: 3.28 us -> 0.03 us
    all_to_all x2, blocking collectives: 53.8 us -> 51.3 us  [shards(): own = exchange(sent, SPREAD)]
    pallas_call x2, Pallas kernels: 1.52 us -> 3.63 us  [the longest x1 2.51 us: shards(): call(start_kernel, [sides, pairs, ((392, H), F32)], [padded, pltpu.VMEM((...]
where the time goes in v3:
time: 116 us; the launch traced here: 115 us
  blocking collectives  109 us (94%)
  Pallas kernels  6.64 us (6%)
    all_to_all x2, blocking collectives, shards(): own = exchange(sent, SPREAD)  51.3 us
    all_to_all x2, blocking collectives, shards(): arrived = exchange(back, SPREAD)  37.9 us
    all_to_all x1, blocking collectives, shards(): right = exchange(right, 'x')  10.5 us
    all_to_all x1, blocking collectives, shards(): parts = exchange(parts, 'x')  8.94 us
    pallas_call x1, Pallas kernels, shards(): call(start_kernel, [sides, pairs, ((392, H), F32)], [padded, pltpu.VMEM((...  2.51 us

profile of v3, /device:TPU:1, one launch (start us, length us, event | category | flops | bytes accessed | tf_op | source)
XLA Modules:
  0.0 115.4 jit_solution(5678267198196388439)
XLA Ops:
  0.0 0.0 copy-start
  0.0 2.5 %shard_map.73 = (bf16[128,3,2,128]{3,2,1,0:T(2,128)(2,1)}, bf16[384,128]{1,0:T(8,128)(2,1)}, f32[392,128]{1,0:T(8,128)}) custom-call(bf16[6,48,128]{2,1,0:T(8,128)(2,1)} %pair_hbm.1, bf16[2,128,640]{2,1,0:T(8,128)(2,1)} %weight_ref.1, f32[2,128]{1,0:T(2,128)} %gain_hbm.1, f32[2,128]{1,0:T(2,128)} %out_gain_hbm.1), custom_call_target="tpu_custom_call" | custom-call | flops 20000000 | bytes 1000000 | tf_op jit(solution)/shard_map/pallas_call | solution.py:207
  2.5 32.4 %all_to_all.30.own_ref = bf16[128,3,2,128]{3,2,1,0:T(2,128)(2,1)S(1)} all-to-all(bf16[128,3,2,128]{3,2,1,0:T(2,128)(2,1)} %get-tuple-element.13), channel_id=1, replica_groups=mesh['yh'=2,'z'=8,'x'=4,'yl'=4,'core'=2] {'yl','core','yh','z'}, dimensions={0} | all-to-all | bytes 393216 | tf_op jit(solution)/shard_map/all_to_all | solution.py:221
  34.9 0.0 copy-done
  34.9 0.4 shard_map.74
  35.3 0.0 copy-start.1
  35.3 10.5 %all_to_all.31.right_ref = bf16[4,96,384]{2,1,0:T(8,128)(2,1)S(1)} all-to-all(bf16[4,96,384]{2,1,0:T(8,128)(2,1)S(1)} %get-tuple-element.15), channel_id=1, replica_groups=mesh['yh'=2,'z'=8,'x'=4,'yl'=4,'core'=2] {'x'}, dimensions={0} | all-to-all | bytes 589824 | tf_op jit(solution)/shard_map/all_to_all | solution.py:223
  45.9 0.0 copy-done.1
  45.9 0.0 copy-start.2
  45.9 0.0 copy-start.4
  45.9 0.0 copy-start.5
  45.9 0.5 shard_map.75
  46.4 0.0 copy-start.3
  46.4 19.0 %all_to_all.32.arrived_ref = bf16[128,4,128]{2,1,0:T(4,128)(2,1)S(1)} all-to-all(bf16[128,4,128]{2,1,0:T(4,128)(2,1)S(1)} %shard_map.75), channel_id=1, replica_groups=mesh['yh'=2,'z'=8,'x'=4,'yl'=4,'core'=2] {'yl','core','yh','z'}, dimensions={0} | all-to-all | bytes 262144 | tf_op jit(solution)/shard_map/all_to_all | solution.py:225
  65.4 0.0 copy-done.2
  65.4 0.0 copy-done.4
  65.4 0.0 copy-done.5
  65.5 0.0 copy-done.3
  65.5 1.1 shard_map.76
  66.6 18.9 %all_to_all.33.own_ref = bf16[128,3,2,128]{3,2,1,0:T(2,128)(2,1)S(1)} all-to-all(bf16[128,3,2,128]{3,2,1,0:T(2,128)(2,1)S(1)} %get-tuple-element.18), channel_id=1, replica_groups=mesh['yh'=2,'z'=8,'x'=4,'yl'=4,'core'=2] {'yl','core','yh','z'}, dimensions={0} | all-to-all | bytes 393216 | tf_op jit(solution)/shard_map/all_to_all | solution.py:230
  85.5 0.7 shard_map.77
  86.1 8.9 %all_to_all.34.parts_ref = bf16[4,96,384]{2,1,0:T(8,128)(2,1)S(1)} all-to-all(bf16[4,96,384]{2,1,0:T(8,128)(2,1)S(1)} %shard_map.77), channel_id=1, replica_groups=mesh['yh'=2,'z'=8,'x'=4,'yl'=4,'core'=2] {'x'}, dimensions={0} | all-to-all | bytes 589824 | tf_op jit(solution)/shard_map/all_to_all | solution.py:232
  95.1 0.4 shard_map.78
  95.4 18.9 %all_to_all.35.arrived_ref = bf16[128,4,128]{2,1,0:T(4,128)(2,1)S(1)} all-to-all(bf16[128,4,128]{2,1,0:T(4,128)(2,1)S(1)} %shard_map.78), channel_id=1, replica_groups=mesh['yh'=2,'z'=8,'x'=4,'yl'=4,'core'=2] {'yl','core','yh','z'}, dimensions={0} | all-to-all | bytes 262144 | tf_op jit(solution)/shard_map/all_to_all | solution.py:234
  114.3 1.1 shard_map.79
Async XLA Ops:
  0.0 34.9 %copy-start = (bf16[512,384]{1,0:T(8,128)(2,1)S(1)}, bf16[512,384]{1,0:T(8,128)(2,1)}, u32[]{:S(2)}) copy-start(bf16[512,384]{1,0:T(8,128)(2,1)} %constant.4.clone.squeeze_ref) | copy-start | bytes 1179652
  35.3 10.5 %copy-start.1 = (bf16[384,512]{1,0:T(8,128)(2,1)S(1)}, bf16[384,512]{1,0:T(8,128)(2,1)}, u32[]{:S(2)}) copy-start(bf16[384,512]{1,0:T(8,128)(2,1)} %constant.5.clone.stretch_ref) | copy-start | bytes 1179652
  45.9 19.6 %copy-start.2 = (bf16[2,128,640]{2,1,0:T(8,128)(2,1)S(1)}, bf16[2,128,640]{2,1,0:T(8,128)(2,1)}, u32[]{:S(2)}) copy-start(bf16[2,128,640]{2,1,0:T(8,128)(2,1)} %weight_ref.1) | copy-start | bytes 983044
  45.9 19.6 %copy-start.4 = (bf16[2,128,128]{2,1,0:T(8,128)(2,1)S(1)}, bf16[2,128,128]{2,1,0:T(8,128)(2,1)}, u32[]{:S(2)}) copy-start(bf16[2,128,128]{2,1,0:T(8,128)(2,1)} %out_weight_ref.3) | copy-start | bytes 196612
  45.9 19.6 %copy-start.5 = (bf16[384,128]{1,0:T(8,128)(2,1)S(1)}, bf16[384,128]{1,0:T(8,128)(2,1)}, u32[]{:S(2)}) copy-start(bf16[384,128]{1,0:T(8,128)(2,1)} %get-tuple-element.16.field_ref) | copy-start | bytes 294916
  46.4 19.0 %copy-start.3 = (f32[392,128]{1,0:T(8,128)S(1)}, f32[392,128]{1,0:T(8,128)}, u32[]{:S(2)}) copy-start(f32[392,128]{1,0:T(8,128)} %get-tuple-element.17.gate_ref.gains_ref) | copy-start | bytes 602116

commit v4 on v3

--- a/solution.py
+++ b/solution.py
@@ -11,7 +11,7 @@
 
 H = 128
 HALF = 64
-SPREAD = ("yl", "core", "yh", "z")
+SPREAD = ("yl", "z1", "yh", "z2", "z0")
 START_ROOM = 60 * 1024
 F32 = jnp.float32
 BF16 = jnp.bfloat16
@@ -50,8 +50,10 @@
         value = projected[2 * side * H : (2 * side + 1) * H]
         gate = projected[(2 * side + 1) * H : (2 * side + 2) * H]
         turned = jax.nn.sigmoid(gate) * value
-        rows.extend(turned[:, t * H : (t + 1) * H] for t in range(3))
-    return by_device(rows).reshape(H, 3, 2, H).astype(BF16)
+        for channel in range(2):
+            part = turned[channel * HALF : (channel + 1) * HALF]
+            rows.extend(part[:, t * H : (t + 1) * H] for t in range(3))
+    return by_device(rows).reshape(HALF, 3, 4, H).astype(BF16)
 
 
 def gate_of(normed, weight):
@@ -59,8 +61,10 @@
 
 
 def finish(arrived, field, gating, weight, gain):
-    by_row = jnp.swapaxes(arrived.astype(F32), 0, 1)
-    summed = jnp.concatenate([by_row[t] for t in range(3)], axis=1)
+    by_row = jnp.swapaxes(arrived.astype(F32).reshape(HALF, 6, H), 0, 1)
+    summed = jnp.concatenate(
+        [jnp.concatenate([by_row[3 * channel + t] for t in range(3)], axis=1) for channel in range(2)], axis=0
+    )
     column = jnp.swapaxes(jnp.broadcast_to(gain, (8, H)), 0, 1)[:, :1]
     mixed = normalize(summed, column, 0).astype(BF16)
     update = lax.dot_general(
@@ -69,34 +73,48 @@
     return field.astype(F32) + gating * update
 
 
-def matrices(own, squeeze):
-    by_row = jnp.swapaxes(own.astype(F32).reshape(H, 6, H), 0, 1)
-    rows = []
-    for side in range(2):
-        for t in range(3):
-            part = by_row[3 * side + t]
-            tiles = [
-                halves(part[32 * u : 32 * u + 16], part[32 * u + 16 : 32 * u + 32]) for u in range(4)
-            ]
-            for e in range(2):
-                rows.append(jnp.concatenate([tile[e] for tile in tiles], axis=1))
-    packed = jnp.dot(
+def rows_of(own):
+    return jnp.swapaxes(own.astype(F32).reshape(HALF, 12, H), 0, 1)
+
+
+def matrix(by_row, side, channel):
+    found = ([], [])
+    for t in range(3):
+        part = by_row[6 * side + 3 * channel + t]
+        tiles = [halves(part[32 * u : 32 * u + 16], part[32 * u + 16 : 32 * u + 32]) for u in range(2)]
+        for e in range(2):
+            both = jnp.concatenate([tile[e] for tile in tiles], axis=1)
+            for z1 in range(2):
+                found[z1].append(both[8 * z1 : 8 * z1 + 8])
+    return [jnp.concatenate(pieces, axis=0) for pieces in found]
+
+
+def whole_matrix(cores, side, channel):
+    parts = [matrix(by_row, side, channel) for by_row in cores]
+    return [jnp.concatenate([parts[0][z1], parts[1][z1]], axis=1) for z1 in range(2)]
+
+
+def squeezed(rows, squeeze):
+    return jnp.dot(
         jnp.concatenate(rows, axis=0).astype(BF16), squeeze, preferred_element_type=F32
     ).astype(BF16)
-    return packed[:96], packed[96:]
 
 
 def send_back(product, stretch):
     wide = jnp.dot(product.astype(BF16), stretch, preferred_element_type=F32)
     rows = []
-    for t in range(3):
-        parts = []
-        for u in range(4):
-            tile = wide[32 * t : 32 * t + 32, u * H : (u + 1) * H]
-            parts.extend(halves(tile[:16], tile[16:]))
-        rows.append(jnp.concatenate(parts, axis=0))
-    rows.append(jnp.zeros((H, H), F32))
-    return by_device(rows).astype(BF16)
+    for channel in range(2):
+        for t in range(3):
+            parts = []
+            for u in range(2):
+                lanes = slice((2 * channel + u) * H, (2 * channel + u + 1) * H)
+                pair = [
+                    jnp.concatenate([wide[8 * a : 8 * a + 8, lanes], wide[48 + 8 * a : 56 + 8 * a, lanes]], axis=0)
+                    for a in (2 * t, 2 * t + 1)
+                ]
+                parts.extend(halves(*pair))
+            rows.append(jnp.concatenate(parts, axis=0))
+    return by_device(rows).reshape(HALF, 3, 2, H).astype(BF16)
 
 
 def start_kernel(
@@ -126,20 +144,28 @@
     gate_ref[384:392] = jnp.concatenate([gain_ref[...], out_gain_ref[...], jnp.zeros((4, H), F32)], axis=0)
 
 
-def pack_kernel(own_ref, squeeze_ref, left_ref, right_ref):
-    left, right = matrices(own_ref[...], squeeze_ref[...])
-    left_ref[...] = left
+def pack_kernel(both_ref, squeeze_ref, left_ref, right_ref):
+    cores = [rows_of(both_ref[core]) for core in range(2)]
+    first = lax.axis_index("core") == 0
+    rows = []
+    for channel in range(2):
+        rows.extend(whole_matrix(cores, 0, channel))
+    for channel in range(2):
+        rows.append(jnp.where(first, *whole_matrix(cores, 1, channel)))
+    packed = squeezed(rows, squeeze_ref[...])
+    left_ref[...] = packed[:192]
     for x in range(4):
-        right_ref[x] = right
+        right_ref[x] = packed[192:]
 
 
 def outgoing_kernel(left_ref, right_ref, stretch_ref, out_ref):
-    product = lax.dot_general(
-        left_ref[...],
-        right_ref[...].reshape(384, 384),
-        (((1,), (1,)), ((), ())),
-        preferred_element_type=F32,
-    )
+    left = jnp.concatenate([left_ref[:96], left_ref[96:]], axis=1)
+    none = jnp.zeros((192, 384), BF16)
+    right = [right_ref[:, 48 * channel : 48 * channel + 48].reshape(192, 384) for channel in range(2)]
+    right = jnp.concatenate(
+        [jnp.concatenate([right[0], none], axis=1), jnp.concatenate([none, right[1]], axis=1)], axis=0
+    )
+    product = lax.dot_general(left, right, (((1,), (1,)), ((), ())), preferred_element_type=F32)
     out_ref[...] = send_back(product, stretch_ref[...])
 
 
@@ -156,12 +182,24 @@
     next_gate_ref[...] = gate_of(normed, weight)
 
 
-def incoming_kernel(own_ref, squeeze_ref, out_ref):
-    left, right = matrices(own_ref[...], squeeze_ref[...])
+def incoming_kernel(own_ref, both_ref, squeeze_ref, out_ref):
+    cores = [rows_of(both_ref[core]) for core in range(2)]
+    own = rows_of(own_ref[...])
+    none = jnp.zeros((96, 256), F32)
+    rows = []
+    for channel in range(2):
+        rows.extend(whole_matrix(cores, 0, channel))
+    for channel in range(2):
+        part = jnp.concatenate(matrix(own, 1, channel), axis=0)
+        rows.append(jnp.concatenate([none, part] if channel else [part, none], axis=1))
+    packed = squeezed(rows, squeeze_ref[...])
     product = lax.dot_general(
-        left, right, (((0,), (0,)), ((), ())), preferred_element_type=F32
-    )
-    out_ref[...] = product.reshape(4, 96, 384).astype(BF16)
+        packed[:192], packed[192:], (((0,), (0,)), ((), ())), preferred_element_type=F32
+    ).astype(BF16)
+    for x in range(4):
+        for z1 in range(2):
+            at = 192 * z1 + 48 * x
+            out_ref[x, 48 * z1 : 48 * z1 + 48] = product[at : at + 48]
 
 
 def sum_kernel(parts_ref, stretch_ref, out_ref):
@@ -181,8 +219,9 @@
 
 
 def squeeze_matrix():
-    places = np.arange(512).reshape(2, 8, 4, 8)[..., :6].transpose(2, 3, 0, 1).reshape(-1)
-    return (np.arange(512)[:, None] == places[None, :]).astype(jnp.bfloat16)
+    places = np.arange(256).reshape(2, 2, 2, 4, 8)[..., :6].transpose(3, 4, 0, 1, 2).reshape(-1)
+    block = np.arange(256)[:, None] == places[None, :]
+    return np.kron(np.eye(2, dtype=bool), block).astype(jnp.bfloat16)
 
 
 def call(kernel, outs, scratch=(), room=48 * 1024, **specs):
@@ -200,8 +239,8 @@
     exchange = functools.partial(lax.all_to_all, split_axis=0, concat_axis=0, tiled=True)
     squeeze, stretch = jnp.asarray(squeeze_matrix()), jnp.asarray(squeeze_matrix().T)
     pairs = ((384, H), BF16)
-    sides, results = ((H, 3, 2, H), BF16), ((H, 4, H), BF16)
-    block, blocks = ((96, 384), BF16), ((4, 96, 384), BF16)
+    sides, results = ((HALF, 3, 4, H), BF16), ((HALF, 3, 2, H), BF16)
+    block, blocks = ((192, 384), BF16), ((4, 96, 384), BF16)
     padded = pltpu.VMEM((296, H), F32)
 
     sent, field, gating = call(
@@ -219,7 +258,8 @@
         in_specs=[pl.BlockSpec(memory_space=pltpu.HBM)] * 4,
     )(pair_field, proj_weight, in_gain, out_gain)
     own = exchange(sent, SPREAD)
-    left, right = call(pack_kernel, [block, blocks])(own, squeeze)
+    both = lax.all_gather(own, "core", axis=0, tiled=False)
+    left, right = call(pack_kernel, [block, blocks])(both, squeeze)
     right = exchange(right, "x")
     [back] = call(outgoing_kernel, [results])(left, right, stretch)
     arrived = exchange(back, SPREAD)
@@ -228,7 +268,8 @@
         arrived, field, gating, out_weight, proj_weight
     )
     own = exchange(sent, SPREAD)
-    [parts] = call(incoming_kernel, [blocks])(own, squeeze)
+    both = lax.all_gather(own, "core", axis=0, tiled=False)
+    [parts] = call(incoming_kernel, [blocks])(own, both, squeeze)
     parts = exchange(parts, "x")
     [back] = call(sum_kernel, [results])(parts, stretch)
     arrived = exchange(back, SPREAD)
@@ -239,8 +280,8 @@
 
 
 def solution(mesh):
-    fine = Mesh(mesh.devices.reshape(2, 8, 4, 4, 2), ("yh", "z", "x", "yl", "core"))
-    row, col = ("yh", "z", "x"), ("yl", "core")
+    fine = Mesh(mesh.devices.reshape(2, 2, 2, 2, 4, 4, 2), ("yh", "z2", "z1", "z0", "x", "yl", "core"))
+    row, col = ("yh", "z2", "z1", "z0", "x"), ("yl", "core")
     return jax.shard_map(
         shards,
         mesh=fine,

time: 116 us -> 110 us (0.948)
  blocking collectives: 109 us -> 103 us
    all_gather x0 -> x2, blocking collectives: none -> 10.2 us  [shards(): both = lax.all_gather(own, 'core', axis=0, tiled=False)]
    all_to_all x2, blocking collectives: 37.9 us -> 28.6 us  [shards(): arrived = exchange(back, SPREAD)]
    all_to_all x2, blocking collectives: 51.3 us -> 44.3 us  [shards(): own = exchange(sent, SPREAD)]
where the time goes in v4:
time: 110 us; the launch traced here: 109 us
  blocking collectives  103 us (94%)
  Pallas kernels  6.67 us (6%)
    all_to_all x2, blocking collectives, shards(): own = exchange(sent, SPREAD)  44.3 us
    all_to_all x2, blocking collectives, shards(): arrived = exchange(back, SPREAD)  28.6 us
    all_to_all x1, blocking collectives, shards(): right = exchange(right, 'x')  10.4 us
    all_gather x2, blocking collectives, shards(): both = lax.all_gather(own, 'core', axis=0, tiled=False)  10.2 us
    all_to_all x1, blocking collectives, shards(): parts = exchange(parts, 'x')  8.99 us
    pallas_call x1, Pallas kernels, shards(): call(start_kernel, [sides, pairs, ((392, H), F32)], [padded, pltpu.VMEM((...  2.35 us

profile of v4, /device:TPU:1, one launch (start us, length us, event | category | flops | bytes accessed | tf_op | source)
XLA Modules:
  0.0 109.3 jit_solution(16832841257665927655)
XLA Ops:
  0.0 2.3 %shard_map.73 = (bf16[64,3,4,128]{3,2,1,0:T(4,128)(2,1)}, bf16[384,128]{1,0:T(8,128)(2,1)}, f32[392,128]{1,0:T(8,128)}) custom-call(bf16[6,48,128]{2,1,0:T(8,128)(2,1)} %pair_hbm.1, bf16[2,128,640]{2,1,0:T(8,128)(2,1)} %weight_ref.1, f32[2,128]{1,0:T(2,128)} %gain_hbm.1, f32[2,128]{1,0:T(2,128)} %out_gain_hbm.1), custom_call_target="tpu_custom_call" | custom-call | flops 20000000 | bytes 1000000 | tf_op jit(solution)/shard_map/pallas_call | solution.py:246
  2.4 28.7 %all_to_all.30 = bf16[64,3,4,128]{3,2,1,0:T(4,128)(2,1)S(1)} all-to-all(bf16[64,3,4,128]{3,2,1,0:T(4,128)(2,1)} %get-tuple-element.13), channel_id=1, replica_groups=mesh['yh'=2,'z2'=2,'z1'=2,'z0'=2,'x'=4,'yl'=4,'core'=2] {'yl','z1','yh',..., dimensions={0} | all-to-all | bytes 393216 | tf_op jit(solution)/shard_map/all_to_all | solution.py:260
  31.1 0.0 copy-start.1
  31.1 4.6 %all-gather = bf16[128,3,4,128]{3,2,1,0:T(4,128)(2,1)S(1)} all-gather(bf16[64,3,4,128]{3,2,1,0:T(4,128)(2,1)S(1)} %all_to_all.30), channel_id=2, replica_groups=mesh['yh'=2,'z2'=2,'z1'=2,'z0'=2,'x'=4,'yl'=4,'core'=2] {'core'}, dimensions={0}, use_global_device_ids=true | all-gather | bytes 589824 | tf_op jit(solution)/shard_map/all_gather | solution.py:261
  35.7 0.0 copy-done.1
  35.7 0.5 shard_map.74
  36.2 0.0 copy-start
  36.2 10.4 %all_to_all.31.right_ref = bf16[4,96,384]{2,1,0:T(8,128)(2,1)S(1)} all-to-all(bf16[4,96,384]{2,1,0:T(8,128)(2,1)S(1)} %get-tuple-element.15), channel_id=1, replica_groups=mesh['yh'=2,'z2'=2,'z1'=2,'z0'=2,'x'=4,'yl'=4,'core'=2] {'x'}, dimensions={0} | all-to-all | bytes 589824 | tf_op jit(solution)/shard_map/all_to_all | solution.py:263
  46.6 0.0 copy-done
  46.6 0.0 copy-start.2
  46.6 0.0 copy-start.3
  46.6 0.7 shard_map.75
  47.3 0.0 copy-start.4
  47.3 0.0 copy-start.5
  47.3 14.4 %all_to_all.32.arrived_ref = bf16[64,3,2,128]{3,2,1,0:T(2,128)(2,1)S(1)} all-to-all(bf16[64,3,2,128]{3,2,1,0:T(2,128)(2,1)S(1)} %shard_map.75), channel_id=1, replica_groups=mesh['yh'=2,'z2'=2,'z1'=2,'z0'=2,'x'=4,'yl'=4,'core'=2] {'yl','z1','yh',..., dimensions={0} | all-to-all | bytes 196608 | tf_op jit(solution)/shard_map/all_to_all | solution.py:265
  61.7 0.0 copy-done.2
  61.7 0.0 copy-done.3
  61.7 0.0 copy-done.4
  61.8 0.0 copy-done.5
  61.8 1.0 shard_map.76
  62.8 15.6 %all_to_all.33.own_ref = bf16[64,3,4,128]{3,2,1,0:T(4,128)(2,1)S(1)} all-to-all(bf16[64,3,4,128]{3,2,1,0:T(4,128)(2,1)S(1)} %get-tuple-element.18), channel_id=1, replica_groups=mesh['yh'=2,'z2'=2,'z1'=2,'z0'=2,'x'=4,'yl'=4,'core'=2] {'yl','z1','yh',..., dimensions={0} | all-to-all | bytes 393216 | tf_op jit(solution)/shard_map/all_to_all | solution.py:270
  78.4 5.5 %all-gather.1 = bf16[128,3,4,128]{3,2,1,0:T(4,128)(2,1)S(1)} all-gather(bf16[64,3,4,128]{3,2,1,0:T(4,128)(2,1)S(1)} %all_to_all.33.own_ref), channel_id=3, replica_groups=mesh['yh'=2,'z2'=2,'z1'=2,'z0'=2,'x'=4,'yl'=4,'core'=2] {'core'}, dimensions={0}, use_global_device_ids=true | all-gather | bytes 589824 | tf_op jit(solution)/shard_map/all_gather | solution.py:271
  83.9 0.7 shard_map.77
  84.6 9.0 %all_to_all.34.parts_ref = bf16[4,96,384]{2,1,0:T(8,128)(2,1)S(1)} all-to-all(bf16[4,96,384]{2,1,0:T(8,128)(2,1)S(1)} %shard_map.77), channel_id=1, replica_groups=mesh['yh'=2,'z2'=2,'z1'=2,'z0'=2,'x'=4,'yl'=4,'core'=2] {'x'}, dimensions={0} | all-to-all | bytes 589824 | tf_op jit(solution)/shard_map/all_to_all | solution.py:273
  93.6 0.4 shard_map.78
  94.0 14.3 %all_to_all.35.arrived_ref = bf16[64,3,2,128]{3,2,1,0:T(2,128)(2,1)S(1)} all-to-all(bf16[64,3,2,128]{3,2,1,0:T(2,128)(2,1)S(1)} %shard_map.78), channel_id=1, replica_groups=mesh['yh'=2,'z2'=2,'z1'=2,'z0'=2,'x'=4,'yl'=4,'core'=2] {'yl','z1','yh',..., dimensions={0} | all-to-all | bytes 196608 | tf_op jit(solution)/shard_map/all_to_all | solution.py:275
  108.2 1.1 shard_map.79
Async XLA Ops:
  31.1 4.6 %copy-start.1 = (bf16[512,384]{1,0:T(8,128)(2,1)S(1)}, bf16[512,384]{1,0:T(8,128)(2,1)}, u32[]{:S(2)}) copy-start(bf16[512,384]{1,0:T(8,128)(2,1)} %constant.4.clone.squeeze_ref) | copy-start | bytes 1179652
  36.2 10.4 %copy-start = (bf16[384,512]{1,0:T(8,128)(2,1)S(1)}, bf16[384,512]{1,0:T(8,128)(2,1)}, u32[]{:S(2)}) copy-start(bf16[384,512]{1,0:T(8,128)(2,1)} %constant.5.clone.stretch_ref) | copy-start | bytes 1179652
  46.6 15.1 %copy-start.2 = (bf16[2,128,640]{2,1,0:T(8,128)(2,1)S(1)}, bf16[2,128,640]{2,1,0:T(8,128)(2,1)}, u32[]{:S(2)}) copy-start(bf16[2,128,640]{2,1,0:T(8,128)(2,1)} %weight_ref.1) | copy-start | bytes 983044
  46.6 15.1 %copy-start.3 = (f32[392,128]{1,0:T(8,128)S(1)}, f32[392,128]{1,0:T(8,128)}, u32[]{:S(2)}) copy-start(f32[392,128]{1,0:T(8,128)} %get-tuple-element.17.gate_ref.gains_ref) | copy-start | bytes 602116
  47.3 14.4 %copy-start.4 = (bf16[2,128,128]{2,1,0:T(8,128)(2,1)S(1)}, bf16[2,128,128]{2,1,0:T(8,128)(2,1)}, u32[]{:S(2)}) copy-start(bf16[2,128,128]{2,1,0:T(8,128)(2,1)} %out_weight_ref.3) | copy-start | bytes 196612
  47.3 14.4 %copy-start.5 = (bf16[384,128]{1,0:T(8,128)(2,1)S(1)}, bf16[384,128]{1,0:T(8,128)(2,1)}, u32[]{:S(2)}) copy-start(bf16[384,128]{1,0:T(8,128)(2,1)} %get-tuple-element.16.field_ref) | copy-start | bytes 294916

commit v5 on v4

--- a/solution.py
+++ b/solution.py
@@ -12,6 +12,8 @@
 H = 128
 HALF = 64
 SPREAD = ("yl", "z1", "yh", "z2", "z0")
+SPREAD_NEXT = ("yl", "x", "yh", "z0")
+GATHER_NEXT = ("z1", "z2", *SPREAD_NEXT)
 START_ROOM = 60 * 1024
 F32 = jnp.float32
 BF16 = jnp.bfloat16
@@ -61,7 +63,9 @@
 
 
 def finish(arrived, field, gating, weight, gain):
-    by_row = jnp.swapaxes(arrived.astype(F32).reshape(HALF, 6, H), 0, 1)
+    devices = arrived.shape[0]
+    by_row = jnp.swapaxes(arrived.astype(F32).reshape(devices, 6, H), 0, 1)
+    by_row = sum(by_row[:, at : at + HALF] for at in range(0, devices, HALF))
     summed = jnp.concatenate(
         [jnp.concatenate([by_row[3 * channel + t] for t in range(3)], axis=1) for channel in range(2)], axis=0
     )
@@ -186,27 +190,32 @@
     cores = [rows_of(both_ref[core]) for core in range(2)]
     own = rows_of(own_ref[...])
     none = jnp.zeros((96, 256), F32)
-    rows = []
-    for channel in range(2):
-        rows.extend(whole_matrix(cores, 0, channel))
-    for channel in range(2):
+    left, right = [], []
+    for channel in range(2):
+        left.extend(whole_matrix(cores, 0, channel))
         part = jnp.concatenate(matrix(own, 1, channel), axis=0)
-        rows.append(jnp.concatenate([none, part] if channel else [part, none], axis=1))
-    packed = squeezed(rows, squeeze_ref[...])
-    product = lax.dot_general(
-        packed[:192], packed[192:], (((0,), (0,)), ((), ())), preferred_element_type=F32
-    ).astype(BF16)
-    for x in range(4):
-        for z1 in range(2):
-            at = 192 * z1 + 48 * x
-            out_ref[x, 48 * z1 : 48 * z1 + 48] = product[at : at + 48]
-
-
-def sum_kernel(parts_ref, stretch_ref, out_ref):
-    total = parts_ref[0].astype(F32)
-    for x in range(1, 4):
-        total = total + parts_ref[x].astype(F32)
-    out_ref[...] = send_back(total, stretch_ref[...])
+        right.append(jnp.concatenate([none, part] if channel else [part, none], axis=1))
+    wide = lax.dot_general(
+        squeezed(left, squeeze_ref[...]),
+        jnp.concatenate(right, axis=0).astype(BF16),
+        (((0,), (0,)), ((), ())),
+        preferred_element_type=F32,
+    )
+    rows = []
+    for channel in range(2):
+        for t in range(3):
+            found = []
+            for u in range(2):
+                lanes = slice((2 * channel + u) * H, (2 * channel + u + 1) * H)
+                pair = [
+                    jnp.concatenate([wide[32 * a : 32 * a + 32, lanes], wide[192 + 32 * a : 224 + 32 * a, lanes]], axis=0)
+                    for a in (2 * t, 2 * t + 1)
+                ]
+                found.extend(halves(*pair))
+            rows.append(
+                jnp.concatenate([part[16 * z : 16 * z + 16] for z in range(4) for part in found], axis=0)
+            )
+    out_ref[...] = by_device(rows).reshape(256, 3, 2, H).astype(BF16)
 
 
 def end_kernel(arrived_ref, field_ref, gate_ref, out_weight_ref, gains_ref, out_ref, scratch):
@@ -218,8 +227,8 @@
     out_ref[...] = scratch[0:288, :].reshape(6, 48, H).astype(BF16)
 
 
-def squeeze_matrix():
-    places = np.arange(256).reshape(2, 2, 2, 4, 8)[..., :6].transpose(3, 4, 0, 1, 2).reshape(-1)
+def squeeze_matrix(order):
+    places = np.arange(256).reshape(2, 2, 2, 4, 8)[..., :6].transpose(order).reshape(-1)
     block = np.arange(256)[:, None] == places[None, :]
     return np.kron(np.eye(2, dtype=bool), block).astype(jnp.bfloat16)
 
@@ -237,7 +246,8 @@
 
 def shards(pair_field, proj_weight, out_weight, in_gain, out_gain):
     exchange = functools.partial(lax.all_to_all, split_axis=0, concat_axis=0, tiled=True)
-    squeeze, stretch = jnp.asarray(squeeze_matrix()), jnp.asarray(squeeze_matrix().T)
+    squeeze = jnp.asarray(squeeze_matrix((4, 1, 3, 0, 2)))
+    stretch = jnp.asarray(squeeze_matrix((3, 4, 0, 1, 2)).T)
     pairs = ((384, H), BF16)
     sides, results = ((HALF, 3, 4, H), BF16), ((HALF, 3, 2, H), BF16)
     block, blocks = ((192, 384), BF16), ((4, 96, 384), BF16)
@@ -267,12 +277,10 @@
     sent, field, next_gating = call(middle_kernel, [sides, pairs, ((384, H), F32)])(
         arrived, field, gating, out_weight, proj_weight
     )
-    own = exchange(sent, SPREAD)
+    own = exchange(sent, SPREAD_NEXT)
     both = lax.all_gather(own, "core", axis=0, tiled=False)
-    [parts] = call(incoming_kernel, [blocks])(own, both, squeeze)
-    parts = exchange(parts, "x")
-    [back] = call(sum_kernel, [results])(parts, stretch)
-    arrived = exchange(back, SPREAD)
+    [parts] = call(incoming_kernel, [((256, 3, 2, H), BF16)])(own, both, squeeze)
+    arrived = exchange(parts, GATHER_NEXT)
     [out] = call(end_kernel, [((6, 48, H), BF16)], [padded])(
         arrived, field, next_gating, out_weight, gating
     )

time: 110 us -> 111 us (level)
    all_to_all x1 -> x2, blocking collectives: 8.99 us -> 38.9 us  [the longest x1 24.3 us: shards(): arrived = exchange(parts, GATHER_NEXT)]
    all_to_all x2 -> x1, blocking collectives: 44.3 us -> 28.7 us  [shards(): own = exchange(sent, SPREAD)]
    all_to_all x2 -> x1, blocking collectives: 28.6 us -> 14.4 us  [shards(): arrived = exchange(back, SPREAD)]
where the time goes in v5:
time: 111 us; the launch traced here: 110 us
  blocking collectives  103 us (93%)
  Pallas kernels  7.31 us (7%)
    all_to_all x1, blocking collectives, shards(): own = exchange(sent, SPREAD)  28.7 us
    all_to_all x1, blocking collectives, shards(): arrived = exchange(parts, GATHER_NEXT)  24.3 us
    all_to_all x1, blocking collectives, shards(): own = exchange(sent, SPREAD_NEXT)  14.6 us
    all_to_all x1, blocking collectives, shards(): arrived = exchange(back, SPREAD)  14.4 us
    all_to_all x1, blocking collectives, shards(): right = exchange(right, 'x')  10.4 us
    all_gather x2, blocking collectives, shards(): both = lax.all_gather(own, 'core', axis=0, tiled=False)  10.4 us
    pallas_call x1, Pallas kernels, shards(): call(start_kernel, [sides, pairs, ((392, H), F32)], [padded, pltpu.VMEM((...  2.35 us

profile of v5, /device:TPU:1, one launch (start us, length us, event | category | flops | bytes accessed | tf_op | source)
XLA Modules:
  0.0 110.3 jit_solution(5379378830022946367)
XLA Ops:
  0.0 2.3 %shard_map.73 = (bf16[64,3,4,128]{3,2,1,0:T(4,128)(2,1)}, bf16[384,128]{1,0:T(8,128)(2,1)}, f32[392,128]{1,0:T(8,128)}) custom-call(bf16[6,48,128]{2,1,0:T(8,128)(2,1)} %pair_hbm.1, bf16[2,128,640]{2,1,0:T(8,128)(2,1)} %weight_ref.1, f32[2,128]{1,0:T(2,128)} %gain_hbm.1, f32[2,128]{1,0:T(2,128)} %out_gain_hbm.1), custom_call_target="tpu_custom_call" | custom-call | flops 20000000 | bytes 1000000 | tf_op jit(solution)/shard_map/pallas_call | solution.py:256
  2.4 28.7 %all_to_all.25 = bf16[64,3,4,128]{3,2,1,0:T(4,128)(2,1)S(1)} all-to-all(bf16[64,3,4,128]{3,2,1,0:T(4,128)(2,1)} %get-tuple-element.13), channel_id=1, replica_groups=mesh['yh'=2,'z2'=2,'z1'=2,'z0'=2,'x'=4,'yl'=4,'core'=2] {'yl','z1','yh',..., dimensions={0} | all-to-all | bytes 393216 | tf_op jit(solution)/shard_map/all_to_all | solution.py:270
  31.1 0.0 copy-start
  31.1 4.6 %all-gather = bf16[128,3,4,128]{3,2,1,0:T(4,128)(2,1)S(1)} all-gather(bf16[64,3,4,128]{3,2,1,0:T(4,128)(2,1)S(1)} %all_to_all.25), channel_id=2, replica_groups=mesh['yh'=2,'z2'=2,'z1'=2,'z0'=2,'x'=4,'yl'=4,'core'=2] {'core'}, dimensions={0}, use_global_device_ids=true | all-gather | bytes 589824 | tf_op jit(solution)/shard_map/all_gather | solution.py:271
  35.7 0.0 copy-done
  35.7 0.5 shard_map.74
  36.2 0.0 copy-start.3
  36.2 10.4 %all_to_all.26.right_ref = bf16[4,96,384]{2,1,0:T(8,128)(2,1)S(1)} all-to-all(bf16[4,96,384]{2,1,0:T(8,128)(2,1)S(1)} %get-tuple-element.15), channel_id=1, replica_groups=mesh['yh'=2,'z2'=2,'z1'=2,'z0'=2,'x'=4,'yl'=4,'core'=2] {'x'}, dimensions={0} | all-to-all | bytes 589824 | tf_op jit(solution)/shard_map/all_to_all | solution.py:273
  46.6 0.0 copy-done.3
  46.6 0.0 copy-start.1
  46.6 0.0 copy-start.2
  46.6 0.7 shard_map.75
  47.3 0.0 copy-start.4
  47.3 0.0 copy-start.5
  47.3 14.4 %all_to_all.27.arrived_ref = bf16[64,3,2,128]{3,2,1,0:T(2,128)(2,1)S(1)} all-to-all(bf16[64,3,2,128]{3,2,1,0:T(2,128)(2,1)S(1)} %shard_map.75), channel_id=1, replica_groups=mesh['yh'=2,'z2'=2,'z1'=2,'z0'=2,'x'=4,'yl'=4,'core'=2] {'yl','z1','yh',..., dimensions={0} | all-to-all | bytes 196608 | tf_op jit(solution)/shard_map/all_to_all | solution.py:275
  61.7 0.0 copy-done.1
  61.7 0.0 copy-done.2
  61.7 0.0 copy-done.4
  61.8 0.0 copy-done.5
  61.8 1.0 shard_map.76
  62.8 14.6 %all_to_all.28.own_ref = bf16[64,3,4,128]{3,2,1,0:T(4,128)(2,1)S(1)} all-to-all(bf16[64,3,4,128]{3,2,1,0:T(4,128)(2,1)S(1)} %get-tuple-element.18), channel_id=1, replica_groups=mesh['yh'=2,'z2'=2,'z1'=2,'z0'=2,'x'=4,'yl'=4,'core'=2] {'yl','x','yh','..., dimensions={0} | all-to-all | bytes 393216 | tf_op jit(solution)/shard_map/all_to_all | solution.py:280
  77.4 5.8 %all-gather.1 = bf16[128,3,4,128]{3,2,1,0:T(4,128)(2,1)S(1)} all-gather(bf16[64,3,4,128]{3,2,1,0:T(4,128)(2,1)S(1)} %all_to_all.28.own_ref), channel_id=3, replica_groups=mesh['yh'=2,'z2'=2,'z1'=2,'z0'=2,'x'=4,'yl'=4,'core'=2] {'core'}, dimensions={0}, use_global_device_ids=true | all-gather | bytes 589824 | tf_op jit(solution)/shard_map/all_gather | solution.py:281
  83.2 1.1 %shard_map.77 = bf16[256,3,2,128]{3,2,1,0:T(2,128)(2,1)S(1)} custom-call(bf16[64,3,4,128]{3,2,1,0:T(4,128)(2,1)S(1)} %all_to_all.28.own_ref, bf16[2,64,3,4,128]{4,3,2,1,0:T(4,128)(2,1)S(1)} %bitcast.3, bf16[512,384]{1,0:T(8,128)(2,1)S(1)} %copy-done), custom_call_target="tpu_custom_call" | custom-call | flops 20000000 | bytes 1000000 | tf_op jit(solution)/shard_map/pallas_call | solution.py:282
  84.3 24.3 %all_to_all.29.arrived_ref = bf16[256,3,2,128]{3,2,1,0:T(2,128)(2,1)S(1)} all-to-all(bf16[256,3,2,128]{3,2,1,0:T(2,128)(2,1)S(1)} %shard_map.77), channel_id=1, replica_groups=mesh['yh'=2,'z2'=2,'z1'=2,'z0'=2,'x'=4,'yl'=4,'core'=2] {'z1','z2','yl',..., dimensions={0} | all-to-all | bytes 786432 | tf_op jit(solution)/shard_map/all_to_all | solution.py:283
  108.6 1.7 %shard_map.78 = bf16[6,48,128]{2,1,0:T(8,128)(2,1)} custom-call(bf16[256,3,2,128]{3,2,1,0:T(2,128)(2,1)S(1)} %all_to_all.29.arrived_ref, bf16[384,128]{1,0:T(8,128)(2,1)S(1)} %get-tuple-element.19.field_ref, f32[384,128]{1,0:T(8,128)S(1)} %get-tuple-element.20.gate_ref, bf16[2,128,128]{2,1,0:T(8,128)(2,1)S(1)} %copy-done.4, f32[392,128]{1,0:T(8,128)S(1)} %copy-done.2), custom_call_target="tpu_custom_call" | custom-call | flops 20000000 | bytes 1000000 | tf_op jit(solution)/shard_map/pallas_call | solution.py:284
Async XLA Ops:
  31.1 4.6 %copy-start = (bf16[512,384]{1,0:T(8,128)(2,1)S(1)}, bf16[512,384]{1,0:T(8,128)(2,1)}, u32[]{:S(2)}) copy-start(bf16[512,384]{1,0:T(8,128)(2,1)} %constant.4.clone.squeeze_ref) | copy-start | bytes 1179652
  36.2 10.4 %copy-start.3 = (bf16[384,512]{1,0:T(8,128)(2,1)S(1)}, bf16[384,512]{1,0:T(8,128)(2,1)}, u32[]{:S(2)}) copy-start(bf16[384,512]{1,0:T(8,128)(2,1)} %constant.5.clone.stretch_ref) | copy-start | bytes 1179652
  46.6 15.1 %copy-start.1 = (bf16[2,128,640]{2,1,0:T(8,128)(2,1)S(1)}, bf16[2,128,640]{2,1,0:T(8,128)(2,1)}, u32[]{:S(2)}) copy-start(bf16[2,128,640]{2,1,0:T(8,128)(2,1)} %weight_ref.1) | copy-start | bytes 983044
  46.6 15.1 %copy-start.2 = (f32[392,128]{1,0:T(8,128)S(1)}, f32[392,128]{1,0:T(8,128)}, u32[]{:S(2)}) copy-start(f32[392,128]{1,0:T(8,128)} %get-tuple-element.17.gate_ref.gains_ref) | copy-start | bytes 602116
  47.3 14.4 %copy-start.4 = (bf16[2,128,128]{2,1,0:T(8,128)(2,1)S(1)}, bf16[2,128,128]{2,1,0:T(8,128)(2,1)}, u32[]{:S(2)}) copy-start(bf16[2,128,128]{2,1,0:T(8,128)(2,1)} %out_weight_ref.3) | copy-start | bytes 196612
  47.3 14.4 %copy-start.5 = (bf16[384,128]{1,0:T(8,128)(2,1)S(1)}, bf16[384,128]{1,0:T(8,128)(2,1)}, u32[]{:S(2)}) copy-start(bf16[384,128]{1,0:T(8,128)(2,1)} %get-tuple-element.16.field_ref) | copy-start | bytes 294916

commit v6 on v5

--- a/solution.py
+++ b/solution.py
@@ -12,8 +12,8 @@
 H = 128
 HALF = 64
 SPREAD = ("yl", "z1", "yh", "z2", "z0")
-SPREAD_NEXT = ("yl", "x", "yh", "z0")
-GATHER_NEXT = ("z1", "z2", *SPREAD_NEXT)
+SPREAD_NEXT = ("yl", "yh", "z0", "x")
+GATHER_NEXT = ("yl", "yh", "z2", "z1", "z0", "x")
 START_ROOM = 60 * 1024
 F32 = jnp.float32
 BF16 = jnp.bfloat16
@@ -63,9 +63,10 @@
 
 
 def finish(arrived, field, gating, weight, gain):
-    devices = arrived.shape[0]
-    by_row = jnp.swapaxes(arrived.astype(F32).reshape(devices, 6, H), 0, 1)
-    by_row = sum(by_row[:, at : at + HALF] for at in range(0, devices, HALF))
+    parts = arrived.shape[0] // HALF
+    total = arrived.astype(F32).reshape(8, parts, 8, 3, 2, H)
+    total = sum(total[:, n] for n in range(parts)).reshape(HALF, 6, H)
+    by_row = jnp.swapaxes(total, 0, 1)
     summed = jnp.concatenate(
         [jnp.concatenate([by_row[3 * channel + t] for t in range(3)], axis=1) for channel in range(2)], axis=0
     )
@@ -212,9 +213,8 @@
                     for a in (2 * t, 2 * t + 1)
                 ]
                 found.extend(halves(*pair))
-            rows.append(
-                jnp.concatenate([part[16 * z : 16 * z + 16] for z in range(4) for part in found], axis=0)
-            )
+            at = [32 * z1 + 8 * pair for pair in range(4) for z1 in range(2)]
+            rows.append(jnp.concatenate([part[n : n + 8] for part in found for n in at], axis=0))
     out_ref[...] = by_device(rows).reshape(256, 3, 2, H).astype(BF16)
 
 
@@ -246,7 +246,7 @@
 
 def shards(pair_field, proj_weight, out_weight, in_gain, out_gain):
     exchange = functools.partial(lax.all_to_all, split_axis=0, concat_axis=0, tiled=True)
-    squeeze = jnp.asarray(squeeze_matrix((4, 1, 3, 0, 2)))
+    squeeze = jnp.asarray(squeeze_matrix((4, 0, 1, 2, 3)))
     stretch = jnp.asarray(squeeze_matrix((3, 4, 0, 1, 2)).T)
     pairs = ((384, H), BF16)
     sides, results = ((HALF, 3, 4, H), BF16), ((HALF, 3, 2, H), BF16)

time: 111 us -> 111 us (level)
  no operation moved by 1% of the time
where the time goes in v6:
time: 111 us; the launch traced here: 110 us
  blocking collectives  102 us (92%)
  Pallas kernels  7.12 us (6%)
    all_to_all x1, blocking collectives, shards(): own = exchange(sent, SPREAD)  28.7 us
    all_to_all x1, blocking collectives, shards(): arrived = exchange(parts, GATHER_NEXT)  24.6 us
    all_to_all x1, blocking collectives, shards(): arrived = exchange(back, SPREAD)  14.4 us
    all_to_all x1, blocking collectives, shards(): own = exchange(sent, SPREAD_NEXT)  13.9 us
    all_to_all x1, blocking collectives, shards(): right = exchange(right, 'x')  10.4 us
    all_gather x2, blocking collectives, shards(): both = lax.all_gather(own, 'core', axis=0, tiled=False)  10.3 us
    pallas_call x1, Pallas kernels, shards(): call(start_kernel, [sides, pairs, ((392, H), F32)], [padded, pltpu.VMEM((...  2.35 us

profile of v6, /device:TPU:1, one launch (start us, length us, event | category | flops | bytes accessed | tf_op | source)
XLA Modules:
  0.0 109.6 jit_solution(12707390291751283564)
XLA Ops:
  0.0 2.3 %shard_map.73 = (bf16[64,3,4,128]{3,2,1,0:T(4,128)(2,1)}, bf16[384,128]{1,0:T(8,128)(2,1)}, f32[392,128]{1,0:T(8,128)}) custom-call(bf16[6,48,128]{2,1,0:T(8,128)(2,1)} %pair_hbm.1, bf16[2,128,640]{2,1,0:T(8,128)(2,1)} %weight_ref.1, f32[2,128]{1,0:T(2,128)} %gain_hbm.1, f32[2,128]{1,0:T(2,128)} %out_gain_hbm.1), custom_call_target="tpu_custom_call" | custom-call | flops 20000000 | bytes 1000000 | tf_op jit(solution)/shard_map/pallas_call | solution.py:256
  2.4 28.7 %all_to_all.25 = bf16[64,3,4,128]{3,2,1,0:T(4,128)(2,1)S(1)} all-to-all(bf16[64,3,4,128]{3,2,1,0:T(4,128)(2,1)} %get-tuple-element.13), channel_id=1, replica_groups=mesh['yh'=2,'z2'=2,'z1'=2,'z0'=2,'x'=4,'yl'=4,'core'=2] {'yl','z1','yh',..., dimensions={0} | all-to-all | bytes 393216 | tf_op jit(solution)/shard_map/all_to_all | solution.py:270
  31.1 0.0 copy-start
  31.1 4.6 %all-gather = bf16[128,3,4,128]{3,2,1,0:T(4,128)(2,1)S(1)} all-gather(bf16[64,3,4,128]{3,2,1,0:T(4,128)(2,1)S(1)} %all_to_all.25), channel_id=2, replica_groups=mesh['yh'=2,'z2'=2,'z1'=2,'z0'=2,'x'=4,'yl'=4,'core'=2] {'core'}, dimensions={0}, use_global_device_ids=true | all-gather | bytes 589824 | tf_op jit(solution)/shard_map/all_gather | solution.py:271
  35.7 0.0 copy-done
  35.7 0.5 shard_map.74
  36.2 0.0 copy-start.3
  36.2 10.4 %all_to_all.26.right_ref = bf16[4,96,384]{2,1,0:T(8,128)(2,1)S(1)} all-to-all(bf16[4,96,384]{2,1,0:T(8,128)(2,1)S(1)} %get-tuple-element.15), channel_id=1, replica_groups=mesh['yh'=2,'z2'=2,'z1'=2,'z0'=2,'x'=4,'yl'=4,'core'=2] {'x'}, dimensions={0} | all-to-all | bytes 589824 | tf_op jit(solution)/shard_map/all_to_all | solution.py:273
  46.6 0.0 copy-done.3
  46.6 0.0 copy-start.1
  46.6 0.0 copy-start.2
  46.6 0.7 shard_map.75
  47.3 0.0 copy-start.4
  47.3 0.0 copy-start.5
  47.3 14.4 %all_to_all.27.arrived_ref = bf16[64,3,2,128]{3,2,1,0:T(2,128)(2,1)S(1)} all-to-all(bf16[64,3,2,128]{3,2,1,0:T(2,128)(2,1)S(1)} %shard_map.75), channel_id=1, replica_groups=mesh['yh'=2,'z2'=2,'z1'=2,'z0'=2,'x'=4,'yl'=4,'core'=2] {'yl','z1','yh',..., dimensions={0} | all-to-all | bytes 196608 | tf_op jit(solution)/shard_map/all_to_all | solution.py:275
  61.7 0.0 copy-done.1
  61.7 0.0 copy-done.2
  61.7 0.0 copy-done.4
  61.8 0.0 copy-done.5
  61.8 1.0 shard_map.76
  62.8 13.9 %all_to_all.28.own_ref = bf16[64,3,4,128]{3,2,1,0:T(4,128)(2,1)S(1)} all-to-all(bf16[64,3,4,128]{3,2,1,0:T(4,128)(2,1)S(1)} %get-tuple-element.18), channel_id=1, replica_groups=mesh['yh'=2,'z2'=2,'z1'=2,'z0'=2,'x'=4,'yl'=4,'core'=2] {'yl','yh','z0',..., dimensions={0} | all-to-all | bytes 393216 | tf_op jit(solution)/shard_map/all_to_all | solution.py:280
  76.7 5.7 %all-gather.1 = bf16[128,3,4,128]{3,2,1,0:T(4,128)(2,1)S(1)} all-gather(bf16[64,3,4,128]{3,2,1,0:T(4,128)(2,1)S(1)} %all_to_all.28.own_ref), channel_id=3, replica_groups=mesh['yh'=2,'z2'=2,'z1'=2,'z0'=2,'x'=4,'yl'=4,'core'=2] {'core'}, dimensions={0}, use_global_device_ids=true | all-gather | bytes 589824 | tf_op jit(solution)/shard_map/all_gather | solution.py:281
  82.4 1.1 %shard_map.77 = bf16[256,3,2,128]{3,2,1,0:T(2,128)(2,1)S(1)} custom-call(bf16[64,3,4,128]{3,2,1,0:T(4,128)(2,1)S(1)} %all_to_all.28.own_ref, bf16[2,64,3,4,128]{4,3,2,1,0:T(4,128)(2,1)S(1)} %bitcast.3, bf16[512,384]{1,0:T(8,128)(2,1)S(1)} %copy-done), custom_call_target="tpu_custom_call" | custom-call | flops 20000000 | bytes 1000000 | tf_op jit(solution)/shard_map/pallas_call | solution.py:282
  83.5 24.6 %all_to_all.29.arrived_ref = bf16[256,3,2,128]{3,2,1,0:T(2,128)(2,1)S(1)} all-to-all(bf16[256,3,2,128]{3,2,1,0:T(2,128)(2,1)S(1)} %shard_map.77), channel_id=1, replica_groups=mesh['yh'=2,'z2'=2,'z1'=2,'z0'=2,'x'=4,'yl'=4,'core'=2] {'yl','yh','z2',..., dimensions={0} | all-to-all | bytes 786432 | tf_op jit(solution)/shard_map/all_to_all | solution.py:283
  108.1 1.5 %shard_map.78 = bf16[6,48,128]{2,1,0:T(8,128)(2,1)} custom-call(bf16[256,3,2,128]{3,2,1,0:T(2,128)(2,1)S(1)} %all_to_all.29.arrived_ref, bf16[384,128]{1,0:T(8,128)(2,1)S(1)} %get-tuple-element.19.field_ref, f32[384,128]{1,0:T(8,128)S(1)} %get-tuple-element.20.gate_ref, bf16[2,128,128]{2,1,0:T(8,128)(2,1)S(1)} %copy-done.4, f32[392,128]{1,0:T(8,128)S(1)} %copy-done.2), custom_call_target="tpu_custom_call" | custom-call | flops 20000000 | bytes 1000000 | tf_op jit(solution)/shard_map/pallas_call | solution.py:284
Async XLA Ops:
  31.1 4.6 %copy-start = (bf16[512,384]{1,0:T(8,128)(2,1)S(1)}, bf16[512,384]{1,0:T(8,128)(2,1)}, u32[]{:S(2)}) copy-start(bf16[512,384]{1,0:T(8,128)(2,1)} %constant.4.clone.squeeze_ref) | copy-start | bytes 1179652
  36.2 10.4 %copy-start.3 = (bf16[384,512]{1,0:T(8,128)(2,1)S(1)}, bf16[384,512]{1,0:T(8,128)(2,1)}, u32[]{:S(2)}) copy-start(bf16[384,512]{1,0:T(8,128)(2,1)} %constant.5.clone.stretch_ref) | copy-start | bytes 1179652
  46.6 15.1 %copy-start.1 = (bf16[2,128,640]{2,1,0:T(8,128)(2,1)S(1)}, bf16[2,128,640]{2,1,0:T(8,128)(2,1)}, u32[]{:S(2)}) copy-start(bf16[2,128,640]{2,1,0:T(8,128)(2,1)} %weight_ref.1) | copy-start | bytes 983044
  46.6 15.1 %copy-start.2 = (f32[392,128]{1,0:T(8,128)S(1)}, f32[392,128]{1,0:T(8,128)}, u32[]{:S(2)}) copy-start(f32[392,128]{1,0:T(8,128)} %get-tuple-element.17.gate_ref.gains_ref) | copy-start | bytes 602116
  47.3 14.4 %copy-start.4 = (bf16[2,128,128]{2,1,0:T(8,128)(2,1)S(1)}, bf16[2,128,128]{2,1,0:T(8,128)(2,1)}, u32[]{:S(2)}) copy-start(bf16[2,128,128]{2,1,0:T(8,128)(2,1)} %out_weight_ref.3) | copy-start | bytes 196612
  47.3 14.4 %copy-start.5 = (bf16[384,128]{1,0:T(8,128)(2,1)S(1)}, bf16[384,128]{1,0:T(8,128)(2,1)}, u32[]{:S(2)}) copy-start(bf16[384,128]{1,0:T(8,128)(2,1)} %get-tuple-element.16.field_ref) | copy-start | bytes 294916

commit v7 on v4

--- a/solution.py
+++ b/solution.py
@@ -12,7 +12,6 @@
 H = 128
 HALF = 64
 SPREAD = ("yl", "z1", "yh", "z2", "z0")
-START_ROOM = 60 * 1024
 F32 = jnp.float32
 BF16 = jnp.bfloat16
 
@@ -100,8 +99,7 @@
     ).astype(BF16)
 
 
-def send_back(product, stretch):
-    wide = jnp.dot(product.astype(BF16), stretch, preferred_element_type=F32)
+def send_back(wide):
     rows = []
     for channel in range(2):
         for t in range(3):
@@ -117,31 +115,13 @@
     return by_device(rows).reshape(HALF, 3, 2, H).astype(BF16)
 
 
-def start_kernel(
-    pair_hbm, weight_hbm, gain_hbm, out_gain_hbm,
-    out_ref, field_ref, gate_ref,
-    scratch, pair_ref, weight_ref, gain_ref, out_gain_ref, sems,
-):
-    moves = [
-        (pair_hbm, pair_ref),
-        (gain_hbm, gain_ref),
-        (weight_hbm.at[0], weight_ref),
-        (out_gain_hbm, out_gain_ref),
-    ]
-    copies = [pltpu.make_async_copy(source, target, sems.at[n]) for n, (source, target) in enumerate(moves)]
-    for copy in copies:
-        copy.start()
-    copies[0].wait()
+def start_kernel(pair_ref, weight_ref, gain_ref, out_ref, field_ref, gate_ref, scratch):
     field = widen_groups(pair_ref[...].reshape(288, H).astype(F32), scratch)
     field_ref[...] = field.astype(BF16)
-    copies[1].wait()
-    normed = normalize(field, gain_ref[0:1, :], 1).astype(BF16)
-    copies[2].wait()
+    normed = normalize(field, gain_ref[...], 1).astype(BF16)
     weight = weight_ref[...]
     out_ref[...] = spread_sides(normed, weight)
-    gate_ref[:384] = gate_of(normed, weight)
-    copies[3].wait()
-    gate_ref[384:392] = jnp.concatenate([gain_ref[...], out_gain_ref[...], jnp.zeros((4, H), F32)], axis=0)
+    gate_ref[...] = gate_of(normed, weight)
 
 
 def pack_kernel(both_ref, squeeze_ref, left_ref, right_ref):
@@ -159,24 +139,26 @@
 
 
 def outgoing_kernel(left_ref, right_ref, stretch_ref, out_ref):
-    left = jnp.concatenate([left_ref[:96], left_ref[96:]], axis=1)
-    none = jnp.zeros((192, 384), BF16)
-    right = [right_ref[:, 48 * channel : 48 * channel + 48].reshape(192, 384) for channel in range(2)]
-    right = jnp.concatenate(
-        [jnp.concatenate([right[0], none], axis=1), jnp.concatenate([none, right[1]], axis=1)], axis=0
-    )
-    product = lax.dot_general(left, right, (((1,), (1,)), ((), ())), preferred_element_type=F32)
-    out_ref[...] = send_back(product, stretch_ref[...])
+    wide = []
+    for channel in range(2):
+        product = lax.dot_general(
+            left_ref[96 * channel : 96 * channel + 96],
+            right_ref[:, 48 * channel : 48 * channel + 48].reshape(192, 384),
+            (((1,), (1,)), ((), ())),
+            preferred_element_type=F32,
+        ).astype(BF16)
+        wide.append(jnp.dot(product, stretch_ref[:192, :256], preferred_element_type=F32))
+    out_ref[...] = send_back(jnp.concatenate(wide, axis=1))
 
 
 def middle_kernel(
-    arrived_ref, field_ref, gate_ref, out_weight_ref, weight_ref, out_ref, first_ref, next_gate_ref
+    arrived_ref, field_ref, gate_ref, out_weight_ref, out_gain_ref, weight_ref, gain_ref, out_ref, first_ref, next_gate_ref
 ):
     first = finish(
-        arrived_ref[...], field_ref[...], gate_ref[:384], out_weight_ref[0], gate_ref[386:387]
+        arrived_ref[...], field_ref[...], gate_ref[...], out_weight_ref[0], out_gain_ref[...]
     ).astype(BF16)
-    normed = normalize(first.astype(F32), gate_ref[385:386], 1).astype(BF16)
-    weight = weight_ref[1]
+    normed = normalize(first.astype(F32), gain_ref[...], 1).astype(BF16)
+    weight = weight_ref[...]
     out_ref[...] = spread_sides(normed, weight)
     first_ref[...] = first
     next_gate_ref[...] = gate_of(normed, weight)
@@ -206,12 +188,12 @@
     total = parts_ref[0].astype(F32)
     for x in range(1, 4):
         total = total + parts_ref[x].astype(F32)
-    out_ref[...] = send_back(total, stretch_ref[...])
-
-
-def end_kernel(arrived_ref, field_ref, gate_ref, out_weight_ref, gains_ref, out_ref, scratch):
+    out_ref[...] = send_back(jnp.dot(total.astype(BF16), stretch_ref[...], preferred_element_type=F32))
+
+
+def end_kernel(arrived_ref, field_ref, gate_ref, out_weight_ref, gain_ref, out_ref, scratch):
     final = finish(
-        arrived_ref[...], field_ref[...], gate_ref[...], out_weight_ref[1], gains_ref[387:388]
+        arrived_ref[...], field_ref[...], gate_ref[...], out_weight_ref[1], gain_ref[...]
     )
     for n in range(48):
         scratch[6 * n : 6 * n + 8, :] = final[8 * n : 8 * n + 8]
@@ -224,39 +206,27 @@
     return np.kron(np.eye(2, dtype=bool), block).astype(jnp.bfloat16)
 
 
-def call(kernel, outs, scratch=(), room=48 * 1024, **specs):
+def call(kernel, outs, scratch=()):
     return pl.pallas_call(
         kernel,
         out_shape=[jax.ShapeDtypeStruct(shape, dtype) for shape, dtype in outs],
         scratch_shapes=list(scratch),
-        compiler_params=pltpu.CompilerParams(vmem_limit_bytes=room * 1024),
+        compiler_params=pltpu.CompilerParams(vmem_limit_bytes=48 * 1024 * 1024),
         cost_estimate=pl.CostEstimate(flops=20_000_000, bytes_accessed=1_000_000, transcendentals=100_000),
-        **specs,
     )
 
 
 def shards(pair_field, proj_weight, out_weight, in_gain, out_gain):
     exchange = functools.partial(lax.all_to_all, split_axis=0, concat_axis=0, tiled=True)
     squeeze, stretch = jnp.asarray(squeeze_matrix()), jnp.asarray(squeeze_matrix().T)
-    pairs = ((384, H), BF16)
+    pairs, gates = ((384, H), BF16), ((384, H), F32)
     sides, results = ((HALF, 3, 4, H), BF16), ((HALF, 3, 2, H), BF16)
     block, blocks = ((192, 384), BF16), ((4, 96, 384), BF16)
     padded = pltpu.VMEM((296, H), F32)
 
-    sent, field, gating = call(
-        start_kernel,
-        [sides, pairs, ((392, H), F32)],
-        [
-            padded,
-            pltpu.VMEM((6, 48, H), BF16),
-            pltpu.VMEM((H, 5 * H), BF16),
-            pltpu.VMEM((2, H), F32),
-            pltpu.VMEM((2, H), F32),
-            pltpu.SemaphoreType.DMA((4,)),
-        ],
-        START_ROOM,
-        in_specs=[pl.BlockSpec(memory_space=pltpu.HBM)] * 4,
-    )(pair_field, proj_weight, in_gain, out_gain)
+    sent, field, gating = call(start_kernel, [sides, pairs, gates], [padded])(
+        pair_field, proj_weight[0], in_gain[:1]
+    )
     own = exchange(sent, SPREAD)
     both = lax.all_gather(own, "core", axis=0, tiled=False)
     left, right = call(pack_kernel, [block, blocks])(both, squeeze)
@@ -264,8 +234,8 @@
     [back] = call(outgoing_kernel, [results])(left, right, stretch)
     arrived = exchange(back, SPREAD)
 
-    sent, field, next_gating = call(middle_kernel, [sides, pairs, ((384, H), F32)])(
-        arrived, field, gating, out_weight, proj_weight
+    sent, field, gating = call(middle_kernel, [sides, pairs, gates])(
+        arrived, field, gating, out_weight, out_gain[:1], proj_weight[1], in_gain[1:]
     )
     own = exchange(sent, SPREAD)
     both = lax.all_gather(own, "core", axis=0, tiled=False)
@@ -274,7 +244,7 @@
     [back] = call(sum_kernel, [results])(parts, stretch)
     arrived = exchange(back, SPREAD)
     [out] = call(end_kernel, [((6, 48, H), BF16)], [padded])(
-        arrived, field, next_gating, out_weight, gating
+        arrived, field, gating, out_weight, out_gain[1:]
     )
     return out
 

time: 110 us -> 111 us (level)
  blocking collectives: 103 us -> 87.8 us
  waiting for transfers between devices: 0 us -> 10.4 us
  starting transfers between devices: 0 us -> 4.72 us
  Pallas kernels: 6.67 us -> 5.56 us
    all_to_all x2 -> x1, blocking collectives: 28.6 us -> 14.3 us  [shards(): arrived = exchange(back, SPREAD)]
    all_to_all x0 -> x1, waiting for transfers between devices: none -> 10.4 us  [shards(): arrived = exchange(back, SPREAD)]
    all_to_all x0 -> x1, starting transfers between devices: none -> 4.72 us  [shards(): arrived = exchange(back, SPREAD)]
    pallas_call x2, Pallas kernels: 3.35 us -> 1.56 us  [the longest x1 1 us: shards(): call(middle_kernel, [sides, pairs, gates])]
  transfers between devices with their start and end apart: 0 -> 1, of which waited for: 0 -> 1; matrix products, arithmetic and copies ran while one was open for 0% -> 0% of each run, Pallas kernels for 0% -> 0%
where the time goes in v7:
time: 111 us; the launch traced here: 110 us
  blocking collectives  87.8 us (79%)
  waiting for transfers between devices  10.4 us (9%)
  Pallas kernels  5.56 us (5%)
  starting transfers between devices  4.72 us (4%)
    all_to_all x2, blocking collectives, shards(): own = exchange(sent, SPREAD)  44.2 us
    all_to_all x1, blocking collectives, shards(): arrived = exchange(back, SPREAD)  14.3 us
    all_to_all x1, waiting for transfers between devices, shards(): arrived = exchange(back, SPREAD)  10.4 us
    all_to_all x1, blocking collectives, shards(): right = exchange(right, 'x')  10.4 us
    all_gather x2, blocking collectives, shards(): both = lax.all_gather(own, 'core', axis=0, tiled=False)  9.99 us
    all_to_all x1, blocking collectives, shards(): parts = exchange(parts, 'x')  8.99 us
    all_to_all x1, starting transfers between devices, shards(): arrived = exchange(back, SPREAD)  4.72 us
  transfers between devices with their start and end apart: 1, of which 1 were waited for; matrix products, arithmetic and copies ran while one was open for 0% of the time, Pallas kernels for 0%

profile of v7, /device:TPU:1, one launch (start us, length us, event | category | flops | bytes accessed | tf_op | source)
XLA Modules:
  0.0 109.7 jit_solution(6666916572683873991)
XLA Ops:
  0.0 0.0 copy-start.4
  0.0 0.0 copy-start.3
  0.0 1.1 slice_bitcast_fusion
  1.1 0.0 copy-done.4
  1.1 0.0 copy-done.3
  1.1 0.6 shard_map.73
  1.7 28.5 %all_to_all.30 = bf16[64,3,4,128]{3,2,1,0:T(4,128)(2,1)S(1)} all-to-all(bf16[64,3,4,128]{3,2,1,0:T(4,128)(2,1)S(1)} %get-tuple-element.13), channel_id=1, replica_groups=mesh['yh'=2,'z2'=2,'z1'=2,'z0'=2,'x'=4,'yl'=4,'core'=2] {'yl','z1','yh',..., dimensions={0} | all-to-all | bytes 393216 | tf_op jit(solution)/shard_map/all_to_all | solution.py:230
  30.2 0.0 copy-start.1
  30.2 4.6 %all-gather = bf16[128,3,4,128]{3,2,1,0:T(4,128)(2,1)S(1)} all-gather(bf16[64,3,4,128]{3,2,1,0:T(4,128)(2,1)S(1)} %all_to_all.30), channel_id=2, replica_groups=mesh['yh'=2,'z2'=2,'z1'=2,'z0'=2,'x'=4,'yl'=4,'core'=2] {'core'}, dimensions={0}, use_global_device_ids=true | all-gather | bytes 589824 | tf_op jit(solution)/shard_map/all_gather | solution.py:231
  34.8 0.0 copy-done.1
  34.8 0.5 shard_map.74
  35.3 0.0 copy-start
  35.3 10.4 %all_to_all.31.right_ref = bf16[4,96,384]{2,1,0:T(8,128)(2,1)S(1)} all-to-all(bf16[4,96,384]{2,1,0:T(8,128)(2,1)S(1)} %get-tuple-element.15), channel_id=1, replica_groups=mesh['yh'=2,'z2'=2,'z1'=2,'z0'=2,'x'=4,'yl'=4,'core'=2] {'x'}, dimensions={0} | all-to-all | bytes 589824 | tf_op jit(solution)/shard_map/all_to_all | solution.py:233
  45.7 0.0 copy-done
  45.7 1.4 %shard_map.75 = bf16[64,3,2,128]{3,2,1,0:T(2,128)(2,1)} custom-call(bf16[192,384]{1,0:T(8,128)(2,1)S(1)} %get-tuple-element.14.left_ref, bf16[4,96,384]{2,1,0:T(8,128)(2,1)S(1)} %all_to_all.31.right_ref, bf16[384,512]{1,0:T(8,128)(2,1)S(1)} %copy-done), custom_call_target="tpu_custom_call" | custom-call | flops 20000000 | bytes 1000000 | tf_op jit(solution)/shard_map/pallas_call | solution.py:234
  47.1 0.0 copy-start.5
  47.1 0.0 copy-start.2
  47.1 4.7 %all-to-all-start.2 = ((bf16[64,3,2,128]{3,2,1,0:T(2,128)(2,1)}), bf16[64,3,2,128]{3,2,1,0:T(2,128)(2,1)S(1)}, u32[]{:S(2)}, u32[]{:S(2)}) async-start(bf16[64,3,2,128]{3,2,1,0:T(2,128)(2,1)} %shard_map.75), calls=%async_computation.2 | async-start | bytes 196608 | tf_op jit(solution)/shard_map/all_to_all | solution.py:235
  51.8 0.0 copy-done.5
  51.8 10.4 %all-to-all-done.2.arrived_ref = bf16[64,3,2,128]{3,2,1,0:T(2,128)(2,1)S(1)} async-done(((bf16[64,3,2,128]{3,2,1,0:T(2,128)(2,1)}), bf16[64,3,2,128]{3,2,1,0:T(2,128)(2,1)S(1)}, u32[]{:S(2)}, u32[]{:S(2)}) %all-to-all-start.2) | async-done | bytes 98336 | tf_op jit(solution)/shard_map/all_to_all | solution.py:235
  62.3 0.0 copy-done.2
  62.3 1.0 shard_map.76
  63.3 15.6 %all_to_all.32.own_ref = bf16[64,3,4,128]{3,2,1,0:T(4,128)(2,1)S(1)} all-to-all(bf16[64,3,4,128]{3,2,1,0:T(4,128)(2,1)S(1)} %get-tuple-element.18), channel_id=1, replica_groups=mesh['yh'=2,'z2'=2,'z1'=2,'z0'=2,'x'=4,'yl'=4,'core'=2] {'yl','z1','yh',..., dimensions={0} | all-to-all | bytes 393216 | tf_op jit(solution)/shard_map/all_to_all | solution.py:240
  78.9 5.4 %all-gather.1 = bf16[128,3,4,128]{3,2,1,0:T(4,128)(2,1)S(1)} all-gather(bf16[64,3,4,128]{3,2,1,0:T(4,128)(2,1)S(1)} %all_to_all.32.own_ref), channel_id=3, replica_groups=mesh['yh'=2,'z2'=2,'z1'=2,'z0'=2,'x'=4,'yl'=4,'core'=2] {'core'}, dimensions={0}, use_global_device_ids=true | all-gather | bytes 589824 | tf_op jit(solution)/shard_map/all_gather | solution.py:241
  84.3 0.7 shard_map.77
  85.0 9.0 %all_to_all.33.parts_ref = bf16[4,96,384]{2,1,0:T(8,128)(2,1)S(1)} all-to-all(bf16[4,96,384]{2,1,0:T(8,128)(2,1)S(1)} %shard_map.77), channel_id=1, replica_groups=mesh['yh'=2,'z2'=2,'z1'=2,'z0'=2,'x'=4,'yl'=4,'core'=2] {'x'}, dimensions={0} | all-to-all | bytes 589824 | tf_op jit(solution)/shard_map/all_to_all | solution.py:243
  94.0 0.4 shard_map.78
  94.4 14.3 %all_to_all.34.arrived_ref = bf16[64,3,2,128]{3,2,1,0:T(2,128)(2,1)S(1)} all-to-all(bf16[64,3,2,128]{3,2,1,0:T(2,128)(2,1)S(1)} %shard_map.78), channel_id=1, replica_groups=mesh['yh'=2,'z2'=2,'z1'=2,'z0'=2,'x'=4,'yl'=4,'core'=2] {'yl','z1','yh',..., dimensions={0} | all-to-all | bytes 196608 | tf_op jit(solution)/shard_map/all_to_all | solution.py:245
  108.6 1.1 shard_map.79
  (2 shorter events, 0.0 us)
Async XLA Ops:
  0.0 1.1 copy-start.4
  0.0 1.1 copy-start.3
  30.2 4.6 %copy-start.1 = (bf16[512,384]{1,0:T(8,128)(2,1)S(1)}, bf16[512,384]{1,0:T(8,128)(2,1)}, u32[]{:S(2)}) copy-start(bf16[512,384]{1,0:T(8,128)(2,1)} %constant.4.clone.squeeze_ref) | copy-start | bytes 1179652
  35.3 10.4 %copy-start = (bf16[384,512]{1,0:T(8,128)(2,1)S(1)}, bf16[384,512]{1,0:T(8,128)(2,1)}, u32[]{:S(2)}) copy-start(bf16[384,512]{1,0:T(8,128)(2,1)} %constant.5.clone.stretch_ref) | copy-start | bytes 1179652
  47.1 4.7 %copy-start.5 = (f32[2,128]{1,0:T(2,128)S(1)}, f32[2,128]{1,0:T(2,128)}, u32[]{:S(2)}) copy-start(f32[2,128]{1,0:T(2,128)} %param.11) | copy-start | bytes 3076
  47.1 15.2 %copy-start.2 = (bf16[2,128,128]{2,1,0:T(8,128)(2,1)S(1)}, bf16[2,128,128]{2,1,0:T(8,128)(2,1)}, u32[]{:S(2)}) copy-start(bf16[2,128,128]{2,1,0:T(8,128)(2,1)} %out_weight_ref.3) | copy-start | bytes 196612
  47.1 15.2 %all-to-all-start.2 = ((bf16[64,3,2,128]{3,2,1,0:T(2,128)(2,1)}), bf16[64,3,2,128]{3,2,1,0:T(2,128)(2,1)S(1)}, u32[]{:S(2)}, u32[]{:S(2)}) async-start(bf16[64,3,2,128]{3,2,1,0:T(2,128)(2,1)} %shard_map.75), calls=%async_computation.2 | async-start | bytes 196608 | tf_op jit(solution)/shard_map/all_to_all | solution.py:235

commit v8 on v7

--- a/solution.py
+++ b/solution.py
@@ -118,7 +118,7 @@
 def start_kernel(pair_ref, weight_ref, gain_ref, out_ref, field_ref, gate_ref, scratch):
     field = widen_groups(pair_ref[...].reshape(288, H).astype(F32), scratch)
     field_ref[...] = field.astype(BF16)
-    normed = normalize(field, gain_ref[...], 1).astype(BF16)
+    normed = normalize(field, gain_ref[0:1], 1).astype(BF16)
     weight = weight_ref[...]
     out_ref[...] = spread_sides(normed, weight)
     gate_ref[...] = gate_of(normed, weight)
@@ -152,12 +152,12 @@
 
 
 def middle_kernel(
-    arrived_ref, field_ref, gate_ref, out_weight_ref, out_gain_ref, weight_ref, gain_ref, out_ref, first_ref, next_gate_ref
+    arrived_ref, field_ref, gate_ref, out_weight_ref, weight_ref, gain_ref, out_ref, first_ref, next_gate_ref
 ):
     first = finish(
-        arrived_ref[...], field_ref[...], gate_ref[...], out_weight_ref[0], out_gain_ref[...]
+        arrived_ref[...], field_ref[...], gate_ref[...], out_weight_ref[0], gain_ref[2:3]
     ).astype(BF16)
-    normed = normalize(first.astype(F32), gain_ref[...], 1).astype(BF16)
+    normed = normalize(first.astype(F32), gain_ref[1:2], 1).astype(BF16)
     weight = weight_ref[...]
     out_ref[...] = spread_sides(normed, weight)
     first_ref[...] = first
@@ -193,7 +193,7 @@
 
 def end_kernel(arrived_ref, field_ref, gate_ref, out_weight_ref, gain_ref, out_ref, scratch):
     final = finish(
-        arrived_ref[...], field_ref[...], gate_ref[...], out_weight_ref[1], gain_ref[...]
+        arrived_ref[...], field_ref[...], gate_ref[...], out_weight_ref[1], gain_ref[3:4]
     )
     for n in range(48):
         scratch[6 * n : 6 * n + 8, :] = final[8 * n : 8 * n + 8]
@@ -224,8 +224,9 @@
     block, blocks = ((192, 384), BF16), ((4, 96, 384), BF16)
     padded = pltpu.VMEM((296, H), F32)
 
+    gains = jnp.concatenate([in_gain, out_gain], axis=0)
     sent, field, gating = call(start_kernel, [sides, pairs, gates], [padded])(
-        pair_field, proj_weight[0], in_gain[:1]
+        pair_field, proj_weight[0], gains
     )
     own = exchange(sent, SPREAD)
     both = lax.all_gather(own, "core", axis=0, tiled=False)
@@ -235,7 +236,7 @@
     arrived = exchange(back, SPREAD)
 
     sent, field, gating = call(middle_kernel, [sides, pairs, gates])(
-        arrived, field, gating, out_weight, out_gain[:1], proj_weight[1], in_gain[1:]
+        arrived, field, gating, out_weight, proj_weight[1], gains
     )
     own = exchange(sent, SPREAD)
     both = lax.all_gather(own, "core", axis=0, tiled=False)
@@ -244,7 +245,7 @@
     [back] = call(sum_kernel, [results])(parts, stretch)
     arrived = exchange(back, SPREAD)
     [out] = call(end_kernel, [((6, 48, H), BF16)], [padded])(
-        arrived, field, gating, out_weight, out_gain[1:]
+        arrived, field, gating, out_weight, gains
     )
     return out
 

time: 111 us -> 109 us (0.982)
  blocking collectives: 87.8 us -> 102 us
  waiting for transfers between devices: 10.4 us -> 0 us
  starting transfers between devices: 4.72 us -> 0 us
    all_to_all x1 -> x2, blocking collectives: 14.3 us -> 28.7 us  [shards(): arrived = exchange(back, SPREAD)]
    all_to_all x1 -> x0, waiting for transfers between devices: 10.4 us -> none  [shards(): arrived = exchange(back, SPREAD)]
    all_to_all x1 -> x0, starting transfers between devices: 4.72 us -> none  [shards(): arrived = exchange(back, SPREAD)]
  transfers between devices with their start and end apart: 1 -> 0, of which waited for: 1 -> 0; matrix products, arithmetic and copies ran while one was open for 0% -> 0% of each run, Pallas kernels for 0% -> 0%
where the time goes in v8:
time: 109 us; the launch traced here: 108 us
  blocking collectives  102 us (94%)
  Pallas kernels  4.92 us (5%)
  local copies, waits for them, and re-layouts  1.09 us (1%)
    all_to_all x2, blocking collectives, shards(): own = exchange(sent, SPREAD)  44.1 us
    all_to_all x2, blocking collectives, shards(): arrived = exchange(back, SPREAD)  28.7 us
    all_to_all x1, blocking collectives, shards(): right = exchange(right, 'x')  10.4 us
    all_gather x2, blocking collectives, shards(): both = lax.all_gather(own, 'core', axis=0, tiled=False)  10.2 us
    all_to_all x1, blocking collectives, shards(): parts = exchange(parts, 'x')  8.99 us

profile of v8, /device:TPU:1, one launch (start us, length us, event | category | flops | bytes accessed | tf_op | source)
XLA Modules:
  0.0 108.5 jit_solution(15414185190743903781)
XLA Ops:
  0.0 0.0 copy-start.4
  0.0 0.0 copy-start.5
  0.0 0.0 copy-start.3
  0.0 1.1 slice_bitcast_fusion
  1.1 0.0 copy-done.4
  1.1 0.0 copy-done.5
  1.1 0.0 copy-done.3
  1.1 0.6 shard_map.73
  1.7 28.5 %all_to_all.30 = bf16[64,3,4,128]{3,2,1,0:T(4,128)(2,1)S(1)} all-to-all(bf16[64,3,4,128]{3,2,1,0:T(4,128)(2,1)S(1)} %get-tuple-element.13), channel_id=1, replica_groups=mesh['yh'=2,'z2'=2,'z1'=2,'z0'=2,'x'=4,'yl'=4,'core'=2] {'yl','z1','yh',..., dimensions={0} | all-to-all | bytes 393216 | tf_op jit(solution)/shard_map/all_to_all | solution.py:231
  30.2 0.0 copy-start.1
  30.2 4.6 %all-gather = bf16[128,3,4,128]{3,2,1,0:T(4,128)(2,1)S(1)} all-gather(bf16[64,3,4,128]{3,2,1,0:T(4,128)(2,1)S(1)} %all_to_all.30), channel_id=2, replica_groups=mesh['yh'=2,'z2'=2,'z1'=2,'z0'=2,'x'=4,'yl'=4,'core'=2] {'core'}, dimensions={0}, use_global_device_ids=true | all-gather | bytes 589824 | tf_op jit(solution)/shard_map/all_gather | solution.py:232
  34.8 0.0 copy-done.1
  34.8 0.5 shard_map.74
  35.3 0.0 copy-start
  35.3 10.4 %all_to_all.31.right_ref = bf16[4,96,384]{2,1,0:T(8,128)(2,1)S(1)} all-to-all(bf16[4,96,384]{2,1,0:T(8,128)(2,1)S(1)} %get-tuple-element.15), channel_id=1, replica_groups=mesh['yh'=2,'z2'=2,'z1'=2,'z0'=2,'x'=4,'yl'=4,'core'=2] {'x'}, dimensions={0} | all-to-all | bytes 589824 | tf_op jit(solution)/shard_map/all_to_all | solution.py:234
  45.7 0.0 copy-done
  45.7 0.7 shard_map.75
  46.5 0.0 copy-start.2
  46.5 14.4 %all_to_all.32.arrived_ref = bf16[64,3,2,128]{3,2,1,0:T(2,128)(2,1)S(1)} all-to-all(bf16[64,3,2,128]{3,2,1,0:T(2,128)(2,1)S(1)} %shard_map.75), channel_id=1, replica_groups=mesh['yh'=2,'z2'=2,'z1'=2,'z0'=2,'x'=4,'yl'=4,'core'=2] {'yl','z1','yh',..., dimensions={0} | all-to-all | bytes 196608 | tf_op jit(solution)/shard_map/all_to_all | solution.py:236
  60.9 0.0 copy-done.2
  60.9 1.0 shard_map.76
  61.9 15.6 %all_to_all.33.own_ref = bf16[64,3,4,128]{3,2,1,0:T(4,128)(2,1)S(1)} all-to-all(bf16[64,3,4,128]{3,2,1,0:T(4,128)(2,1)S(1)} %get-tuple-element.18), channel_id=1, replica_groups=mesh['yh'=2,'z2'=2,'z1'=2,'z0'=2,'x'=4,'yl'=4,'core'=2] {'yl','z1','yh',..., dimensions={0} | all-to-all | bytes 393216 | tf_op jit(solution)/shard_map/all_to_all | solution.py:241
  77.5 5.5 %all-gather.1 = bf16[128,3,4,128]{3,2,1,0:T(4,128)(2,1)S(1)} all-gather(bf16[64,3,4,128]{3,2,1,0:T(4,128)(2,1)S(1)} %all_to_all.33.own_ref), channel_id=3, replica_groups=mesh['yh'=2,'z2'=2,'z1'=2,'z0'=2,'x'=4,'yl'=4,'core'=2] {'core'}, dimensions={0}, use_global_device_ids=true | all-gather | bytes 589824 | tf_op jit(solution)/shard_map/all_gather | solution.py:242
  83.1 0.7 shard_map.77
  83.7 9.0 %all_to_all.34.parts_ref = bf16[4,96,384]{2,1,0:T(8,128)(2,1)S(1)} all-to-all(bf16[4,96,384]{2,1,0:T(8,128)(2,1)S(1)} %shard_map.77), channel_id=1, replica_groups=mesh['yh'=2,'z2'=2,'z1'=2,'z0'=2,'x'=4,'yl'=4,'core'=2] {'x'}, dimensions={0} | all-to-all | bytes 589824 | tf_op jit(solution)/shard_map/all_to_all | solution.py:244
  92.7 0.4 shard_map.78
  93.1 14.3 %all_to_all.35.arrived_ref = bf16[64,3,2,128]{3,2,1,0:T(2,128)(2,1)S(1)} all-to-all(bf16[64,3,2,128]{3,2,1,0:T(2,128)(2,1)S(1)} %shard_map.78), channel_id=1, replica_groups=mesh['yh'=2,'z2'=2,'z1'=2,'z0'=2,'x'=4,'yl'=4,'core'=2] {'yl','z1','yh',..., dimensions={0} | all-to-all | bytes 196608 | tf_op jit(solution)/shard_map/all_to_all | solution.py:246
  107.4 1.1 shard_map.79
  (1 shorter events, 0.0 us)
Async XLA Ops:
  0.0 1.1 copy-start.4
  0.0 1.1 %copy-start.5 = (f32[2,128]{1,0:T(2,128)S(1)}, f32[2,128]{1,0:T(2,128)}, u32[]{:S(2)}) copy-start(f32[2,128]{1,0:T(2,128)} %param.10) | copy-start | bytes 3076
  0.0 1.1 %copy-start.3 = (bf16[6,48,128]{2,1,0:T(8,128)(2,1)S(1)}, bf16[6,48,128]{2,1,0:T(8,128)(2,1)}, u32[]{:S(2)}) copy-start(bf16[6,48,128]{2,1,0:T(8,128)(2,1)} %pair_ref.1) | copy-start | bytes 221188
  30.2 4.6 %copy-start.1 = (bf16[512,384]{1,0:T(8,128)(2,1)S(1)}, bf16[512,384]{1,0:T(8,128)(2,1)}, u32[]{:S(2)}) copy-start(bf16[512,384]{1,0:T(8,128)(2,1)} %constant.4.clone.squeeze_ref) | copy-start | bytes 1179652
  35.3 10.4 %copy-start = (bf16[384,512]{1,0:T(8,128)(2,1)S(1)}, bf16[384,512]{1,0:T(8,128)(2,1)}, u32[]{:S(2)}) copy-start(bf16[384,512]{1,0:T(8,128)(2,1)} %constant.5.clone.stretch_ref) | copy-start | bytes 1179652
  46.5 14.4 %copy-start.2 = (bf16[2,128,128]{2,1,0:T(8,128)(2,1)S(1)}, bf16[2,128,128]{2,1,0:T(8,128)(2,1)}, u32[]{:S(2)}) copy-start(bf16[2,128,128]{2,1,0:T(8,128)(2,1)} %out_weight_ref.3) | copy-start | bytes 196612

commit v9 on v8

--- a/solution.py
+++ b/solution.py
@@ -59,11 +59,12 @@
     return jax.nn.sigmoid(jnp.dot(normed, weight[:, 4 * H :], preferred_element_type=F32))
 
 
-def finish(arrived, field, gating, weight, gain):
+def summed_rows(arrived):
     by_row = jnp.swapaxes(arrived.astype(F32).reshape(HALF, 6, H), 0, 1)
-    summed = jnp.concatenate(
-        [jnp.concatenate([by_row[3 * channel + t] for t in range(3)], axis=1) for channel in range(2)], axis=0
-    )
+    return [jnp.concatenate([by_row[t], by_row[3 + t]], axis=0) for t in range(3)]
+
+
+def finish(summed, field, gating, weight, gain):
     column = jnp.swapaxes(jnp.broadcast_to(gain, (8, H)), 0, 1)[:, :1]
     mixed = normalize(summed, column, 0).astype(BF16)
     update = lax.dot_general(
@@ -99,7 +100,8 @@
     ).astype(BF16)
 
 
-def send_back(wide):
+def send_back(product, stretch):
+    wide = jnp.dot(product.astype(BF16), stretch, preferred_element_type=F32)
     rows = []
     for channel in range(2):
         for t in range(3):
@@ -139,26 +141,24 @@
 
 
 def outgoing_kernel(left_ref, right_ref, stretch_ref, out_ref):
-    wide = []
-    for channel in range(2):
-        product = lax.dot_general(
-            left_ref[96 * channel : 96 * channel + 96],
-            right_ref[:, 48 * channel : 48 * channel + 48].reshape(192, 384),
-            (((1,), (1,)), ((), ())),
-            preferred_element_type=F32,
-        ).astype(BF16)
-        wide.append(jnp.dot(product, stretch_ref[:192, :256], preferred_element_type=F32))
-    out_ref[...] = send_back(jnp.concatenate(wide, axis=1))
+    left = jnp.concatenate([left_ref[:96], left_ref[96:]], axis=1)
+    none = jnp.zeros((192, 384), BF16)
+    right = [right_ref[:, 48 * channel : 48 * channel + 48].reshape(192, 384) for channel in range(2)]
+    right = jnp.concatenate(
+        [jnp.concatenate([right[0], none], axis=1), jnp.concatenate([none, right[1]], axis=1)], axis=0
+    )
+    product = lax.dot_general(left, right, (((1,), (1,)), ((), ())), preferred_element_type=F32)
+    out_ref[...] = send_back(product, stretch_ref[...])
 
 
 def middle_kernel(
     arrived_ref, field_ref, gate_ref, out_weight_ref, weight_ref, gain_ref, out_ref, first_ref, next_gate_ref
 ):
     first = finish(
-        arrived_ref[...], field_ref[...], gate_ref[...], out_weight_ref[0], gain_ref[2:3]
+        jnp.concatenate(summed_rows(arrived_ref[...]), axis=1), field_ref[...], gate_ref[...], out_weight_ref[0], gain_ref[2:3]
     ).astype(BF16)
     normed = normalize(first.astype(F32), gain_ref[1:2], 1).astype(BF16)
-    weight = weight_ref[...]
+    weight = weight_ref[1]
     out_ref[...] = spread_sides(normed, weight)
     first_ref[...] = first
     next_gate_ref[...] = gate_of(normed, weight)
@@ -188,16 +188,23 @@
     total = parts_ref[0].astype(F32)
     for x in range(1, 4):
         total = total + parts_ref[x].astype(F32)
-    out_ref[...] = send_back(jnp.dot(total.astype(BF16), stretch_ref[...], preferred_element_type=F32))
-
-
-def end_kernel(arrived_ref, field_ref, gate_ref, out_weight_ref, gain_ref, out_ref, scratch):
-    final = finish(
-        arrived_ref[...], field_ref[...], gate_ref[...], out_weight_ref[1], gain_ref[3:4]
-    )
-    for n in range(48):
-        scratch[6 * n : 6 * n + 8, :] = final[8 * n : 8 * n + 8]
-    out_ref[...] = scratch[0:288, :].reshape(6, 48, H).astype(BF16)
+    out_ref[...] = send_back(total, stretch_ref[...])
+
+
+def end_kernel(arrived_ref, field_ref, gate_ref, out_weight_ref, gain_ref, out_hbm, scratch, stage, sems):
+    copies = []
+    for t, summed in enumerate(summed_rows(arrived_ref[...])):
+        pairs = slice(H * t, H * t + H)
+        final = finish(summed, field_ref[pairs], gate_ref[pairs], out_weight_ref[1], gain_ref[3:4])
+        for n in range(16):
+            scratch[t, 6 * n : 6 * n + 8, :] = final[8 * n : 8 * n + 8]
+        stage[2 * t : 2 * t + 2] = scratch[t, :96].reshape(2, 48, H).astype(BF16)
+        copies.append(
+            pltpu.make_async_copy(stage.at[2 * t : 2 * t + 2], out_hbm.at[2 * t : 2 * t + 2], sems.at[t])
+        )
+        copies[t].start()
+    for copy in copies:
+        copy.wait()
 
 
 def squeeze_matrix():
@@ -206,13 +213,14 @@
     return np.kron(np.eye(2, dtype=bool), block).astype(jnp.bfloat16)
 
 
-def call(kernel, outs, scratch=()):
+def call(kernel, outs, scratch=(), **specs):
     return pl.pallas_call(
         kernel,
         out_shape=[jax.ShapeDtypeStruct(shape, dtype) for shape, dtype in outs],
         scratch_shapes=list(scratch),
         compiler_params=pltpu.CompilerParams(vmem_limit_bytes=48 * 1024 * 1024),
         cost_estimate=pl.CostEstimate(flops=20_000_000, bytes_accessed=1_000_000, transcendentals=100_000),
+        **specs,
     )
 
 
@@ -236,7 +244,7 @@
     arrived = exchange(back, SPREAD)
 
     sent, field, gating = call(middle_kernel, [sides, pairs, gates])(
-        arrived, field, gating, out_weight, proj_weight[1], gains
+        arrived, field, gating, out_weight, proj_weight, gains
     )
     own = exchange(sent, SPREAD)
     both = lax.all_gather(own, "core", axis=0, tiled=False)
@@ -244,9 +252,12 @@
     parts = exchange(parts, "x")
     [back] = call(sum_kernel, [results])(parts, stretch)
     arrived = exchange(back, SPREAD)
-    [out] = call(end_kernel, [((6, 48, H), BF16)], [padded])(
-        arrived, field, gating, out_weight, gains
-    )
+    [out] = call(
+        end_kernel,
+        [((6, 48, H), BF16)],
+        [pltpu.VMEM((3, 104, H), F32), pltpu.VMEM((6, 48, H), BF16), pltpu.SemaphoreType.DMA((3,))],
+        out_specs=[pl.BlockSpec(memory_space=pl.ANY)],
+    )(arrived, field, gating, out_weight, gains)
     return out
 
 

time: 109 us -> 109 us (level)
  no operation moved by 1% of the time
where the time goes in v9:
time: 109 us; the launch traced here: 108 us
  blocking collectives  102 us (94%)
  Pallas kernels  4.94 us (5%)
    all_to_all x2, blocking collectives, shards(): own = exchange(sent, SPREAD)  44.1 us
    all_to_all x2, blocking collectives, shards(): arrived = exchange(back, SPREAD)  28.7 us
    all_to_all x1, blocking collectives, shards(): right = exchange(right, 'x')  10.4 us
    all_gather x2, blocking collectives, shards(): both = lax.all_gather(own, 'core', axis=0, tiled=False)  10.2 us
    all_to_all x1, blocking collectives, shards(): parts = exchange(parts, 'x')  8.99 us

profile of v9, /device:TPU:1, one launch (start us, length us, event | category | flops | bytes accessed | tf_op | source)
XLA Modules:
  0.0 108.4 jit_solution(15231589039688475213)
XLA Ops:
  0.0 0.0 copy-start.5
  0.0 0.0 copy-start.6
  0.0 0.0 copy-start.4
  0.0 1.0 slice_bitcast_fusion.weight_ref
  1.0 0.0 copy-done.5
  1.0 0.0 copy-done.6
  1.0 0.0 copy-done.4
  1.0 0.6 shard_map.73
  1.6 28.5 %all_to_all.30 = bf16[64,3,4,128]{3,2,1,0:T(4,128)(2,1)S(1)} all-to-all(bf16[64,3,4,128]{3,2,1,0:T(4,128)(2,1)S(1)} %get-tuple-element.13), channel_id=1, replica_groups=mesh['yh'=2,'z2'=2,'z1'=2,'z0'=2,'x'=4,'yl'=4,'core'=2] {'yl','z1','yh',..., dimensions={0} | all-to-all | bytes 393216 | tf_op jit(solution)/shard_map/all_to_all | solution.py:239
  30.1 0.0 copy-start.1
  30.1 4.6 %all-gather = bf16[128,3,4,128]{3,2,1,0:T(4,128)(2,1)S(1)} all-gather(bf16[64,3,4,128]{3,2,1,0:T(4,128)(2,1)S(1)} %all_to_all.30), channel_id=2, replica_groups=mesh['yh'=2,'z2'=2,'z1'=2,'z0'=2,'x'=4,'yl'=4,'core'=2] {'core'}, dimensions={0}, use_global_device_ids=true | all-gather | bytes 589824 | tf_op jit(solution)/shard_map/all_gather | solution.py:240
  34.7 0.0 copy-done.1
  34.7 0.5 shard_map.74
  35.2 0.0 copy-start
  35.2 10.4 %all_to_all.31.right_ref = bf16[4,96,384]{2,1,0:T(8,128)(2,1)S(1)} all-to-all(bf16[4,96,384]{2,1,0:T(8,128)(2,1)S(1)} %get-tuple-element.15), channel_id=1, replica_groups=mesh['yh'=2,'z2'=2,'z1'=2,'z0'=2,'x'=4,'yl'=4,'core'=2] {'x'}, dimensions={0} | all-to-all | bytes 589824 | tf_op jit(solution)/shard_map/all_to_all | solution.py:242
  45.6 0.0 copy-done
  45.6 0.0 copy-start.2
  45.6 0.7 shard_map.75
  46.4 0.0 copy-start.3
  46.4 14.4 %all_to_all.32.arrived_ref = bf16[64,3,2,128]{3,2,1,0:T(2,128)(2,1)S(1)} all-to-all(bf16[64,3,2,128]{3,2,1,0:T(2,128)(2,1)S(1)} %shard_map.75), channel_id=1, replica_groups=mesh['yh'=2,'z2'=2,'z1'=2,'z0'=2,'x'=4,'yl'=4,'core'=2] {'yl','z1','yh',..., dimensions={0} | all-to-all | bytes 196608 | tf_op jit(solution)/shard_map/all_to_all | solution.py:244
  60.8 0.0 copy-done.2
  60.8 0.0 copy-done.3
  60.8 1.0 shard_map.76
  61.8 15.6 %all_to_all.33.own_ref = bf16[64,3,4,128]{3,2,1,0:T(4,128)(2,1)S(1)} all-to-all(bf16[64,3,4,128]{3,2,1,0:T(4,128)(2,1)S(1)} %get-tuple-element.18), channel_id=1, replica_groups=mesh['yh'=2,'z2'=2,'z1'=2,'z0'=2,'x'=4,'yl'=4,'core'=2] {'yl','z1','yh',..., dimensions={0} | all-to-all | bytes 393216 | tf_op jit(solution)/shard_map/all_to_all | solution.py:249
  77.4 5.5 %all-gather.1 = bf16[128,3,4,128]{3,2,1,0:T(4,128)(2,1)S(1)} all-gather(bf16[64,3,4,128]{3,2,1,0:T(4,128)(2,1)S(1)} %all_to_all.33.own_ref), channel_id=3, replica_groups=mesh['yh'=2,'z2'=2,'z1'=2,'z0'=2,'x'=4,'yl'=4,'core'=2] {'core'}, dimensions={0}, use_global_device_ids=true | all-gather | bytes 589824 | tf_op jit(solution)/shard_map/all_gather | solution.py:250
  82.9 0.7 shard_map.77
  83.6 9.0 %all_to_all.34.parts_ref = bf16[4,96,384]{2,1,0:T(8,128)(2,1)S(1)} all-to-all(bf16[4,96,384]{2,1,0:T(8,128)(2,1)S(1)} %shard_map.77), channel_id=1, replica_groups=mesh['yh'=2,'z2'=2,'z1'=2,'z0'=2,'x'=4,'yl'=4,'core'=2] {'x'}, dimensions={0} | all-to-all | bytes 589824 | tf_op jit(solution)/shard_map/all_to_all | solution.py:252
  92.6 0.4 shard_map.78
  93.0 14.3 %all_to_all.35.arrived_ref = bf16[64,3,2,128]{3,2,1,0:T(2,128)(2,1)S(1)} all-to-all(bf16[64,3,2,128]{3,2,1,0:T(2,128)(2,1)S(1)} %shard_map.78), channel_id=1, replica_groups=mesh['yh'=2,'z2'=2,'z1'=2,'z0'=2,'x'=4,'yl'=4,'core'=2] {'yl','z1','yh',..., dimensions={0} | all-to-all | bytes 196608 | tf_op jit(solution)/shard_map/all_to_all | solution.py:254
  107.3 1.1 %shard_map.79 = bf16[6,48,128]{2,1,0:T(8,128)(2,1)} custom-call(bf16[64,3,2,128]{3,2,1,0:T(2,128)(2,1)S(1)} %all_to_all.35.arrived_ref, bf16[384,128]{1,0:T(8,128)(2,1)S(1)} %get-tuple-element.19.field_ref, f32[384,128]{1,0:T(8,128)S(1)} %get-tuple-element.20.gate_ref, bf16[2,128,128]{2,1,0:T(8,128)(2,1)S(1)} %copy-done.3, f32[4,128]{1,0:T(4,128)S(1)} %pad_maximum_fusion.gain_ref), custom_call_target="tpu_custom_call" | custom-call | flops 20000000 | bytes 1000000 | tf_op jit(solution)/shard_map/pallas_call | solution.py:255
  (1 shorter events, 0.0 us)
Async XLA Ops:
  0.0 1.0 copy-start.5
  0.0 1.0 copy-start.6
  0.0 1.0 copy-start.4
  30.1 4.6 %copy-start.1 = (bf16[512,384]{1,0:T(8,128)(2,1)S(1)}, bf16[512,384]{1,0:T(8,128)(2,1)}, u32[]{:S(2)}) copy-start(bf16[512,384]{1,0:T(8,128)(2,1)} %constant.4.clone.squeeze_ref) | copy-start | bytes 1179652
  35.2 10.4 %copy-start = (bf16[384,512]{1,0:T(8,128)(2,1)S(1)}, bf16[384,512]{1,0:T(8,128)(2,1)}, u32[]{:S(2)}) copy-start(bf16[384,512]{1,0:T(8,128)(2,1)} %constant.5.clone.stretch_ref) | copy-start | bytes 1179652
  45.6 15.1 %copy-start.2 = (bf16[2,128,640]{2,1,0:T(8,128)(2,1)S(1)}, bf16[2,128,640]{2,1,0:T(8,128)(2,1)}, u32[]{:S(2)}) copy-start(bf16[2,128,640]{2,1,0:T(8,128)(2,1)} %weight_ref.1) | copy-start | bytes 983044
  46.4 14.4 %copy-start.3 = (bf16[2,128,128]{2,1,0:T(8,128)(2,1)S(1)}, bf16[2,128,128]{2,1,0:T(8,128)(2,1)}, u32[]{:S(2)}) copy-start(bf16[2,128,128]{2,1,0:T(8,128)(2,1)} %out_weight_ref.3) | copy-start | bytes 196612

commit v10 on v9

--- a/solution.py
+++ b/solution.py
@@ -32,27 +32,21 @@
     return jnp.swapaxes(jnp.stack(rows, axis=0), 0, 1)
 
 
-def widen_groups(values, scratch):
-    scratch[0:288, :] = values
-    keep = lax.broadcasted_iota(jnp.int32, (8, H), 0) < 6
-    return jnp.concatenate(
-        [jnp.where(keep, scratch[6 * n : 6 * n + 8, :], 0.0) for n in range(48)], axis=0
-    )
-
-
 def spread_sides(normed, weight):
     projected = lax.dot_general(
         weight[:, : 4 * H], normed, (((0,), (1,)), ((), ())), preferred_element_type=F32
     )
-    rows = []
+    rows, ends = [], []
     for side in range(2):
         value = projected[2 * side * H : (2 * side + 1) * H]
         gate = projected[(2 * side + 1) * H : (2 * side + 2) * H]
         turned = jax.nn.sigmoid(gate) * value
         for channel in range(2):
             part = turned[channel * HALF : (channel + 1) * HALF]
-            rows.extend(part[:, t * H : (t + 1) * H] for t in range(3))
-    return by_device(rows).reshape(HALF, 3, 4, H).astype(BF16)
+            rows.extend([part[:, :H], part[:, H : 2 * H]])
+            ends.append(part[:, 2 * H :])
+    rows.extend([jnp.concatenate(ends, axis=1), jnp.zeros((HALF, H), F32)])
+    return by_device(rows).reshape(HALF, 5, 2, H).astype(BF16)
 
 
 def gate_of(normed, weight):
@@ -61,7 +55,7 @@
 
 def summed_rows(arrived):
     by_row = jnp.swapaxes(arrived.astype(F32).reshape(HALF, 6, H), 0, 1)
-    return [jnp.concatenate([by_row[t], by_row[3 + t]], axis=0) for t in range(3)]
+    return jnp.concatenate([jnp.concatenate([by_row[t], by_row[3 + t]], axis=0) for t in range(3)], axis=1)
 
 
 def finish(summed, field, gating, weight, gain):
@@ -70,22 +64,41 @@
     update = lax.dot_general(
         mixed, weight, (((0,), (0,)), ((), ())), preferred_element_type=F32
     )
+    update = jnp.concatenate([update[HALF * a : HALF * a + 48] for a in range(6)], axis=0)
     return field.astype(F32) + gating * update
 
 
 def rows_of(own):
-    return jnp.swapaxes(own.astype(F32).reshape(HALF, 12, H), 0, 1)
+    return jnp.swapaxes(own.astype(F32).reshape(HALF, 10, H), 0, 1)
+
+
+def moved(tile, lanes):
+    return pltpu.roll(tile, lanes % H, 1) if lanes % H else tile
 
 
 def matrix(by_row, side, channel):
+    q = 2 * side + channel
+    lane = lax.broadcasted_iota(jnp.int32, (16, H), 1)
+    cut = lax.broadcasted_iota(jnp.int32, (HALF, H), 1) >= 96
+    first, second, last = by_row[2 * q], by_row[2 * q + 1], by_row[8]
+    across = jnp.where(cut, first, second)
+    begins = ((first, 0), (first, 48), (across, 96), (second, 16), (second, 64), (second, 112))
     found = ([], [])
-    for t in range(3):
-        part = by_row[6 * side + 3 * channel + t]
-        tiles = [halves(part[32 * u : 32 * u + 16], part[32 * u + 16 : 32 * u + 32]) for u in range(2)]
-        for e in range(2):
-            both = jnp.concatenate([tile[e] for tile in tiles], axis=1)
-            for z1 in range(2):
-                found[z1].append(both[8 * z1 : 8 * z1 + 8])
+    for a in range(6):
+        row, begin = begins[a]
+        tiles = []
+        for u in range(2):
+            pair = []
+            for e in range(2):
+                at = slice(32 * u + 16 * e, 32 * u + 16 * e + 16)
+                piece = moved(row[at], HALF * e - begin)
+                if a == 5:
+                    piece = jnp.where(lane < HALF * e + 16, piece, moved(last[at], HALF * e + 16 - 32 * q))
+                pair.append(piece)
+            tiles.append(jnp.where(lane < HALF, *pair))
+        both = jnp.concatenate(tiles, axis=1)
+        for half in range(2):
+            found[half].append(both[8 * half : 8 * half + 8])
     return [jnp.concatenate(pieces, axis=0) for pieces in found]
 
 
@@ -117,9 +130,8 @@
     return by_device(rows).reshape(HALF, 3, 2, H).astype(BF16)
 
 
-def start_kernel(pair_ref, weight_ref, gain_ref, out_ref, field_ref, gate_ref, scratch):
-    field = widen_groups(pair_ref[...].reshape(288, H).astype(F32), scratch)
-    field_ref[...] = field.astype(BF16)
+def start_kernel(pair_ref, weight_ref, gain_ref, out_ref, gate_ref):
+    field = pair_ref[...].reshape(288, H).astype(F32)
     normed = normalize(field, gain_ref[0:1], 1).astype(BF16)
     weight = weight_ref[...]
     out_ref[...] = spread_sides(normed, weight)
@@ -155,12 +167,12 @@
     arrived_ref, field_ref, gate_ref, out_weight_ref, weight_ref, gain_ref, out_ref, first_ref, next_gate_ref
 ):
     first = finish(
-        jnp.concatenate(summed_rows(arrived_ref[...]), axis=1), field_ref[...], gate_ref[...], out_weight_ref[0], gain_ref[2:3]
+        summed_rows(arrived_ref[...]), field_ref[...].reshape(288, H), gate_ref[...], out_weight_ref[0], gain_ref[2:3]
     ).astype(BF16)
     normed = normalize(first.astype(F32), gain_ref[1:2], 1).astype(BF16)
     weight = weight_ref[1]
     out_ref[...] = spread_sides(normed, weight)
-    first_ref[...] = first
+    first_ref[...] = first.reshape(6, 48, H)
     next_gate_ref[...] = gate_of(normed, weight)
 
 
@@ -191,24 +203,16 @@
     out_ref[...] = send_back(total, stretch_ref[...])
 
 
-def end_kernel(arrived_ref, field_ref, gate_ref, out_weight_ref, gain_ref, out_hbm, scratch, stage, sems):
-    copies = []
-    for t, summed in enumerate(summed_rows(arrived_ref[...])):
-        pairs = slice(H * t, H * t + H)
-        final = finish(summed, field_ref[pairs], gate_ref[pairs], out_weight_ref[1], gain_ref[3:4])
-        for n in range(16):
-            scratch[t, 6 * n : 6 * n + 8, :] = final[8 * n : 8 * n + 8]
-        stage[2 * t : 2 * t + 2] = scratch[t, :96].reshape(2, 48, H).astype(BF16)
-        copies.append(
-            pltpu.make_async_copy(stage.at[2 * t : 2 * t + 2], out_hbm.at[2 * t : 2 * t + 2], sems.at[t])
-        )
-        copies[t].start()
-    for copy in copies:
-        copy.wait()
+def end_kernel(arrived_ref, field_ref, gate_ref, out_weight_ref, gain_ref, out_ref):
+    final = finish(
+        summed_rows(arrived_ref[...]), field_ref[...].reshape(288, H), gate_ref[...], out_weight_ref[1], gain_ref[3:4]
+    )
+    out_ref[...] = final.reshape(6, 48, H).astype(BF16)
 
 
 def squeeze_matrix():
-    places = np.arange(256).reshape(2, 2, 2, 4, 8)[..., :6].transpose(3, 4, 0, 1, 2).reshape(-1)
+    places = np.pad(np.ones((4, 48), bool), ((0, 0), (0, 16))).reshape(-1).nonzero()[0]
+    places = places.reshape(2, 2, 2, 4, 6).transpose(3, 4, 0, 1, 2).reshape(-1)
     block = np.arange(256)[:, None] == places[None, :]
     return np.kron(np.eye(2, dtype=bool), block).astype(jnp.bfloat16)
 
@@ -227,15 +231,12 @@
 def shards(pair_field, proj_weight, out_weight, in_gain, out_gain):
     exchange = functools.partial(lax.all_to_all, split_axis=0, concat_axis=0, tiled=True)
     squeeze, stretch = jnp.asarray(squeeze_matrix()), jnp.asarray(squeeze_matrix().T)
-    pairs, gates = ((384, H), BF16), ((384, H), F32)
-    sides, results = ((HALF, 3, 4, H), BF16), ((HALF, 3, 2, H), BF16)
+    pairs, gates = ((6, 48, H), BF16), ((288, H), F32)
+    sides, results = ((HALF, 5, 2, H), BF16), ((HALF, 3, 2, H), BF16)
     block, blocks = ((192, 384), BF16), ((4, 96, 384), BF16)
-    padded = pltpu.VMEM((296, H), F32)
 
     gains = jnp.concatenate([in_gain, out_gain], axis=0)
-    sent, field, gating = call(start_kernel, [sides, pairs, gates], [padded])(
-        pair_field, proj_weight[0], gains
-    )
+    sent, gating = call(start_kernel, [sides, gates])(pair_field, proj_weight[0], gains)
     own = exchange(sent, SPREAD)
     both = lax.all_gather(own, "core", axis=0, tiled=False)
     left, right = call(pack_kernel, [block, blocks])(both, squeeze)
@@ -243,8 +244,8 @@
     [back] = call(outgoing_kernel, [results])(left, right, stretch)
     arrived = exchange(back, SPREAD)
 
-    sent, field, gating = call(middle_kernel, [sides, pairs, gates])(
-        arrived, field, gating, out_weight, proj_weight, gains
+    sent, first_pair, gating = call(middle_kernel, [sides, pairs, gates])(
+        arrived, pair_field, gating, out_weight, proj_weight, gains
     )
     own = exchange(sent, SPREAD)
     both = lax.all_gather(own, "core", axis=0, tiled=False)
@@ -252,12 +253,7 @@
     parts = exchange(parts, "x")
     [back] = call(sum_kernel, [results])(parts, stretch)
     arrived = exchange(back, SPREAD)
-    [out] = call(
-        end_kernel,
-        [((6, 48, H), BF16)],
-        [pltpu.VMEM((3, 104, H), F32), pltpu.VMEM((6, 48, H), BF16), pltpu.SemaphoreType.DMA((3,))],
-        out_specs=[pl.BlockSpec(memory_space=pl.ANY)],
-    )(arrived, field, gating, out_weight, gains)
+    [out] = call(end_kernel, [pairs])(arrived, first_pair, gating, out_weight, gains)
     return out
 
 

time: 109 us -> 108 us (level)
  no operation moved by 1% of the time
where the time goes in v10:
time: 108 us
  blocking collectives  101 us (94%)
  Pallas kernels  5.21 us (5%)
    all_to_all x2, blocking collectives, shards(): own = exchange(sent, SPREAD)  43.4 us
    all_to_all x2, blocking collectives, shards(): arrived = exchange(back, SPREAD)  28.6 us
    all_to_all x1, blocking collectives, shards(): right = exchange(right, 'x')  10.4 us
    all_gather x2, blocking collectives, shards(): both = lax.all_gather(own, 'core', axis=0, tiled=False)  9.81 us
    all_to_all x1, blocking collectives, shards(): parts = exchange(parts, 'x')  8.99 us

profile of v10, /device:TPU:1, one launch (start us, length us, event | category | flops | bytes accessed | tf_op | source)
XLA Modules:
  0.0 107.6 jit_solution(11308359457548395925)
XLA Ops:
  0.0 0.0 copy-start.5
  0.0 0.0 copy-start.6
  0.0 0.0 copy-start.3
  0.0 1.0 slice_bitcast_fusion.weight_ref
  1.0 0.0 copy-done.5
  1.0 0.0 copy-done.6
  1.0 0.0 copy-done.3
  1.0 0.6 shard_map.73
  1.6 0.0 copy-start.1
  1.7 28.2 %all_to_all.30 = bf16[64,5,2,128]{3,2,1,0:T(2,128)(2,1)S(1)} all-to-all(bf16[64,5,2,128]{3,2,1,0:T(2,128)(2,1)S(1)} %get-tuple-element.12), channel_id=1, replica_groups=mesh['yh'=2,'z2'=2,'z1'=2,'z0'=2,'x'=4,'yl'=4,'core'=2] {'yl','z1','yh',..., dimensions={0} | all-to-all | bytes 327680 | tf_op jit(solution)/shard_map/all_to_all | solution.py:240
  29.9 4.2 %all-gather = bf16[128,5,2,128]{3,2,1,0:T(2,128)(2,1)S(1)} all-gather(bf16[64,5,2,128]{3,2,1,0:T(2,128)(2,1)S(1)} %all_to_all.30), channel_id=2, replica_groups=mesh['yh'=2,'z2'=2,'z1'=2,'z0'=2,'x'=4,'yl'=4,'core'=2] {'core'}, dimensions={0}, use_global_device_ids=true | all-gather | bytes 491520 | tf_op jit(solution)/shard_map/all_gather | solution.py:241
  34.1 0.0 copy-done.1
  34.1 0.6 shard_map.74
  34.7 0.0 copy-start
  34.7 10.4 %all_to_all.31.right_ref = bf16[4,96,384]{2,1,0:T(8,128)(2,1)S(1)} all-to-all(bf16[4,96,384]{2,1,0:T(8,128)(2,1)S(1)} %get-tuple-element.14), channel_id=1, replica_groups=mesh['yh'=2,'z2'=2,'z1'=2,'z0'=2,'x'=4,'yl'=4,'core'=2] {'x'}, dimensions={0} | all-to-all | bytes 589824 | tf_op jit(solution)/shard_map/all_to_all | solution.py:243
  45.1 0.0 copy-done
  45.1 0.0 copy-start.2
  45.1 0.7 shard_map.75
  45.8 0.0 copy-start.4
  45.8 14.4 %all_to_all.32.arrived_ref = bf16[64,3,2,128]{3,2,1,0:T(2,128)(2,1)S(1)} all-to-all(bf16[64,3,2,128]{3,2,1,0:T(2,128)(2,1)S(1)} %shard_map.75), channel_id=1, replica_groups=mesh['yh'=2,'z2'=2,'z1'=2,'z0'=2,'x'=4,'yl'=4,'core'=2] {'yl','z1','yh',..., dimensions={0} | all-to-all | bytes 196608 | tf_op jit(solution)/shard_map/all_to_all | solution.py:245
  60.2 0.0 copy-done.2
  60.2 0.0 copy-done.4
  60.2 1.1 shard_map.76
  61.3 15.2 %all_to_all.33.own_ref = bf16[64,5,2,128]{3,2,1,0:T(2,128)(2,1)S(1)} all-to-all(bf16[64,5,2,128]{3,2,1,0:T(2,128)(2,1)S(1)} %get-tuple-element.16), channel_id=1, replica_groups=mesh['yh'=2,'z2'=2,'z1'=2,'z0'=2,'x'=4,'yl'=4,'core'=2] {'yl','z1','yh',..., dimensions={0} | all-to-all | bytes 327680 | tf_op jit(solution)/shard_map/all_to_all | solution.py:250
  76.4 5.6 %all-gather.1 = bf16[128,5,2,128]{3,2,1,0:T(2,128)(2,1)S(1)} all-gather(bf16[64,5,2,128]{3,2,1,0:T(2,128)(2,1)S(1)} %all_to_all.33.own_ref), channel_id=3, replica_groups=mesh['yh'=2,'z2'=2,'z1'=2,'z0'=2,'x'=4,'yl'=4,'core'=2] {'core'}, dimensions={0}, use_global_device_ids=true | all-gather | bytes 491520 | tf_op jit(solution)/shard_map/all_gather | solution.py:251
  82.1 0.8 shard_map.77
  82.9 9.0 %all_to_all.34.parts_ref = bf16[4,96,384]{2,1,0:T(8,128)(2,1)S(1)} all-to-all(bf16[4,96,384]{2,1,0:T(8,128)(2,1)S(1)} %shard_map.77), channel_id=1, replica_groups=mesh['yh'=2,'z2'=2,'z1'=2,'z0'=2,'x'=4,'yl'=4,'core'=2] {'x'}, dimensions={0} | all-to-all | bytes 589824 | tf_op jit(solution)/shard_map/all_to_all | solution.py:253
  91.8 0.4 shard_map.78
  92.3 14.3 %all_to_all.35.arrived_ref = bf16[64,3,2,128]{3,2,1,0:T(2,128)(2,1)S(1)} all-to-all(bf16[64,3,2,128]{3,2,1,0:T(2,128)(2,1)S(1)} %shard_map.78), channel_id=1, replica_groups=mesh['yh'=2,'z2'=2,'z1'=2,'z0'=2,'x'=4,'yl'=4,'core'=2] {'yl','z1','yh',..., dimensions={0} | all-to-all | bytes 196608 | tf_op jit(solution)/shard_map/all_to_all | solution.py:255
  106.5 1.0 shard_map.79
  (1 shorter events, 0.0 us)
Async XLA Ops:
  0.0 1.0 copy-start.5
  0.0 1.0 copy-start.6
  0.0 1.0 copy-start.3
  1.6 32.4 %copy-start.1 = (bf16[512,384]{1,0:T(8,128)(2,1)S(1)}, bf16[512,384]{1,0:T(8,128)(2,1)}, u32[]{:S(2)}) copy-start(bf16[512,384]{1,0:T(8,128)(2,1)} %constant.4.clone.squeeze_ref) | copy-start | bytes 1179652
  34.7 10.4 %copy-start = (bf16[384,512]{1,0:T(8,128)(2,1)S(1)}, bf16[384,512]{1,0:T(8,128)(2,1)}, u32[]{:S(2)}) copy-start(bf16[384,512]{1,0:T(8,128)(2,1)} %constant.5.clone.stretch_ref) | copy-start | bytes 1179652
  45.1 15.1 %copy-start.2 = (bf16[2,128,640]{2,1,0:T(8,128)(2,1)S(1)}, bf16[2,128,640]{2,1,0:T(8,128)(2,1)}, u32[]{:S(2)}) copy-start(bf16[2,128,640]{2,1,0:T(8,128)(2,1)} %weight_ref.1) | copy-start | bytes 983044
  45.8 14.4 %copy-start.4 = (bf16[2,128,128]{2,1,0:T(8,128)(2,1)S(1)}, bf16[2,128,128]{2,1,0:T(8,128)(2,1)}, u32[]{:S(2)}) copy-start(bf16[2,128,128]{2,1,0:T(8,128)(2,1)} %out_weight_ref.3) | copy-start | bytes 196612

commit v11 on v10

--- a/solution.py
+++ b/solution.py
@@ -130,12 +130,31 @@
     return by_device(rows).reshape(HALF, 3, 2, H).astype(BF16)
 
 
-def start_kernel(pair_ref, weight_ref, gain_ref, out_ref, gate_ref):
+def start_kernel(
+    pair_hbm, weight_hbm, in_gain_hbm, out_gain_hbm,
+    out_ref, gate_ref, gain_ref,
+    pair_ref, weight_ref, in_gain_ref, out_gain_ref, sems,
+):
+    moves = [
+        (pair_hbm, pair_ref),
+        (in_gain_hbm, in_gain_ref),
+        (weight_hbm.at[0], weight_ref),
+        (out_gain_hbm, out_gain_ref),
+    ]
+    copies = [pltpu.make_async_copy(source, target, sems.at[n]) for n, (source, target) in enumerate(moves)]
+    for copy in copies:
+        copy.start()
+    copies[0].wait()
+    copies[1].wait()
     field = pair_ref[...].reshape(288, H).astype(F32)
-    normed = normalize(field, gain_ref[0:1], 1).astype(BF16)
+    normed = normalize(field, in_gain_ref[0:1], 1).astype(BF16)
+    copies[2].wait()
     weight = weight_ref[...]
     out_ref[...] = spread_sides(normed, weight)
     gate_ref[...] = gate_of(normed, weight)
+    copies[3].wait()
+    gain_ref[0:2] = in_gain_ref[...]
+    gain_ref[2:4] = out_gain_ref[...]
 
 
 def pack_kernel(both_ref, squeeze_ref, left_ref, right_ref):
@@ -235,8 +254,22 @@
     sides, results = ((HALF, 5, 2, H), BF16), ((HALF, 3, 2, H), BF16)
     block, blocks = ((192, 384), BF16), ((4, 96, 384), BF16)
 
-    gains = jnp.concatenate([in_gain, out_gain], axis=0)
-    sent, gating = call(start_kernel, [sides, gates])(pair_field, proj_weight[0], gains)
+    held = [
+        pltpu.with_memory_space_constraint(array, pltpu.HBM)
+        for array in (pair_field, proj_weight, in_gain, out_gain)
+    ]
+    sent, gating, gains = call(
+        start_kernel,
+        [sides, gates, ((4, H), F32)],
+        [
+            pltpu.VMEM((6, 48, H), BF16),
+            pltpu.VMEM((H, 5 * H), BF16),
+            pltpu.VMEM((2, H), F32),
+            pltpu.VMEM((2, H), F32),
+            pltpu.SemaphoreType.DMA((4,)),
+        ],
+        in_specs=[pl.BlockSpec(memory_space=pltpu.HBM)] * 4,
+    )(*held)
     own = exchange(sent, SPREAD)
     both = lax.all_gather(own, "core", axis=0, tiled=False)
     left, right = call(pack_kernel, [block, blocks])(both, squeeze)

time: 108 us -> 108 us (level)
  no operation moved by 1% of the time
where the time goes in v11:
time: 108 us; the launch traced here: 107 us
  blocking collectives  101 us (94%)
  Pallas kernels  6.2 us (6%)
    all_to_all x2, blocking collectives, shards(): own = exchange(sent, SPREAD)  43.4 us
    all_to_all x2, blocking collectives, shards(): arrived = exchange(back, SPREAD)  28.6 us
    all_to_all x1, blocking collectives, shards(): right = exchange(right, 'x')  10.4 us
    all_gather x2, blocking collectives, shards(): both = lax.all_gather(own, 'core', axis=0, tiled=False)  9.72 us
    all_to_all x1, blocking collectives, shards(): parts = exchange(parts, 'x')  8.99 us

profile of v11, /device:TPU:1, one launch (start us, length us, event | category | flops | bytes accessed | tf_op | source)
XLA Modules:
  0.0 107.4 jit_solution(15252155743678663278)
XLA Ops:
  0.0 1.6 %shard_map.73 = (bf16[64,5,2,128]{3,2,1,0:T(2,128)(2,1)S(1)}, f32[288,128]{1,0:T(8,128)S(1)}, f32[4,128]{1,0:T(4,128)S(1)}) custom-call(bf16[6,48,128]{2,1,0:T(8,128)(2,1)} %field_ref.1, bf16[2,128,640]{2,1,0:T(8,128)(2,1)} %weight_ref.1, f32[2,128]{1,0:T(2,128)} %in_gain_hbm.1, f32[2,128]{1,0:T(2,128)} %out_gain_hbm.1), custom_call_target="tpu_custom_call" | custom-call | flops 20000000 | bytes 1000000 | tf_op jit(solution)/shard_map/pallas_call | solution.py:261
  1.6 0.0 copy-start.1
  1.6 28.2 %all_to_all.30 = bf16[64,5,2,128]{3,2,1,0:T(2,128)(2,1)S(1)} all-to-all(bf16[64,5,2,128]{3,2,1,0:T(2,128)(2,1)S(1)} %get-tuple-element.13), channel_id=1, replica_groups=mesh['yh'=2,'z2'=2,'z1'=2,'z0'=2,'x'=4,'yl'=4,'core'=2] {'yl','z1','yh',..., dimensions={0} | all-to-all | bytes 327680 | tf_op jit(solution)/shard_map/all_to_all | solution.py:273
  29.8 4.2 %all-gather = bf16[128,5,2,128]{3,2,1,0:T(2,128)(2,1)S(1)} all-gather(bf16[64,5,2,128]{3,2,1,0:T(2,128)(2,1)S(1)} %all_to_all.30), channel_id=2, replica_groups=mesh['yh'=2,'z2'=2,'z1'=2,'z0'=2,'x'=4,'yl'=4,'core'=2] {'core'}, dimensions={0}, use_global_device_ids=true | all-gather | bytes 491520 | tf_op jit(solution)/shard_map/all_gather | solution.py:274
  34.0 0.0 copy-done.1
  34.0 0.6 shard_map.74
  34.6 0.0 copy-start
  34.6 10.4 %all_to_all.31.right_ref = bf16[4,96,384]{2,1,0:T(8,128)(2,1)S(1)} all-to-all(bf16[4,96,384]{2,1,0:T(8,128)(2,1)S(1)} %get-tuple-element.15), channel_id=1, replica_groups=mesh['yh'=2,'z2'=2,'z1'=2,'z0'=2,'x'=4,'yl'=4,'core'=2] {'x'}, dimensions={0} | all-to-all | bytes 589824 | tf_op jit(solution)/shard_map/all_to_all | solution.py:276
  45.0 0.0 copy-done
  45.0 0.0 copy-start.2
  45.0 0.7 shard_map.75
  45.7 0.0 copy-start.3
  45.8 0.0 copy-start.4
  45.8 14.4 %all_to_all.32.arrived_ref = bf16[64,3,2,128]{3,2,1,0:T(2,128)(2,1)S(1)} all-to-all(bf16[64,3,2,128]{3,2,1,0:T(2,128)(2,1)S(1)} %shard_map.75), channel_id=1, replica_groups=mesh['yh'=2,'z2'=2,'z1'=2,'z0'=2,'x'=4,'yl'=4,'core'=2] {'yl','z1','yh',..., dimensions={0} | all-to-all | bytes 196608 | tf_op jit(solution)/shard_map/all_to_all | solution.py:278
  60.2 0.0 copy-done.2
  60.2 0.0 copy-done.3
  60.2 0.0 copy-done.4
  60.2 1.1 %shard_map.76 = (bf16[64,5,2,128]{3,2,1,0:T(2,128)(2,1)S(1)}, bf16[6,48,128]{2,1,0:T(8,128)(2,1)S(1)}, f32[288,128]{1,0:T(8,128)S(1)}) custom-call(bf16[64,3,2,128]{3,2,1,0:T(2,128)(2,1)S(1)} %all_to_all.32.arrived_ref, bf16[6,48,128]{2,1,0:T(8,128)(2,1)S(1)} %copy-done.3, f32[288,128]{1,0:T(8,128)S(1)} %get-tuple-element.16.gate_ref, ...), custom_call_target="tpu_custom_call" | custom-call | flops 20000000 | bytes 1000000 | tf_op jit(solution)/shard_map/pallas_call | solution.py:280
  61.2 15.2 %all_to_all.33.own_ref = bf16[64,5,2,128]{3,2,1,0:T(2,128)(2,1)S(1)} all-to-all(bf16[64,5,2,128]{3,2,1,0:T(2,128)(2,1)S(1)} %get-tuple-element.18), channel_id=1, replica_groups=mesh['yh'=2,'z2'=2,'z1'=2,'z0'=2,'x'=4,'yl'=4,'core'=2] {'yl','z1','yh',..., dimensions={0} | all-to-all | bytes 327680 | tf_op jit(solution)/shard_map/all_to_all | solution.py:283
  76.4 5.5 %all-gather.1 = bf16[128,5,2,128]{3,2,1,0:T(2,128)(2,1)S(1)} all-gather(bf16[64,5,2,128]{3,2,1,0:T(2,128)(2,1)S(1)} %all_to_all.33.own_ref), channel_id=3, replica_groups=mesh['yh'=2,'z2'=2,'z1'=2,'z0'=2,'x'=4,'yl'=4,'core'=2] {'core'}, dimensions={0}, use_global_device_ids=true | all-gather | bytes 491520 | tf_op jit(solution)/shard_map/all_gather | solution.py:284
  81.9 0.8 shard_map.77
  82.7 9.0 %all_to_all.34.parts_ref = bf16[4,96,384]{2,1,0:T(8,128)(2,1)S(1)} all-to-all(bf16[4,96,384]{2,1,0:T(8,128)(2,1)S(1)} %shard_map.77), channel_id=1, replica_groups=mesh['yh'=2,'z2'=2,'z1'=2,'z0'=2,'x'=4,'yl'=4,'core'=2] {'x'}, dimensions={0} | all-to-all | bytes 589824 | tf_op jit(solution)/shard_map/all_to_all | solution.py:286
  91.7 0.4 shard_map.78
  92.1 14.3 %all_to_all.35.arrived_ref = bf16[64,3,2,128]{3,2,1,0:T(2,128)(2,1)S(1)} all-to-all(bf16[64,3,2,128]{3,2,1,0:T(2,128)(2,1)S(1)} %shard_map.78), channel_id=1, replica_groups=mesh['yh'=2,'z2'=2,'z1'=2,'z0'=2,'x'=4,'yl'=4,'core'=2] {'yl','z1','yh',..., dimensions={0} | all-to-all | bytes 196608 | tf_op jit(solution)/shard_map/all_to_all | solution.py:288
  106.4 1.0 shard_map.79
Async XLA Ops:
  1.6 32.4 %copy-start.1 = (bf16[512,384]{1,0:T(8,128)(2,1)S(1)}, bf16[512,384]{1,0:T(8,128)(2,1)}, u32[]{:S(2)}) copy-start(bf16[512,384]{1,0:T(8,128)(2,1)} %constant.4.clone.squeeze_ref) | copy-start | bytes 1179652
  34.6 10.4 %copy-start = (bf16[384,512]{1,0:T(8,128)(2,1)S(1)}, bf16[384,512]{1,0:T(8,128)(2,1)}, u32[]{:S(2)}) copy-start(bf16[384,512]{1,0:T(8,128)(2,1)} %constant.5.clone.stretch_ref) | copy-start | bytes 1179652
  45.0 15.1 %copy-start.2 = (bf16[2,128,640]{2,1,0:T(8,128)(2,1)S(1)}, bf16[2,128,640]{2,1,0:T(8,128)(2,1)}, u32[]{:S(2)}) copy-start(bf16[2,128,640]{2,1,0:T(8,128)(2,1)} %weight_ref.1) | copy-start | bytes 983044
  45.7 14.4 %copy-start.3 = (bf16[6,48,128]{2,1,0:T(8,128)(2,1)S(1)}, bf16[6,48,128]{2,1,0:T(8,128)(2,1)}, u32[]{:S(2)}) copy-start(bf16[6,48,128]{2,1,0:T(8,128)(2,1)} %field_ref.1) | copy-start | bytes 221188
  45.8 14.4 %copy-start.4 = (bf16[2,128,128]{2,1,0:T(8,128)(2,1)S(1)}, bf16[2,128,128]{2,1,0:T(8,128)(2,1)}, u32[]{:S(2)}) copy-start(bf16[2,128,128]{2,1,0:T(8,128)(2,1)} %out_weight_ref.3) | copy-start | bytes 196612

commit v12 on v10

v12 whole, which is shorter than its diff:
```python
import functools

import jax
import jax.numpy as jnp
import numpy as np
from jax import lax
from jax.experimental import pallas as pl
from jax.experimental.pallas import tpu as pltpu
from jax.sharding import Mesh
from jax.sharding import PartitionSpec as P

H = 128
HALF = 64
SPREAD = ("yl", "z1", "yh", "z2", "z0")
F32 = jnp.float32
BF16 = jnp.bfloat16


def normalize(values, gain, axis):
    mean = jnp.mean(values, axis=axis, keepdims=True)
    centred = values - mean
    spread = jnp.mean(centred * centred, axis=axis, keepdims=True)
    return centred * lax.rsqrt(spread + 1e-05) * gain


def halves(top, bottom):
    low = lax.broadcasted_iota(jnp.int32, top.shape, 1) < HALF
    return jnp.where(low, top, pltpu.roll(bottom, HALF, 1)), jnp.where(low, pltpu.roll(top, HALF, 1), bottom)


def by_device(rows):
    return jnp.swapaxes(jnp.stack(rows, axis=0), 0, 1)


def spread_sides(normed, weight):
    rows = []
    for core in range(2):
        projected = lax.dot_general(
            weight[:, : 4 * H],
            normed[288 * core : 288 * core + 288],
            (((0,), (1,)), ((), ())),
            preferred_element_type=F32,
        )
        ends = []
        for side in range(2):
            value = projected[2 * side * H : (2 * side + 1) * H]
            gate = projected[(2 * side + 1) * H : (2 * side + 2) * H]
            turned = jax.nn.sigmoid(gate) * value
            for channel in range(2):
                part = turned[channel * HALF : (channel + 1) * HALF]
                rows.extend([part[:, :H], part[:, H : 2 * H]])
                ends.append(part[:, 2 * H :])
        rows.append(jnp.concatenate(ends, axis=1))
    return by_device(rows).reshape(HALF, 9, 2, H).astype(BF16)


def gate_of(normed, weight):
    return jax.nn.sigmoid(jnp.dot(normed, weight[:, 4 * H :], preferred_element_type=F32))


def summed_rows(arrived):
    by_row = jnp.swapaxes(arrived.astype(F32).reshape(HALF, 12, H), 0, 1)
    return jnp.concatenate(
        [jnp.concatenate([by_row[6 * core + t], by_row[6 * core + 3 + t]], axis=0) for core in range(2) for t in range(3)],
        axis=1,
    )


def finish(summed, field, gating, weight, gain):
    column = jnp.swapaxes(jnp.broadcast_to(gain, (8, H)), 0, 1)[:, :1]
    mixed = normalize(summed, column, 0).astype(BF16)
    update = lax.dot_general(
        mixed, weight, (((0,), (0,)), ((), ())), preferred_element_type=F32
    )
    update = jnp.concatenate([update[HALF * a : HALF * a + 48] for a in range(12)], axis=0)
    return field.astype(F32) + gating * update


def rows_of(own):
    by_row = jnp.swapaxes(own.astype(F32).reshape(HALF, 18, H), 0, 1)
    return by_row[:9], by_row[9:]


def moved(tile, lanes):
    return pltpu.roll(tile, lanes % H, 1) if lanes % H else tile


def matrix(by_row, side, channel):
    q = 2 * side + channel
    lane = lax.broadcasted_iota(jnp.int32, (16, H), 1)
    cut = lax.broadcasted_iota(jnp.int32, (HALF, H), 1) >= 96
    first, second, last = by_row[2 * q], by_row[2 * q + 1], by_row[8]
    across = jnp.where(cut, first, second)
    begins = ((first, 0), (first, 48), (across, 96), (second, 16), (second, 64), (second, 112))
    found = ([], [])
    for a in range(6):
        row, begin = begins[a]
        tiles = []
        for u in range(2):
            pair = []
            for e in range(2):
                at = slice(32 * u + 16 * e, 32 * u + 16 * e + 16)
                piece = moved(row[at], HALF * e - begin)
                if a == 5:
                    piece = jnp.where(lane < HALF * e + 16, piece, moved(last[at], HALF * e + 16 - 32 * q))
                pair.append(piece)
            tiles.append(jnp.where(lane < HALF, *pair))
        both = jnp.concatenate(tiles, axis=1)
        for half in range(2):
            found[half].append(both[8 * half : 8 * half + 8])
    return [jnp.concatenate(pieces, axis=0) for pieces in found]


def whole_matrix(cores, side, channel):
    parts = [matrix(by_row, side, channel) for by_row in cores]
    return [jnp.concatenate([parts[0][z1], parts[1][z1]], axis=1) for z1 in range(2)]


def squeezed(rows, squeeze):
    return jnp.dot(
        jnp.concatenate(rows, axis=0).astype(BF16), squeeze, preferred_element_type=F32
    ).astype(BF16)


def send_back(products, stretch):
    wide = jnp.dot(products.astype(BF16), stretch, preferred_element_type=F32)
    rows = []
    for core in range(2):
        for channel in range(2):
            for t in range(3):
                parts = []
                for u in range(2):
                    lanes = slice((2 * core + u) * H, (2 * core + u + 1) * H)
                    pair = [
                        jnp.concatenate([wide[at : at + 8, lanes], wide[at + 48 : at + 56, lanes]], axis=0)
                        for at in (96 * channel + 16 * t, 96 * channel + 16 * t + 8)
                    ]
                    parts.extend(halves(*pair))
                rows.append(jnp.concatenate(parts, axis=0))
    return by_device(rows).reshape(HALF, 3, 4, H).astype(BF16)


def all_rows(own, squeeze):
    cores = rows_of(own)
    rows = []
    for side in range(2):
        for channel in range(2):
            rows.extend(whole_matrix(cores, side, channel))
    return squeezed(rows, squeeze)


def start_kernel(pair_ref, weight_ref, gain_ref, out_ref, gate_ref):
    field = pair_ref[...].reshape(576, H).astype(F32)
    normed = normalize(field, gain_ref[0:1], 1).astype(BF16)
    weight = weight_ref[0]
    out_ref[...] = spread_sides(normed, weight)
    gate_ref[...] = gate_of(normed, weight)


def pack_kernel(own_ref, squeeze_ref, left_ref, right_ref):
    packed = all_rows(own_ref[...], squeeze_ref[...])
    left_ref[...] = packed[:192]
    for x in range(4):
        right_ref[x] = packed[192:]


def outgoing_kernel(left_ref, right_ref, stretch_ref, out_ref):
    products = []
    for channel in range(2):
        right = jnp.concatenate(
            [right_ref[x, 96 * channel + 48 * z1 : 96 * channel + 48 * z1 + 48] for z1 in range(2) for x in range(4)], axis=0
        )
        products.append(
            lax.dot_general(
                left_ref[96 * channel : 96 * channel + 96], right, (((1,), (1,)), ((), ())), preferred_element_type=F32
            )
        )
    out_ref[...] = send_back(jnp.concatenate(products, axis=0), stretch_ref[...])


def middle_kernel(
    arrived_ref, field_ref, gate_ref, out_weight_ref, weight_ref, gain_ref, out_ref, first_ref, next_gate_ref
):
    first = finish(
        summed_rows(arrived_ref[...]), field_ref[...].reshape(576, H), gate_ref[...], out_weight_ref[0], gain_ref[2:3]
    ).astype(BF16)
    normed = normalize(first.astype(F32), gain_ref[1:2], 1).astype(BF16)
    weight = weight_ref[1]
    out_ref[...] = spread_sides(normed, weight)
    first_ref[...] = first
    next_gate_ref[...] = gate_of(normed, weight)


def incoming_kernel(own_ref, squeeze_ref, out_ref):
    packed = all_rows(own_ref[...], squeeze_ref[...])
    for channel in range(2):
        product = lax.dot_general(
            packed[96 * channel : 96 * channel + 96],
            packed[192 + 96 * channel : 288 + 96 * channel],
            (((0,), (0,)), ((), ())),
            preferred_element_type=F32,
        ).astype(BF16)
        for x in range(4):
            for z1 in range(2):
                at, to = 192 * z1 + 48 * x, 96 * channel + 48 * z1
                out_ref[x, to : to + 48] = product[at : at + 48]


def sum_kernel(parts_ref, stretch_ref, out_ref):
    total = parts_ref[0].astype(F32)
    for x in range(1, 4):
        total = total + parts_ref[x].astype(F32)
    out_ref[...] = send_back(total, stretch_ref[...])


def end_kernel(arrived_ref, field_ref, gate_ref, out_weight_ref, gain_ref, other_ref, own_ref):
    final = finish(
        summed_rows(arrived_ref[...]), field_ref[...], gate_ref[...], out_weight_ref[1], gain_ref[3:4]
    ).astype(BF16)
    other_ref[...] = final[:288].reshape(6, 48, H)
    own_ref[...] = final[288:].reshape(6, 48, H)


def squeeze_matrix():
    places = np.pad(np.ones((4, 48), bool), ((0, 0), (0, 16))).reshape(-1).nonzero()[0]
    places = places.reshape(2, 2, 2, 4, 6).transpose(3, 4, 0, 1, 2).reshape(-1)
    block = np.arange(256)[:, None] == places[None, :]
    return np.kron(np.eye(2, dtype=bool), block).astype(jnp.bfloat16)


def call(kernel, outs, scratch=(), **specs):
    return pl.pallas_call(
        kernel,
        out_shape=[jax.ShapeDtypeStruct(shape, dtype) for shape, dtype in outs],
        scratch_shapes=list(scratch),
        compiler_params=pltpu.CompilerParams(vmem_limit_bytes=48 * 1024 * 1024),
        cost_estimate=pl.CostEstimate(flops=20_000_000, bytes_accessed=1_000_000, transcendentals=100_000),
        **specs,
    )


def shards(pair_field, proj_weight, out_weight, in_gain, out_gain):
    leads = lax.axis_index("core") == 1

    def exchange(array, axes):
        swap = functools.partial(lax.all_to_all, axis_name=axes, split_axis=0, concat_axis=0, tiled=True)
        return lax.cond(leads, swap, lambda same: same, array)

    squeeze, stretch = jnp.asarray(squeeze_matrix()), jnp.asarray(squeeze_matrix().T)
    gates, pairs = ((576, H), F32), ((576, H), BF16)
    sides, results = ((HALF, 9, 2, H), BF16), ((HALF, 3, 4, H), BF16)
    block, blocks = ((192, 384), BF16), ((4, 192, 384), BF16)

    gains = jnp.concatenate([in_gain, out_gain], axis=0)
    field = lax.all_gather(pair_field, "core", axis=0, tiled=False)
    sent, gating = call(start_kernel, [sides, gates])(field, proj_weight, gains)
    own = exchange(sent, SPREAD)
    left, right = call(pack_kernel, [block, blocks])(own, squeeze)
    right = exchange(right, "x")
    [back] = call(outgoing_kernel, [results])(left, right, stretch)
    arrived = exchange(back, SPREAD)

    sent, first_pair, gating = call(middle_kernel, [sides, pairs, gates])(
        arrived, field, gating, out_weight, proj_weight, gains
    )
    own = exchange(sent, SPREAD)
    [parts] = call(incoming_kernel, [blocks])(own, squeeze)
    parts = exchange(parts, "x")
    [back] = call(sum_kernel, [results])(parts, stretch)
    arrived = exchange(back, SPREAD)
    one = ((6, 48, H), BF16)
    other, mine = call(end_kernel, [one, one])(arrived, first_pair, gating, out_weight, gains)
    return jnp.where(leads, mine, lax.all_gather(other, "core", axis=0, tiled=False)[1])


def solution(mesh):
    fine = Mesh(mesh.devices.reshape(2, 2, 2, 2, 4, 4, 2), ("yh", "z2", "z1", "z0", "x", "yl", "core"))
    row, col = ("yh", "z2", "z1", "z0", "x"), ("yl", "core")
    return jax.shard_map(
        shards,
        mesh=fine,
        in_specs=(P(row, col, None), P(), P(), P(), P()),
        out_specs=P(row, col, None),
        check_vma=False,
    )
```

time: 108 us -> 111 us (1.028)
  local copies, waits for them, and re-layouts: 1.01 us -> 2.36 us
    unnamed x14, local copies, waits for them, and re-layouts: 0.03 us -> 1.69 us
where the time goes in v12:
time: 111 us
  blocking collectives  102 us (92%)
  Pallas kernels  5.57 us (5%)
  local copies, waits for them, and re-layouts  2.36 us (2%)
    all_to_all x6, blocking collectives, exchange(): return lax.cond(leads, swap, lambda same: same, array)  91.3 us
    all_gather x1, blocking collectives, shards(): field = lax.all_gather(pair_field, 'core', axis=0, tiled=False)  8.64 us

profile of v12, /device:TPU:1, one launch (start us, length us, event | category | flops | bytes accessed | tf_op | source)
XLA Modules:
  0.0 110.7 jit_solution(14134000132734480101)
XLA Ops:
  0.0 0.0 copy-start.6
  0.0 0.0 copy-start.5
  0.0 0.7 copy-done.6
  0.7 0.0 copy-done.5
  0.7 8.6 %all-gather = bf16[12,48,128]{2,1,0:T(8,128)(2,1)S(1)} all-gather(bf16[6,48,128]{2,1,0:T(8,128)(2,1)} %param.19), channel_id=2, replica_groups=mesh['yh'=2,'z2'=2,'z1'=2,'z0'=2,'x'=4,'yl'=4,'core'=2] {'core'}, dimensions={0}, use_global_device_ids=true | all-gather | bytes 221184 | tf_op jit(solution)/shard_map/all_gather | solution.py:255
  9.3 0.0 copy-start.2
  9.3 1.0 copy-done.2
  10.3 1.0 shard_map.73
  11.3 0.0 copy-start
  11.3 23.6 %conditional.6 = (bf16[64,9,2,128]{3,2,1,0:T(2,128)(2,1)S(1)}) conditional(s32[]{:T(128)} %convert_element_type.2, bf16[64,9,2,128]{3,2,1,0:T(2,128)(2,1)S(1)} %get-tuple-element.44, bf16[64,9,2,128]{3,2,1,0:T(2,128)(2,1)S(1)} %get-tuple-element.44), branch_computations={%region_0.0_spmd, %region_1.0_spmd} | conditional | bytes 1179656 | solution.py:247
  11.4 0.2 copy.20
  11.6 23.3 %all_to_all.24 = bf16[64,9,2,128]{3,2,1,0:T(2,128)(2,1)S(1)} all-to-all(bf16[64,9,2,128]{3,2,1,0:T(2,128)(2,1)S(1)} %copy.20), channel_id=1, replica_groups=mesh['yh'=2,'z2'=2,'z1'=2,'z0'=2,'x'=4,'yl'=4,'core'=2] {'yl','z1','yh',..., dimensions={0} | all-to-all | bytes 589824 | tf_op jit(solution)/shard_map/cond/branch_1_fun/all_to_all | solution.py:247
  34.9 0.0 copy-done
  34.9 0.6 shard_map.74
  35.6 0.0 copy-start.1
  35.6 11.3 %conditional.7 = (bf16[4,192,384]{2,1,0:T(8,128)(2,1)S(1)}) conditional(s32[]{:T(128)} %convert_element_type.2, bf16[4,192,384]{2,1,0:T(8,128)(2,1)S(1)} %get-tuple-element.46, bf16[4,192,384]{2,1,0:T(8,128)(2,1)S(1)} %get-tuple-element.46), branch_computations={%region_2.0_spmd, %region_3.0_spmd} | conditional | bytes 2359304 | solution.py:247
  35.6 0.1 copy.21
  35.7 11.2 %all_to_all.25 = bf16[4,192,384]{2,1,0:T(8,128)(2,1)S(1)} all-to-all(bf16[4,192,384]{2,1,0:T(8,128)(2,1)S(1)} %copy.21), channel_id=1, replica_groups=mesh['yh'=2,'z2'=2,'z1'=2,'z0'=2,'x'=4,'yl'=4,'core'=2] {'x'}, dimensions={0} | all-to-all | bytes 1179648 | tf_op jit(solution)/shard_map/cond/branch_1_fun/all_to_all | solution.py:247
  46.9 0.0 copy-done.1
  46.9 0.7 shard_map.75
  47.6 0.0 copy-start.3
  47.6 0.0 copy-start.4
  47.6 15.5 %conditional.8 = (bf16[64,3,4,128]{3,2,1,0:T(4,128)(2,1)S(1)}) conditional(s32[]{:T(128)} %convert_element_type.2, bf16[64,3,4,128]{3,2,1,0:T(4,128)(2,1)S(1)} %shard_map.75, bf16[64,3,4,128]{3,2,1,0:T(4,128)(2,1)S(1)} %shard_map.75), branch_computations={%region_4.0_spmd, %region_5.0_spmd} | conditional | bytes 786440 | solution.py:247
  47.6 0.1 copy.22
  47.7 15.4 %all_to_all.26 = bf16[64,3,4,128]{3,2,1,0:T(4,128)(2,1)S(1)} all-to-all(bf16[64,3,4,128]{3,2,1,0:T(4,128)(2,1)S(1)} %copy.22), channel_id=1, replica_groups=mesh['yh'=2,'z2'=2,'z1'=2,'z0'=2,'x'=4,'yl'=4,'core'=2] {'yl','z1','yh',..., dimensions={0} | all-to-all | bytes 393216 | tf_op jit(solution)/shard_map/cond/branch_1_fun/all_to_all | solution.py:247
  63.1 0.0 copy-done.3
  63.1 0.0 copy-done.4
  63.1 1.4 %shard_map.76 = (bf16[64,9,2,128]{3,2,1,0:T(2,128)(2,1)S(1)}, bf16[576,128]{1,0:T(8,128)(2,1)S(1)}, f32[576,128]{1,0:T(8,128)S(1)}) custom-call(bf16[64,3,4,128]{3,2,1,0:T(4,128)(2,1)S(1)} %get-tuple-element.55.arrived_ref, bf16[2,6,48,128]{3,2,1,0:T(8,128)(2,1)S(1)} %bitcast.2, f32[576,128]{1,0:T(8,128)S(1)} %get-tuple-element.47.gate_ref, ...), custom_call_target="tpu_custom_call" | custom-call | flops 20000000 | bytes 1000000 | tf_op jit(solution)/shard_map/pallas_call | solution.py:263
  64.5 16.5 %conditional.9 = (bf16[64,9,2,128]{3,2,1,0:T(2,128)(2,1)S(1)}) conditional(s32[]{:T(128)} %convert_element_type.2, bf16[64,9,2,128]{3,2,1,0:T(2,128)(2,1)S(1)} %get-tuple-element.48, bf16[64,9,2,128]{3,2,1,0:T(2,128)(2,1)S(1)} %get-tuple-element.48), branch_computations={%region_6.0_spmd, %region_7.0_spmd} | conditional | bytes 1179656 | solution.py:247
  64.5 0.2 copy.23
  64.7 16.3 %all_to_all.27 = bf16[64,9,2,128]{3,2,1,0:T(2,128)(2,1)S(1)} all-to-all(bf16[64,9,2,128]{3,2,1,0:T(2,128)(2,1)S(1)} %copy.23), channel_id=1, replica_groups=mesh['yh'=2,'z2'=2,'z1'=2,'z0'=2,'x'=4,'yl'=4,'core'=2] {'yl','z1','yh',..., dimensions={0} | all-to-all | bytes 589824 | tf_op jit(solution)/shard_map/cond/branch_1_fun/all_to_all | solution.py:247
  81.0 0.9 shard_map.77
  81.9 9.8 %conditional.10 = (bf16[4,192,384]{2,1,0:T(8,128)(2,1)S(1)}) conditional(s32[]{:T(128)} %convert_element_type.2, bf16[4,192,384]{2,1,0:T(8,128)(2,1)S(1)} %shard_map.77, bf16[4,192,384]{2,1,0:T(8,128)(2,1)S(1)} %shard_map.77), branch_computations={%region_8.0_spmd, %region_9.0_spmd} | conditional | bytes 2359304 | solution.py:247
  81.9 0.1 copy.24
  82.0 9.7 %all_to_all.28 = bf16[4,192,384]{2,1,0:T(8,128)(2,1)S(1)} all-to-all(bf16[4,192,384]{2,1,0:T(8,128)(2,1)S(1)} %copy.24), channel_id=1, replica_groups=mesh['yh'=2,'z2'=2,'z1'=2,'z0'=2,'x'=4,'yl'=4,'core'=2] {'x'}, dimensions={0} | all-to-all | bytes 1179648 | tf_op jit(solution)/shard_map/cond/branch_1_fun/all_to_all | solution.py:247
  91.7 0.5 shard_map.78
  92.2 15.5 %conditional.11 = (bf16[64,3,4,128]{3,2,1,0:T(4,128)(2,1)S(1)}) conditional(s32[]{:T(128)} %convert_element_type.2, bf16[64,3,4,128]{3,2,1,0:T(4,128)(2,1)S(1)} %shard_map.78, bf16[64,3,4,128]{3,2,1,0:T(4,128)(2,1)S(1)} %shard_map.78), branch_computations={%region_10.0_spmd, %region_11.0_spmd} | conditional | bytes 786440 | solution.py:247
  92.2 0.1 copy.25
  92.3 15.4 %all_to_all.29 = bf16[64,3,4,128]{3,2,1,0:T(4,128)(2,1)S(1)} all-to-all(bf16[64,3,4,128]{3,2,1,0:T(4,128)(2,1)S(1)} %copy.25), channel_id=1, replica_groups=mesh['yh'=2,'z2'=2,'z1'=2,'z0'=2,'x'=4,'yl'=4,'core'=2] {'yl','z1','yh',..., dimensions={0} | all-to-all | bytes 393216 | tf_op jit(solution)/shard_map/cond/branch_1_fun/all_to_all | solution.py:247
  107.6 0.5 shard_map.79
  108.1 1.9 %all-gather.1 = bf16[12,48,128]{2,1,0:T(8,128)(2,1)S(1)} all-gather(bf16[6,48,128]{2,1,0:T(8,128)(2,1)S(1)} %get-tuple-element.52), channel_id=3, replica_groups=mesh['yh'=2,'z2'=2,'z1'=2,'z0'=2,'x'=4,'yl'=4,'core'=2] {'core'}, dimensions={0}, use_global_device_ids=true | all-gather | bytes 221184 | tf_op jit(solution)/shard_map/all_gather | solution.py:273
  110.0 0.6 slice_select_fusion
  (1 shorter events, 0.0 us)
Async XLA Ops:
  0.0 0.7 copy-start.6
  0.0 0.7 copy-start.5
  9.3 1.0 copy-start.2
  11.3 23.6 %copy-start = (bf16[512,384]{1,0:T(8,128)(2,1)S(1)}, bf16[512,384]{1,0:T(8,128)(2,1)}, u32[]{:S(2)}) copy-start(bf16[512,384]{1,0:T(8,128)(2,1)} %constant.10.clone.squeeze_ref) | copy-start | bytes 1179652
  35.6 11.3 %copy-start.1 = (bf16[384,512]{1,0:T(8,128)(2,1)S(1)}, bf16[384,512]{1,0:T(8,128)(2,1)}, u32[]{:S(2)}) copy-start(bf16[384,512]{1,0:T(8,128)(2,1)} %constant.11.clone.stretch_ref) | copy-start | bytes 1179652
  47.6 15.5 %copy-start.3 = (bf16[2,128,640]{2,1,0:T(8,128)(2,1)S(1)}, bf16[2,128,640]{2,1,0:T(8,128)(2,1)}, u32[]{:S(2)}) copy-start(bf16[2,128,640]{2,1,0:T(8,128)(2,1)} %weight_ref.3) | copy-start | bytes 983044
  47.6 15.5 %copy-start.4 = (bf16[2,128,128]{2,1,0:T(8,128)(2,1)S(1)}, bf16[2,128,128]{2,1,0:T(8,128)(2,1)}, u32[]{:S(2)}) copy-start(bf16[2,128,128]{2,1,0:T(8,128)(2,1)} %out_weight_ref.3) | copy-start | bytes 196612

commit v13 on v12

--- a/solution.py
+++ b/solution.py
@@ -149,12 +149,26 @@
     return squeezed(rows, squeeze)
 
 
-def start_kernel(pair_ref, weight_ref, gain_ref, out_ref, gate_ref):
+def start_kernel(
+    pair_ref, weight_hbm, in_gain_hbm, out_gain_hbm,
+    out_ref, gate_ref, gain_ref,
+    weight_ref, in_gain_ref, out_gain_ref, sems,
+):
+    moves = [(in_gain_hbm, in_gain_ref), (weight_hbm.at[0], weight_ref), (out_gain_hbm, out_gain_ref)]
+    copies = [pltpu.make_async_copy(source, target, sems.at[n]) for n, (source, target) in enumerate(moves)]
+    for copy in copies:
+        copy.start()
     field = pair_ref[...].reshape(576, H).astype(F32)
-    normed = normalize(field, gain_ref[0:1], 1).astype(BF16)
-    weight = weight_ref[0]
+    centred = normalize(field, 1.0, 1)
+    copies[0].wait()
+    normed = (centred * in_gain_ref[0:1]).astype(BF16)
+    copies[1].wait()
+    weight = weight_ref[...]
     out_ref[...] = spread_sides(normed, weight)
     gate_ref[...] = gate_of(normed, weight)
+    copies[2].wait()
+    gain_ref[0:2] = in_gain_ref[...]
+    gain_ref[2:4] = out_gain_ref[...]
 
 
 def pack_kernel(own_ref, squeeze_ref, left_ref, right_ref):
@@ -244,16 +258,26 @@
 
     def exchange(array, axes):
         swap = functools.partial(lax.all_to_all, axis_name=axes, split_axis=0, concat_axis=0, tiled=True)
-        return lax.cond(leads, swap, lambda same: same, array)
+        return lax.cond(leads, swap, jnp.zeros_like, array)
 
     squeeze, stretch = jnp.asarray(squeeze_matrix()), jnp.asarray(squeeze_matrix().T)
     gates, pairs = ((576, H), F32), ((576, H), BF16)
     sides, results = ((HALF, 9, 2, H), BF16), ((HALF, 3, 4, H), BF16)
     block, blocks = ((192, 384), BF16), ((4, 192, 384), BF16)
 
-    gains = jnp.concatenate([in_gain, out_gain], axis=0)
+    held = [pltpu.with_memory_space_constraint(array, pltpu.HBM) for array in (proj_weight, in_gain, out_gain)]
     field = lax.all_gather(pair_field, "core", axis=0, tiled=False)
-    sent, gating = call(start_kernel, [sides, gates])(field, proj_weight, gains)
+    sent, gating, gains = call(
+        start_kernel,
+        [sides, gates, ((4, H), F32)],
+        [
+            pltpu.VMEM((H, 5 * H), BF16),
+            pltpu.VMEM((2, H), F32),
+            pltpu.VMEM((2, H), F32),
+            pltpu.SemaphoreType.DMA((3,)),
+        ],
+        in_specs=[pl.BlockSpec(memory_space=pltpu.VMEM)] + [pl.BlockSpec(memory_space=pltpu.HBM)] * 3,
+    )(field, *held)
     own = exchange(sent, SPREAD)
     left, right = call(pack_kernel, [block, blocks])(own, squeeze)
     right = exchange(right, "x")

time: 111 us -> 110 us (level)
  local copies, waits for them, and re-layouts: 2.36 us -> 0.03 us
    unnamed x14 -> x8, local copies, waits for them, and re-layouts: 1.69 us -> 0.03 us
where the time goes in v13:
time: 110 us; the launch traced here: 109 us
  blocking collectives  102 us (93%)
  Pallas kernels  6.3 us (6%)
    all_to_all x6, blocking collectives, exchange(): return lax.cond(leads, swap, jnp.zeros_like, array)  91.4 us
    all_gather x1, blocking collectives, shards(): field = lax.all_gather(pair_field, 'core', axis=0, tiled=False)  8.64 us

profile of v13, /device:TPU:1, one launch (start us, length us, event | category | flops | bytes accessed | tf_op | source)
XLA Modules:
  0.0 109.2 jit_solution(15464858657365398094)
XLA Ops:
  0.0 8.6 %all-gather = bf16[12,48,128]{2,1,0:T(8,128)(2,1)S(1)} all-gather(bf16[6,48,128]{2,1,0:T(8,128)(2,1)} %param.19), channel_id=2, replica_groups=mesh['yh'=2,'z2'=2,'z1'=2,'z0'=2,'x'=4,'yl'=4,'core'=2] {'core'}, dimensions={0}, use_global_device_ids=true | all-gather | bytes 221184 | tf_op jit(solution)/shard_map/all_gather | solution.py:269
  8.6 1.8 %shard_map.73 = (bf16[64,9,2,128]{3,2,1,0:T(2,128)(2,1)S(1)}, f32[576,128]{1,0:T(8,128)S(1)}, f32[4,128]{1,0:T(4,128)S(1)}) custom-call(bf16[2,6,48,128]{3,2,1,0:T(8,128)(2,1)S(1)} %bitcast.1, bf16[2,128,640]{2,1,0:T(8,128)(2,1)} %weight_ref.1, f32[2,128]{1,0:T(2,128)} %in_gain_hbm.1, f32[2,128]{1,0:T(2,128)} %out_gain_hbm.1), custom_call_target="tpu_custom_call" | custom-call | flops 20000000 | bytes 1000000 | tf_op jit(solution)/shard_map/pallas_call | solution.py:270
  10.4 0.0 copy-start
  10.4 23.5 %conditional.6 = (bf16[64,9,2,128]{3,2,1,0:T(2,128)(2,1)S(1)}) conditional(s32[]{:T(128)} %convert_element_type.2, () %tuple.45, bf16[64,9,2,128]{3,2,1,0:T(2,128)(2,1)S(1)} %get-tuple-element.39), branch_computations={%region_0.0_spmd, %region_1.0_spmd} | conditional | bytes 589832 | solution.py:261
  10.4 23.5 %all_to_all.24 = bf16[64,9,2,128]{3,2,1,0:T(2,128)(2,1)S(1)} all-to-all(bf16[64,9,2,128]{3,2,1,0:T(2,128)(2,1)S(1)} %param.1), channel_id=1, replica_groups=mesh['yh'=2,'z2'=2,'z1'=2,'z0'=2,'x'=4,'yl'=4,'core'=2] {'yl','z1','yh',..., dimensions={0} | all-to-all | bytes 589824 | tf_op jit(solution)/shard_map/cond/branch_1_fun/all_to_all | solution.py:261
  33.9 0.0 copy-done
  33.9 0.6 shard_map.74
  34.5 0.0 copy-start.1
  34.6 11.3 %conditional.7 = (bf16[4,192,384]{2,1,0:T(8,128)(2,1)S(1)}) conditional(s32[]{:T(128)} %convert_element_type.2, () %tuple.46, bf16[4,192,384]{2,1,0:T(8,128)(2,1)S(1)} %get-tuple-element.41), branch_computations={%region_2.0_spmd, %region_3.0_spmd} | conditional | bytes 1179656 | solution.py:261
  34.6 11.2 %all_to_all.25 = bf16[4,192,384]{2,1,0:T(8,128)(2,1)S(1)} all-to-all(bf16[4,192,384]{2,1,0:T(8,128)(2,1)S(1)} %param.3), channel_id=1, replica_groups=mesh['yh'=2,'z2'=2,'z1'=2,'z0'=2,'x'=4,'yl'=4,'core'=2] {'x'}, dimensions={0} | all-to-all | bytes 1179648 | tf_op jit(solution)/shard_map/cond/branch_1_fun/all_to_all | solution.py:261
  45.8 0.0 copy-done.1
  45.8 0.7 shard_map.75
  46.5 0.0 copy-start.2
  46.5 0.0 copy-start.3
  46.6 15.4 %conditional.8 = (bf16[64,3,4,128]{3,2,1,0:T(4,128)(2,1)S(1)}) conditional(s32[]{:T(128)} %convert_element_type.2, () %tuple.44, bf16[64,3,4,128]{3,2,1,0:T(4,128)(2,1)S(1)} %shard_map.75), branch_computations={%region_4.0_spmd, %region_5.0_spmd} | conditional | bytes 393224 | solution.py:261
  46.6 15.4 %all_to_all.26 = bf16[64,3,4,128]{3,2,1,0:T(4,128)(2,1)S(1)} all-to-all(bf16[64,3,4,128]{3,2,1,0:T(4,128)(2,1)S(1)} %param.5), channel_id=1, replica_groups=mesh['yh'=2,'z2'=2,'z1'=2,'z0'=2,'x'=4,'yl'=4,'core'=2] {'yl','z1','yh',..., dimensions={0} | all-to-all | bytes 393216 | tf_op jit(solution)/shard_map/cond/branch_1_fun/all_to_all | solution.py:261
  62.0 0.0 copy-done.2
  62.0 0.0 copy-done.3
  62.0 1.4 %shard_map.76 = (bf16[64,9,2,128]{3,2,1,0:T(2,128)(2,1)S(1)}, bf16[576,128]{1,0:T(8,128)(2,1)S(1)}, f32[576,128]{1,0:T(8,128)S(1)}) custom-call(bf16[64,3,4,128]{3,2,1,0:T(4,128)(2,1)S(1)} %get-tuple-element.51.arrived_ref, bf16[2,6,48,128]{3,2,1,0:T(8,128)(2,1)S(1)} %bitcast.2, f32[576,128]{1,0:T(8,128)S(1)} %get-tuple-element.42.gate_ref, ...), custom_call_target="tpu_custom_call" | custom-call | flops 20000000 | bytes 1000000 | tf_op jit(solution)/shard_map/pallas_call | solution.py:287
  63.4 16.3 %conditional.9 = (bf16[64,9,2,128]{3,2,1,0:T(2,128)(2,1)S(1)}) conditional(s32[]{:T(128)} %convert_element_type.2, () %tuple.43, bf16[64,9,2,128]{3,2,1,0:T(2,128)(2,1)S(1)} %get-tuple-element.44), branch_computations={%region_6.0_spmd, %region_7.0_spmd} | conditional | bytes 589832 | solution.py:261
  63.4 16.3 %all_to_all.27 = bf16[64,9,2,128]{3,2,1,0:T(2,128)(2,1)S(1)} all-to-all(bf16[64,9,2,128]{3,2,1,0:T(2,128)(2,1)S(1)} %param.7), channel_id=1, replica_groups=mesh['yh'=2,'z2'=2,'z1'=2,'z0'=2,'x'=4,'yl'=4,'core'=2] {'yl','z1','yh',..., dimensions={0} | all-to-all | bytes 589824 | tf_op jit(solution)/shard_map/cond/branch_1_fun/all_to_all | solution.py:261
  79.7 0.9 shard_map.77
  80.5 9.7 %conditional.10 = (bf16[4,192,384]{2,1,0:T(8,128)(2,1)S(1)}) conditional(s32[]{:T(128)} %convert_element_type.2, () %tuple.42, bf16[4,192,384]{2,1,0:T(8,128)(2,1)S(1)} %shard_map.77), branch_computations={%region_8.0_spmd, %region_9.0_spmd} | conditional | bytes 1179656 | solution.py:261
  80.6 9.7 %all_to_all.28 = bf16[4,192,384]{2,1,0:T(8,128)(2,1)S(1)} all-to-all(bf16[4,192,384]{2,1,0:T(8,128)(2,1)S(1)} %param.9), channel_id=1, replica_groups=mesh['yh'=2,'z2'=2,'z1'=2,'z0'=2,'x'=4,'yl'=4,'core'=2] {'x'}, dimensions={0} | all-to-all | bytes 1179648 | tf_op jit(solution)/shard_map/cond/branch_1_fun/all_to_all | solution.py:261
  90.2 0.5 shard_map.78
  90.7 15.4 %conditional.11 = (bf16[64,3,4,128]{3,2,1,0:T(4,128)(2,1)S(1)}) conditional(s32[]{:T(128)} %convert_element_type.2, () %tuple.41, bf16[64,3,4,128]{3,2,1,0:T(4,128)(2,1)S(1)} %shard_map.78), branch_computations={%region_10.0_spmd, %region_11.0_spmd} | conditional | bytes 393224 | solution.py:261
  90.7 15.4 %all_to_all.29 = bf16[64,3,4,128]{3,2,1,0:T(4,128)(2,1)S(1)} all-to-all(bf16[64,3,4,128]{3,2,1,0:T(4,128)(2,1)S(1)} %param.11), channel_id=1, replica_groups=mesh['yh'=2,'z2'=2,'z1'=2,'z0'=2,'x'=4,'yl'=4,'core'=2] {'yl','z1','yh',..., dimensions={0} | all-to-all | bytes 393216 | tf_op jit(solution)/shard_map/cond/branch_1_fun/all_to_all | solution.py:261
  106.1 0.5 shard_map.79
  106.6 1.9 %all-gather.1 = bf16[12,48,128]{2,1,0:T(8,128)(2,1)S(1)} all-gather(bf16[6,48,128]{2,1,0:T(8,128)(2,1)S(1)} %get-tuple-element.48), channel_id=3, replica_groups=mesh['yh'=2,'z2'=2,'z1'=2,'z0'=2,'x'=4,'yl'=4,'core'=2] {'core'}, dimensions={0}, use_global_device_ids=true | all-gather | bytes 221184 | tf_op jit(solution)/shard_map/all_gather | solution.py:297
  108.5 0.6 slice_select_fusion
Async XLA Ops:
  10.4 23.5 %copy-start = (bf16[512,384]{1,0:T(8,128)(2,1)S(1)}, bf16[512,384]{1,0:T(8,128)(2,1)}, u32[]{:S(2)}) copy-start(bf16[512,384]{1,0:T(8,128)(2,1)} %constant.22.clone.squeeze_ref) | copy-start | bytes 1179652
  34.5 11.3 %copy-start.1 = (bf16[384,512]{1,0:T(8,128)(2,1)S(1)}, bf16[384,512]{1,0:T(8,128)(2,1)}, u32[]{:S(2)}) copy-start(bf16[384,512]{1,0:T(8,128)(2,1)} %constant.23.clone.stretch_ref) | copy-start | bytes 1179652
  46.5 15.4 %copy-start.2 = (bf16[2,128,640]{2,1,0:T(8,128)(2,1)S(1)}, bf16[2,128,640]{2,1,0:T(8,128)(2,1)}, u32[]{:S(2)}) copy-start(bf16[2,128,640]{2,1,0:T(8,128)(2,1)} %weight_ref.1) | copy-start | bytes 983044
  46.5 15.4 %copy-start.3 = (bf16[2,128,128]{2,1,0:T(8,128)(2,1)S(1)}, bf16[2,128,128]{2,1,0:T(8,128)(2,1)}, u32[]{:S(2)}) copy-start(bf16[2,128,128]{2,1,0:T(8,128)(2,1)} %out_weight_ref.3) | copy-start | bytes 196612

commit v14 on v10

--- a/solution.py
+++ b/solution.py
@@ -29,13 +29,11 @@
 
 
 def by_device(rows):
-    return jnp.swapaxes(jnp.stack(rows, axis=0), 0, 1)
-
-
-def spread_sides(normed, weight):
-    projected = lax.dot_general(
-        weight[:, : 4 * H], normed, (((0,), (1,)), ((), ())), preferred_element_type=F32
-    )
+    pairs = [jnp.stack(rows[n : n + 2], axis=0) for n in range(0, len(rows), 2)]
+    return jnp.transpose(jnp.stack(pairs, axis=0), (2, 0, 1, 3))
+
+
+def spread_rows(projected):
     rows, ends = [], []
     for side in range(2):
         value = projected[2 * side * H : (2 * side + 1) * H]
@@ -46,7 +44,19 @@
             rows.extend([part[:, :H], part[:, H : 2 * H]])
             ends.append(part[:, 2 * H :])
     rows.extend([jnp.concatenate(ends, axis=1), jnp.zeros((HALF, H), F32)])
-    return by_device(rows).reshape(HALF, 5, 2, H).astype(BF16)
+    return by_device(rows).astype(BF16)
+
+
+def spread_sides(normed, weight):
+    return spread_rows(
+        lax.dot_general(weight[:, : 4 * H], normed, (((0,), (1,)), ((), ())), preferred_element_type=F32)
+    )
+
+
+def spread_turned(normed, weight):
+    return spread_rows(
+        lax.dot_general(weight[:, : 4 * H], normed, (((0,), (0,)), ((), ())), preferred_element_type=F32)
+    )
 
 
 def gate_of(normed, weight):
@@ -58,9 +68,30 @@
     return jnp.concatenate([jnp.concatenate([by_row[t], by_row[3 + t]], axis=0) for t in range(3)], axis=1)
 
 
+def column(gain):
+    return jnp.swapaxes(jnp.broadcast_to(gain, (8, H)), 0, 1)[:, :1]
+
+
+def moved(tile, lanes):
+    return pltpu.roll(tile, lanes % H, 1) if lanes % H else tile
+
+
+def closed_up(summed):
+    lane = lax.broadcasted_iota(jnp.int32, (H, H), 1)
+    tiles = [summed[:, t * H : (t + 1) * H] for t in range(3)]
+
+    def piece(a, out):
+        return moved(tiles[a // 2], 48 * a - HALF * (a % 2) - H * out)
+
+    begin = jnp.where(lane < 48, piece(0, 0), jnp.where(lane < 96, piece(1, 0), piece(2, 0)))
+    middle = jnp.where(
+        lane < 16, piece(2, 1), jnp.where(lane < 64, piece(3, 1), jnp.where(lane < 112, piece(4, 1), piece(5, 1)))
+    )
+    return jnp.concatenate([begin, middle, piece(5, 2)[:, :32]], axis=1)
+
+
 def finish(summed, field, gating, weight, gain):
-    column = jnp.swapaxes(jnp.broadcast_to(gain, (8, H)), 0, 1)[:, :1]
-    mixed = normalize(summed, column, 0).astype(BF16)
+    mixed = normalize(summed, column(gain), 0).astype(BF16)
     update = lax.dot_general(
         mixed, weight, (((0,), (0,)), ((), ())), preferred_element_type=F32
     )
@@ -70,10 +101,6 @@
 
 def rows_of(own):
     return jnp.swapaxes(own.astype(F32).reshape(HALF, 10, H), 0, 1)
-
-
-def moved(tile, lanes):
-    return pltpu.roll(tile, lanes % H, 1) if lanes % H else tile
 
 
 def matrix(by_row, side, channel):
@@ -127,7 +154,7 @@
                 ]
                 parts.extend(halves(*pair))
             rows.append(jnp.concatenate(parts, axis=0))
-    return by_device(rows).reshape(HALF, 3, 2, H).astype(BF16)
+    return by_device(rows).astype(BF16)
 
 
 def start_kernel(pair_ref, weight_ref, gain_ref, out_ref, gate_ref):
@@ -166,30 +193,36 @@
 def middle_kernel(
     arrived_ref, field_ref, gate_ref, out_weight_ref, weight_ref, gain_ref, out_ref, first_ref, next_gate_ref
 ):
-    first = finish(
-        summed_rows(arrived_ref[...]), field_ref[...].reshape(288, H), gate_ref[...], out_weight_ref[0], gain_ref[2:3]
+    field = jnp.swapaxes(field_ref[...].reshape(288, H).astype(F32), 0, 1)
+    gating = jnp.swapaxes(gate_ref[...], 0, 1)
+    mixed = normalize(closed_up(summed_rows(arrived_ref[...])), column(gain_ref[2:3]), 0).astype(BF16)
+    update = lax.dot_general(out_weight_ref[0], mixed, (((0,), (0,)), ((), ())), preferred_element_type=F32)
+    first = (field + gating * update).astype(BF16).astype(F32)
+    normed = normalize(first, column(gain_ref[1:2]), 0).astype(BF16)
+    weight = weight_ref[1]
+    out_ref[...] = spread_turned(normed, weight)
+    first_ref[...] = jnp.swapaxes(first, 0, 1).reshape(6, 48, H).astype(BF16)
+    next_gate_ref[...] = jax.nn.sigmoid(
+        lax.dot_general(normed, weight[:, 4 * H :], (((0,), (0,)), ((), ())), preferred_element_type=F32)
+    )
+
+
+def incoming_kernel(both_ref, squeeze_ref, stretch_ref, out_ref):
+    cores = [rows_of(both_ref[core]) for core in range(2)]
+    own = jnp.where(lax.axis_index("core") == 0, *cores)
+    none = jnp.zeros((96, 256), F32)
+    left, right = [], []
+    for channel in range(2):
+        left.extend(whole_matrix(cores, 0, channel))
+        part = jnp.concatenate(matrix(own, 1, channel), axis=0)
+        right.append(jnp.concatenate([none, part] if channel else [part, none], axis=1))
+    left = lax.dot_general(
+        stretch_ref[...],
+        jnp.concatenate(left, axis=0).astype(BF16),
+        (((1,), (1,)), ((), ())),
+        preferred_element_type=F32,
     ).astype(BF16)
-    normed = normalize(first.astype(F32), gain_ref[1:2], 1).astype(BF16)
-    weight = weight_ref[1]
-    out_ref[...] = spread_sides(normed, weight)
-    first_ref[...] = first.reshape(6, 48, H)
-    next_gate_ref[...] = gate_of(normed, weight)
-
-
-def incoming_kernel(own_ref, both_ref, squeeze_ref, out_ref):
-    cores = [rows_of(both_ref[core]) for core in range(2)]
-    own = rows_of(own_ref[...])
-    none = jnp.zeros((96, 256), F32)
-    rows = []
-    for channel in range(2):
-        rows.extend(whole_matrix(cores, 0, channel))
-    for channel in range(2):
-        part = jnp.concatenate(matrix(own, 1, channel), axis=0)
-        rows.append(jnp.concatenate([none, part] if channel else [part, none], axis=1))
-    packed = squeezed(rows, squeeze_ref[...])
-    product = lax.dot_general(
-        packed[:192], packed[192:], (((0,), (0,)), ((), ())), preferred_element_type=F32
-    ).astype(BF16)
+    product = jnp.dot(left, squeezed(right, squeeze_ref[...]), preferred_element_type=F32).astype(BF16)
     for x in range(4):
         for z1 in range(2):
             at = 192 * z1 + 48 * x
@@ -249,7 +282,7 @@
     )
     own = exchange(sent, SPREAD)
     both = lax.all_gather(own, "core", axis=0, tiled=False)
-    [parts] = call(incoming_kernel, [blocks])(own, both, squeeze)
+    [parts] = call(incoming_kernel, [blocks])(both, squeeze, stretch)
     parts = exchange(parts, "x")
     [back] = call(sum_kernel, [results])(parts, stretch)
     arrived = exchange(back, SPREAD)

time: 108 us -> 108 us (level)
  no operation moved by 1% of the time
where the time goes in v14:
time: 108 us; the launch traced here: 107 us
  blocking collectives  101 us (94%)
  Pallas kernels  4.94 us (5%)
    all_to_all x2, blocking collectives, shards(): own = exchange(sent, SPREAD)  43.4 us
    all_to_all x2, blocking collectives, shards(): arrived = exchange(back, SPREAD)  28.6 us
    all_to_all x1, blocking collectives, shards(): right = exchange(right, 'x')  10.4 us
    all_gather x2, blocking collectives, shards(): both = lax.all_gather(own, 'core', axis=0, tiled=False)  9.8 us
    all_to_all x1, blocking collectives, shards(): parts = exchange(parts, 'x')  8.98 us

profile of v14, /device:TPU:1, one launch (start us, length us, event | category | flops | bytes accessed | tf_op | source)
XLA Modules:
  0.0 107.3 jit_solution(2669912704127352483)
XLA Ops:
  0.0 0.0 copy-start.5
  0.0 0.0 copy-start.6
  0.0 0.0 copy-start.3
  0.0 1.0 slice_bitcast_fusion.weight_ref
  1.0 0.0 copy-done.5
  1.0 0.0 copy-done.6
  1.0 0.0 copy-done.3
  1.0 0.6 shard_map.73
  1.6 0.0 copy-start.1
  1.6 28.2 %all_to_all.30 = bf16[64,5,2,128]{3,2,1,0:T(2,128)(2,1)S(1)} all-to-all(bf16[64,5,2,128]{3,2,1,0:T(2,128)(2,1)S(1)} %get-tuple-element.12), channel_id=1, replica_groups=mesh['yh'=2,'z2'=2,'z1'=2,'z0'=2,'x'=4,'yl'=4,'core'=2] {'yl','z1','yh',..., dimensions={0} | all-to-all | bytes 327680 | tf_op jit(solution)/shard_map/all_to_all | solution.py:273
  29.8 4.2 %all-gather = bf16[128,5,2,128]{3,2,1,0:T(2,128)(2,1)S(1)} all-gather(bf16[64,5,2,128]{3,2,1,0:T(2,128)(2,1)S(1)} %all_to_all.30), channel_id=2, replica_groups=mesh['yh'=2,'z2'=2,'z1'=2,'z0'=2,'x'=4,'yl'=4,'core'=2] {'core'}, dimensions={0}, use_global_device_ids=true | all-gather | bytes 491520 | tf_op jit(solution)/shard_map/all_gather | solution.py:274
  34.0 0.0 copy-done.1
  34.0 0.6 shard_map.74
  34.6 0.0 copy-start
  34.6 10.4 %all_to_all.31.right_ref = bf16[4,96,384]{2,1,0:T(8,128)(2,1)S(1)} all-to-all(bf16[4,96,384]{2,1,0:T(8,128)(2,1)S(1)} %get-tuple-element.14), channel_id=1, replica_groups=mesh['yh'=2,'z2'=2,'z1'=2,'z0'=2,'x'=4,'yl'=4,'core'=2] {'x'}, dimensions={0} | all-to-all | bytes 589824 | tf_op jit(solution)/shard_map/all_to_all | solution.py:276
  45.0 0.0 copy-done
  45.0 0.0 copy-start.2
  45.0 0.6 shard_map.75
  45.7 0.0 copy-start.4
  45.7 14.4 %all_to_all.32.arrived_ref = bf16[64,3,2,128]{3,2,1,0:T(2,128)(2,1)S(1)} all-to-all(bf16[64,3,2,128]{3,2,1,0:T(2,128)(2,1)S(1)} %shard_map.75), channel_id=1, replica_groups=mesh['yh'=2,'z2'=2,'z1'=2,'z0'=2,'x'=4,'yl'=4,'core'=2] {'yl','z1','yh',..., dimensions={0} | all-to-all | bytes 196608 | tf_op jit(solution)/shard_map/all_to_all | solution.py:278
  60.1 0.0 copy-done.2
  60.1 0.0 copy-done.4
  60.1 0.9 shard_map.76
  61.0 15.2 %all_to_all.33 = bf16[64,5,2,128]{3,2,1,0:T(2,128)(2,1)S(1)} all-to-all(bf16[64,5,2,128]{3,2,1,0:T(2,128)(2,1)S(1)} %get-tuple-element.16), channel_id=1, replica_groups=mesh['yh'=2,'z2'=2,'z1'=2,'z0'=2,'x'=4,'yl'=4,'core'=2] {'yl','z1','yh',..., dimensions={0} | all-to-all | bytes 327680 | tf_op jit(solution)/shard_map/all_to_all | solution.py:283
  76.2 5.6 %all-gather.1 = bf16[128,5,2,128]{3,2,1,0:T(2,128)(2,1)S(1)} all-gather(bf16[64,5,2,128]{3,2,1,0:T(2,128)(2,1)S(1)} %all_to_all.33), channel_id=3, replica_groups=mesh['yh'=2,'z2'=2,'z1'=2,'z0'=2,'x'=4,'yl'=4,'core'=2] {'core'}, dimensions={0}, use_global_device_ids=true | all-gather | bytes 491520 | tf_op jit(solution)/shard_map/all_gather | solution.py:284
  81.8 0.8 shard_map.77
  82.6 9.0 %all_to_all.34.parts_ref = bf16[4,96,384]{2,1,0:T(8,128)(2,1)S(1)} all-to-all(bf16[4,96,384]{2,1,0:T(8,128)(2,1)S(1)} %shard_map.77), channel_id=1, replica_groups=mesh['yh'=2,'z2'=2,'z1'=2,'z0'=2,'x'=4,'yl'=4,'core'=2] {'x'}, dimensions={0} | all-to-all | bytes 589824 | tf_op jit(solution)/shard_map/all_to_all | solution.py:286
  91.6 0.4 shard_map.78
  92.0 14.3 %all_to_all.35.arrived_ref = bf16[64,3,2,128]{3,2,1,0:T(2,128)(2,1)S(1)} all-to-all(bf16[64,3,2,128]{3,2,1,0:T(2,128)(2,1)S(1)} %shard_map.78), channel_id=1, replica_groups=mesh['yh'=2,'z2'=2,'z1'=2,'z0'=2,'x'=4,'yl'=4,'core'=2] {'yl','z1','yh',..., dimensions={0} | all-to-all | bytes 196608 | tf_op jit(solution)/shard_map/all_to_all | solution.py:288
  106.2 1.0 shard_map.79
  (1 shorter events, 0.0 us)
Async XLA Ops:
  0.0 1.0 copy-start.5
  0.0 1.0 copy-start.6
  0.0 1.0 copy-start.3
  1.6 32.4 %copy-start.1 = (bf16[512,384]{1,0:T(8,128)(2,1)S(1)}, bf16[512,384]{1,0:T(8,128)(2,1)}, u32[]{:S(2)}) copy-start(bf16[512,384]{1,0:T(8,128)(2,1)} %constant.4.clone.squeeze_ref) | copy-start | bytes 1179652
  34.6 10.4 %copy-start = (bf16[384,512]{1,0:T(8,128)(2,1)S(1)}, bf16[384,512]{1,0:T(8,128)(2,1)}, u32[]{:S(2)}) copy-start(bf16[384,512]{1,0:T(8,128)(2,1)} %constant.5.clone.stretch_ref) | copy-start | bytes 1179652
  45.0 15.1 %copy-start.2 = (bf16[2,128,640]{2,1,0:T(8,128)(2,1)S(1)}, bf16[2,128,640]{2,1,0:T(8,128)(2,1)}, u32[]{:S(2)}) copy-start(bf16[2,128,640]{2,1,0:T(8,128)(2,1)} %weight_ref.1) | copy-start | bytes 983044
  45.7 14.4 %copy-start.4 = (bf16[2,128,128]{2,1,0:T(8,128)(2,1)S(1)}, bf16[2,128,128]{2,1,0:T(8,128)(2,1)}, u32[]{:S(2)}) copy-start(bf16[2,128,128]{2,1,0:T(8,128)(2,1)} %out_weight_ref.3) | copy-start | bytes 196612

commit v15 on v14

--- a/solution.py
+++ b/solution.py
@@ -157,12 +157,29 @@
     return by_device(rows).astype(BF16)
 
 
-def start_kernel(pair_ref, weight_ref, gain_ref, out_ref, gate_ref):
+def start_kernel(
+    pair_hbm, weight_hbm, in_gain_hbm, out_gain_hbm,
+    out_ref, gate_ref, gain_ref,
+    pair_ref, weight_ref, in_gain_ref, out_gain_ref, sems,
+):
+    moves = [(in_gain_hbm, in_gain_ref)]
+    moves.extend((pair_hbm.at[n : n + 3], pair_ref.at[n : n + 3]) for n in (0, 3))
+    moves.extend((weight_hbm.at[0, n : n + 32], weight_ref.at[n : n + 32]) for n in range(0, H, 32))
+    moves.append((out_gain_hbm, out_gain_ref))
+    copies = [pltpu.make_async_copy(source, target, sems.at[n]) for n, (source, target) in enumerate(moves)]
+    for copy in copies:
+        copy.start()
+    for copy in copies[:3]:
+        copy.wait()
     field = pair_ref[...].reshape(288, H).astype(F32)
-    normed = normalize(field, gain_ref[0:1], 1).astype(BF16)
+    normed = normalize(field, in_gain_ref[0:1], 1).astype(BF16)
+    for copy in copies[3:]:
+        copy.wait()
     weight = weight_ref[...]
     out_ref[...] = spread_sides(normed, weight)
     gate_ref[...] = gate_of(normed, weight)
+    gain_ref[0:2] = in_gain_ref[...]
+    gain_ref[2:4] = out_gain_ref[...]
 
 
 def pack_kernel(both_ref, squeeze_ref, left_ref, right_ref):
@@ -268,8 +285,22 @@
     sides, results = ((HALF, 5, 2, H), BF16), ((HALF, 3, 2, H), BF16)
     block, blocks = ((192, 384), BF16), ((4, 96, 384), BF16)
 
-    gains = jnp.concatenate([in_gain, out_gain], axis=0)
-    sent, gating = call(start_kernel, [sides, gates])(pair_field, proj_weight[0], gains)
+    held = [
+        pltpu.with_memory_space_constraint(array, pltpu.HBM)
+        for array in (pair_field, proj_weight, in_gain, out_gain)
+    ]
+    sent, gating, gains = call(
+        start_kernel,
+        [sides, gates, ((4, H), F32)],
+        [
+            pltpu.VMEM((6, 48, H), BF16),
+            pltpu.VMEM((H, 5 * H), BF16),
+            pltpu.VMEM((2, H), F32),
+            pltpu.VMEM((2, H), F32),
+            pltpu.SemaphoreType.DMA((8,)),
+        ],
+        in_specs=[pl.BlockSpec(memory_space=pltpu.HBM)] * 4,
+    )(*held)
     own = exchange(sent, SPREAD)
     both = lax.all_gather(own, "core", axis=0, tiled=False)
     left, right = call(pack_kernel, [block, blocks])(both, squeeze)

time: 108 us -> 108 us (level)
  no operation moved by 1% of the time
where the time goes in v15:
time: 108 us; the launch traced here: 107 us
  blocking collectives  101 us (94%)
  Pallas kernels  5.87 us (5%)
    all_to_all x2, blocking collectives, shards(): own = exchange(sent, SPREAD)  43.4 us
    all_to_all x2, blocking collectives, shards(): arrived = exchange(back, SPREAD)  28.6 us
    all_to_all x1, blocking collectives, shards(): right = exchange(right, 'x')  10.4 us
    all_gather x2, blocking collectives, shards(): both = lax.all_gather(own, 'core', axis=0, tiled=False)  9.8 us
    all_to_all x1, blocking collectives, shards(): parts = exchange(parts, 'x')  8.98 us

profile of v15, /device:TPU:1, one launch (start us, length us, event | category | flops | bytes accessed | tf_op | source)
XLA Modules:
  0.0 107.2 jit_solution(238432041340186671)
XLA Ops:
  0.0 1.5 %shard_map.73 = (bf16[64,5,2,128]{3,2,1,0:T(2,128)(2,1)S(1)}, f32[288,128]{1,0:T(8,128)S(1)}, f32[4,128]{1,0:T(4,128)S(1)}) custom-call(bf16[6,48,128]{2,1,0:T(8,128)(2,1)} %field_ref.1, bf16[2,128,640]{2,1,0:T(8,128)(2,1)} %weight_ref.1, f32[2,128]{1,0:T(2,128)} %in_gain_hbm.1, f32[2,128]{1,0:T(2,128)} %out_gain_hbm.1), custom_call_target="tpu_custom_call" | custom-call | flops 20000000 | bytes 1000000 | tf_op jit(solution)/shard_map/pallas_call | solution.py:292
  1.5 0.0 copy-start.1
  1.5 28.2 %all_to_all.30 = bf16[64,5,2,128]{3,2,1,0:T(2,128)(2,1)S(1)} all-to-all(bf16[64,5,2,128]{3,2,1,0:T(2,128)(2,1)S(1)} %get-tuple-element.13), channel_id=1, replica_groups=mesh['yh'=2,'z2'=2,'z1'=2,'z0'=2,'x'=4,'yl'=4,'core'=2] {'yl','z1','yh',..., dimensions={0} | all-to-all | bytes 327680 | tf_op jit(solution)/shard_map/all_to_all | solution.py:304
  29.7 4.2 %all-gather = bf16[128,5,2,128]{3,2,1,0:T(2,128)(2,1)S(1)} all-gather(bf16[64,5,2,128]{3,2,1,0:T(2,128)(2,1)S(1)} %all_to_all.30), channel_id=2, replica_groups=mesh['yh'=2,'z2'=2,'z1'=2,'z0'=2,'x'=4,'yl'=4,'core'=2] {'core'}, dimensions={0}, use_global_device_ids=true | all-gather | bytes 491520 | tf_op jit(solution)/shard_map/all_gather | solution.py:305
  33.9 0.0 copy-done.1
  33.9 0.6 shard_map.74
  34.5 0.0 copy-start
  34.5 10.4 %all_to_all.31.right_ref = bf16[4,96,384]{2,1,0:T(8,128)(2,1)S(1)} all-to-all(bf16[4,96,384]{2,1,0:T(8,128)(2,1)S(1)} %get-tuple-element.15), channel_id=1, replica_groups=mesh['yh'=2,'z2'=2,'z1'=2,'z0'=2,'x'=4,'yl'=4,'core'=2] {'x'}, dimensions={0} | all-to-all | bytes 589824 | tf_op jit(solution)/shard_map/all_to_all | solution.py:307
  44.9 0.0 copy-done
  44.9 0.0 copy-start.2
  44.9 0.6 shard_map.75
  45.6 0.0 copy-start.3
  45.6 0.0 copy-start.4
  45.6 14.4 %all_to_all.32.arrived_ref = bf16[64,3,2,128]{3,2,1,0:T(2,128)(2,1)S(1)} all-to-all(bf16[64,3,2,128]{3,2,1,0:T(2,128)(2,1)S(1)} %shard_map.75), channel_id=1, replica_groups=mesh['yh'=2,'z2'=2,'z1'=2,'z0'=2,'x'=4,'yl'=4,'core'=2] {'yl','z1','yh',..., dimensions={0} | all-to-all | bytes 196608 | tf_op jit(solution)/shard_map/all_to_all | solution.py:309
  60.0 0.0 copy-done.2
  60.0 0.0 copy-done.3
  60.0 0.0 copy-done.4
  60.0 0.9 shard_map.76
  61.0 15.2 %all_to_all.33 = bf16[64,5,2,128]{3,2,1,0:T(2,128)(2,1)S(1)} all-to-all(bf16[64,5,2,128]{3,2,1,0:T(2,128)(2,1)S(1)} %get-tuple-element.18), channel_id=1, replica_groups=mesh['yh'=2,'z2'=2,'z1'=2,'z0'=2,'x'=4,'yl'=4,'core'=2] {'yl','z1','yh',..., dimensions={0} | all-to-all | bytes 327680 | tf_op jit(solution)/shard_map/all_to_all | solution.py:314
  76.1 5.6 %all-gather.1 = bf16[128,5,2,128]{3,2,1,0:T(2,128)(2,1)S(1)} all-gather(bf16[64,5,2,128]{3,2,1,0:T(2,128)(2,1)S(1)} %all_to_all.33), channel_id=3, replica_groups=mesh['yh'=2,'z2'=2,'z1'=2,'z0'=2,'x'=4,'yl'=4,'core'=2] {'core'}, dimensions={0}, use_global_device_ids=true | all-gather | bytes 491520 | tf_op jit(solution)/shard_map/all_gather | solution.py:315
  81.7 0.8 shard_map.77
  82.5 9.0 %all_to_all.34.parts_ref = bf16[4,96,384]{2,1,0:T(8,128)(2,1)S(1)} all-to-all(bf16[4,96,384]{2,1,0:T(8,128)(2,1)S(1)} %shard_map.77), channel_id=1, replica_groups=mesh['yh'=2,'z2'=2,'z1'=2,'z0'=2,'x'=4,'yl'=4,'core'=2] {'x'}, dimensions={0} | all-to-all | bytes 589824 | tf_op jit(solution)/shard_map/all_to_all | solution.py:317
  91.5 0.4 shard_map.78
  91.9 14.3 %all_to_all.35.arrived_ref = bf16[64,3,2,128]{3,2,1,0:T(2,128)(2,1)S(1)} all-to-all(bf16[64,3,2,128]{3,2,1,0:T(2,128)(2,1)S(1)} %shard_map.78), channel_id=1, replica_groups=mesh['yh'=2,'z2'=2,'z1'=2,'z0'=2,'x'=4,'yl'=4,'core'=2] {'yl','z1','yh',..., dimensions={0} | all-to-all | bytes 196608 | tf_op jit(solution)/shard_map/all_to_all | solution.py:319
  106.1 1.1 shard_map.79
Async XLA Ops:
  1.5 32.4 %copy-start.1 = (bf16[512,384]{1,0:T(8,128)(2,1)S(1)}, bf16[512,384]{1,0:T(8,128)(2,1)}, u32[]{:S(2)}) copy-start(bf16[512,384]{1,0:T(8,128)(2,1)} %constant.4.clone.squeeze_ref) | copy-start | bytes 1179652
  34.5 10.4 %copy-start = (bf16[384,512]{1,0:T(8,128)(2,1)S(1)}, bf16[384,512]{1,0:T(8,128)(2,1)}, u32[]{:S(2)}) copy-start(bf16[384,512]{1,0:T(8,128)(2,1)} %constant.5.clone.stretch_ref) | copy-start | bytes 1179652
  44.9 15.1 %copy-start.2 = (bf16[2,128,640]{2,1,0:T(8,128)(2,1)S(1)}, bf16[2,128,640]{2,1,0:T(8,128)(2,1)}, u32[]{:S(2)}) copy-start(bf16[2,128,640]{2,1,0:T(8,128)(2,1)} %weight_ref.1) | copy-start | bytes 983044
  45.6 14.4 %copy-start.3 = (bf16[6,48,128]{2,1,0:T(8,128)(2,1)S(1)}, bf16[6,48,128]{2,1,0:T(8,128)(2,1)}, u32[]{:S(2)}) copy-start(bf16[6,48,128]{2,1,0:T(8,128)(2,1)} %field_ref.1) | copy-start | bytes 221188
  45.6 14.4 %copy-start.4 = (bf16[2,128,128]{2,1,0:T(8,128)(2,1)S(1)}, bf16[2,128,128]{2,1,0:T(8,128)(2,1)}, u32[]{:S(2)}) copy-start(bf16[2,128,128]{2,1,0:T(8,128)(2,1)} %out_weight_ref.3) | copy-start | bytes 196612

commit v16 on v14

--- a/solution.py
+++ b/solution.py
@@ -210,19 +210,17 @@
 def incoming_kernel(both_ref, squeeze_ref, stretch_ref, out_ref):
     cores = [rows_of(both_ref[core]) for core in range(2)]
     own = jnp.where(lax.axis_index("core") == 0, *cores)
-    none = jnp.zeros((96, 256), F32)
     left, right = [], []
     for channel in range(2):
         left.extend(whole_matrix(cores, 0, channel))
-        part = jnp.concatenate(matrix(own, 1, channel), axis=0)
-        right.append(jnp.concatenate([none, part] if channel else [part, none], axis=1))
+        right.append(squeezed(matrix(own, 1, channel), squeeze_ref[256 * channel : 256 * channel + 256]))
     left = lax.dot_general(
         stretch_ref[...],
         jnp.concatenate(left, axis=0).astype(BF16),
         (((1,), (1,)), ((), ())),
         preferred_element_type=F32,
     ).astype(BF16)
-    product = jnp.dot(left, squeezed(right, squeeze_ref[...]), preferred_element_type=F32).astype(BF16)
+    product = jnp.dot(left, jnp.concatenate(right, axis=0), preferred_element_type=F32).astype(BF16)
     for x in range(4):
         for z1 in range(2):
             at = 192 * z1 + 48 * x

time: 108 us -> 108 us (level)
  no operation moved by 1% of the time
where the time goes in v16:
time: 108 us; the launch traced here: 107 us
  blocking collectives  101 us (94%)
  Pallas kernels  5.05 us (5%)
    all_to_all x2, blocking collectives, shards(): own = exchange(sent, SPREAD)  43.4 us
    all_to_all x2, blocking collectives, shards(): arrived = exchange(back, SPREAD)  28.6 us
    all_to_all x1, blocking collectives, shards(): right = exchange(right, 'x')  10.4 us
    all_gather x2, blocking collectives, shards(): both = lax.all_gather(own, 'core', axis=0, tiled=False)  9.8 us
    all_to_all x1, blocking collectives, shards(): parts = exchange(parts, 'x')  8.98 us

profile of v16, /device:TPU:1, one launch (start us, length us, event | category | flops | bytes accessed | tf_op | source)
XLA Modules:
  0.0 107.4 jit_solution(13562581014082981597)
XLA Ops:
  0.0 0.0 copy-start.5
  0.0 0.0 copy-start.6
  0.0 0.0 copy-start.3
  0.0 1.0 slice_bitcast_fusion.weight_ref
  1.0 0.0 copy-done.5
  1.0 0.0 copy-done.6
  1.0 0.0 copy-done.3
  1.0 0.6 shard_map.73
  1.6 0.0 copy-start.1
  1.6 28.2 %all_to_all.30 = bf16[64,5,2,128]{3,2,1,0:T(2,128)(2,1)S(1)} all-to-all(bf16[64,5,2,128]{3,2,1,0:T(2,128)(2,1)S(1)} %get-tuple-element.12), channel_id=1, replica_groups=mesh['yh'=2,'z2'=2,'z1'=2,'z0'=2,'x'=4,'yl'=4,'core'=2] {'yl','z1','yh',..., dimensions={0} | all-to-all | bytes 327680 | tf_op jit(solution)/shard_map/all_to_all | solution.py:271
  29.8 4.2 %all-gather = bf16[128,5,2,128]{3,2,1,0:T(2,128)(2,1)S(1)} all-gather(bf16[64,5,2,128]{3,2,1,0:T(2,128)(2,1)S(1)} %all_to_all.30), channel_id=2, replica_groups=mesh['yh'=2,'z2'=2,'z1'=2,'z0'=2,'x'=4,'yl'=4,'core'=2] {'core'}, dimensions={0}, use_global_device_ids=true | all-gather | bytes 491520 | tf_op jit(solution)/shard_map/all_gather | solution.py:272
  34.0 0.0 copy-done.1
  34.0 0.6 shard_map.74
  34.6 0.0 copy-start
  34.6 10.4 %all_to_all.31.right_ref = bf16[4,96,384]{2,1,0:T(8,128)(2,1)S(1)} all-to-all(bf16[4,96,384]{2,1,0:T(8,128)(2,1)S(1)} %get-tuple-element.14), channel_id=1, replica_groups=mesh['yh'=2,'z2'=2,'z1'=2,'z0'=2,'x'=4,'yl'=4,'core'=2] {'x'}, dimensions={0} | all-to-all | bytes 589824 | tf_op jit(solution)/shard_map/all_to_all | solution.py:274
  45.0 0.0 copy-done
  45.0 0.0 copy-start.2
  45.0 0.6 shard_map.75
  45.7 0.0 copy-start.4
  45.7 14.4 %all_to_all.32.arrived_ref = bf16[64,3,2,128]{3,2,1,0:T(2,128)(2,1)S(1)} all-to-all(bf16[64,3,2,128]{3,2,1,0:T(2,128)(2,1)S(1)} %shard_map.75), channel_id=1, replica_groups=mesh['yh'=2,'z2'=2,'z1'=2,'z0'=2,'x'=4,'yl'=4,'core'=2] {'yl','z1','yh',..., dimensions={0} | all-to-all | bytes 196608 | tf_op jit(solution)/shard_map/all_to_all | solution.py:276
  60.1 0.0 copy-done.2
  60.1 0.0 copy-done.4
  60.1 0.9 shard_map.76
  61.0 15.2 %all_to_all.33 = bf16[64,5,2,128]{3,2,1,0:T(2,128)(2,1)S(1)} all-to-all(bf16[64,5,2,128]{3,2,1,0:T(2,128)(2,1)S(1)} %get-tuple-element.16), channel_id=1, replica_groups=mesh['yh'=2,'z2'=2,'z1'=2,'z0'=2,'x'=4,'yl'=4,'core'=2] {'yl','z1','yh',..., dimensions={0} | all-to-all | bytes 327680 | tf_op jit(solution)/shard_map/all_to_all | solution.py:281
  76.2 5.6 %all-gather.1 = bf16[128,5,2,128]{3,2,1,0:T(2,128)(2,1)S(1)} all-gather(bf16[64,5,2,128]{3,2,1,0:T(2,128)(2,1)S(1)} %all_to_all.33), channel_id=3, replica_groups=mesh['yh'=2,'z2'=2,'z1'=2,'z0'=2,'x'=4,'yl'=4,'core'=2] {'core'}, dimensions={0}, use_global_device_ids=true | all-gather | bytes 491520 | tf_op jit(solution)/shard_map/all_gather | solution.py:282
  81.8 0.9 shard_map.77
  82.7 9.0 %all_to_all.34.parts_ref = bf16[4,96,384]{2,1,0:T(8,128)(2,1)S(1)} all-to-all(bf16[4,96,384]{2,1,0:T(8,128)(2,1)S(1)} %shard_map.77), channel_id=1, replica_groups=mesh['yh'=2,'z2'=2,'z1'=2,'z0'=2,'x'=4,'yl'=4,'core'=2] {'x'}, dimensions={0} | all-to-all | bytes 589824 | tf_op jit(solution)/shard_map/all_to_all | solution.py:284
  91.7 0.4 shard_map.78
  92.1 14.3 %all_to_all.35.arrived_ref = bf16[64,3,2,128]{3,2,1,0:T(2,128)(2,1)S(1)} all-to-all(bf16[64,3,2,128]{3,2,1,0:T(2,128)(2,1)S(1)} %shard_map.78), channel_id=1, replica_groups=mesh['yh'=2,'z2'=2,'z1'=2,'z0'=2,'x'=4,'yl'=4,'core'=2] {'yl','z1','yh',..., dimensions={0} | all-to-all | bytes 196608 | tf_op jit(solution)/shard_map/all_to_all | solution.py:286
  106.3 1.0 shard_map.79
  (1 shorter events, 0.0 us)
Async XLA Ops:
  0.0 1.0 copy-start.5
  0.0 1.0 copy-start.6
  0.0 1.0 copy-start.3
  1.6 32.4 %copy-start.1 = (bf16[512,384]{1,0:T(8,128)(2,1)S(1)}, bf16[512,384]{1,0:T(8,128)(2,1)}, u32[]{:S(2)}) copy-start(bf16[512,384]{1,0:T(8,128)(2,1)} %constant.4.clone.squeeze_ref) | copy-start | bytes 1179652
  34.6 10.4 %copy-start = (bf16[384,512]{1,0:T(8,128)(2,1)S(1)}, bf16[384,512]{1,0:T(8,128)(2,1)}, u32[]{:S(2)}) copy-start(bf16[384,512]{1,0:T(8,128)(2,1)} %constant.5.clone.stretch_ref) | copy-start | bytes 1179652
  45.0 15.1 %copy-start.2 = (bf16[2,128,640]{2,1,0:T(8,128)(2,1)S(1)}, bf16[2,128,640]{2,1,0:T(8,128)(2,1)}, u32[]{:S(2)}) copy-start(bf16[2,128,640]{2,1,0:T(8,128)(2,1)} %weight_ref.1) | copy-start | bytes 983044
  45.7 14.4 %copy-start.4 = (bf16[2,128,128]{2,1,0:T(8,128)(2,1)S(1)}, bf16[2,128,128]{2,1,0:T(8,128)(2,1)}, u32[]{:S(2)}) copy-start(bf16[2,128,128]{2,1,0:T(8,128)(2,1)} %out_weight_ref.3) | copy-start | bytes 196612

commit v17 on v14

--- a/solution.py
+++ b/solution.py
@@ -47,20 +47,10 @@
     return by_device(rows).astype(BF16)
 
 
-def spread_sides(normed, weight):
-    return spread_rows(
-        lax.dot_general(weight[:, : 4 * H], normed, (((0,), (1,)), ((), ())), preferred_element_type=F32)
-    )
-
-
 def spread_turned(normed, weight):
     return spread_rows(
         lax.dot_general(weight[:, : 4 * H], normed, (((0,), (0,)), ((), ())), preferred_element_type=F32)
     )
-
-
-def gate_of(normed, weight):
-    return jax.nn.sigmoid(jnp.dot(normed, weight[:, 4 * H :], preferred_element_type=F32))
 
 
 def summed_rows(arrived):
@@ -160,9 +150,11 @@
 def start_kernel(pair_ref, weight_ref, gain_ref, out_ref, gate_ref):
     field = pair_ref[...].reshape(288, H).astype(F32)
     normed = normalize(field, gain_ref[0:1], 1).astype(BF16)
-    weight = weight_ref[...]
-    out_ref[...] = spread_sides(normed, weight)
-    gate_ref[...] = gate_of(normed, weight)
+    projected = lax.dot_general(
+        weight_ref[...], normed, (((0,), (1,)), ((), ())), preferred_element_type=F32
+    )
+    out_ref[...] = spread_rows(projected[: 4 * H])
+    gate_ref[...] = jax.nn.sigmoid(projected[4 * H :])
 
 
 def pack_kernel(both_ref, squeeze_ref, left_ref, right_ref):
@@ -194,10 +186,9 @@
     arrived_ref, field_ref, gate_ref, out_weight_ref, weight_ref, gain_ref, out_ref, first_ref, next_gate_ref
 ):
     field = jnp.swapaxes(field_ref[...].reshape(288, H).astype(F32), 0, 1)
-    gating = jnp.swapaxes(gate_ref[...], 0, 1)
     mixed = normalize(closed_up(summed_rows(arrived_ref[...])), column(gain_ref[2:3]), 0).astype(BF16)
     update = lax.dot_general(out_weight_ref[0], mixed, (((0,), (0,)), ((), ())), preferred_element_type=F32)
-    first = (field + gating * update).astype(BF16).astype(F32)
+    first = (field + gate_ref[...] * update).astype(BF16).astype(F32)
     normed = normalize(first, column(gain_ref[1:2]), 0).astype(BF16)
     weight = weight_ref[1]
     out_ref[...] = spread_turned(normed, weight)
@@ -269,7 +260,7 @@
     block, blocks = ((192, 384), BF16), ((4, 96, 384), BF16)
 
     gains = jnp.concatenate([in_gain, out_gain], axis=0)
-    sent, gating = call(start_kernel, [sides, gates])(pair_field, proj_weight[0], gains)
+    sent, gating = call(start_kernel, [sides, ((H, 288), F32)])(pair_field, proj_weight[0], gains)
     own = exchange(sent, SPREAD)
     both = lax.all_gather(own, "core", axis=0, tiled=False)
     left, right = call(pack_kernel, [block, blocks])(both, squeeze)

time: 108 us -> 108 us (level)
  no operation moved by 1% of the time
where the time goes in v17:
time: 108 us; the launch traced here: 107 us
  blocking collectives  101 us (94%)
  Pallas kernels  4.95 us (5%)
    all_to_all x2, blocking collectives, shards(): own = exchange(sent, SPREAD)  43.4 us
    all_to_all x2, blocking collectives, shards(): arrived = exchange(back, SPREAD)  28.7 us
    all_to_all x1, blocking collectives, shards(): right = exchange(right, 'x')  10.4 us
    all_gather x2, blocking collectives, shards(): both = lax.all_gather(own, 'core', axis=0, tiled=False)  9.8 us
    all_to_all x1, blocking collectives, shards(): parts = exchange(parts, 'x')  8.98 us

profile of v17, /device:TPU:1, one launch (start us, length us, event | category | flops | bytes accessed | tf_op | source)
XLA Modules:
  0.0 107.3 jit_solution(13976625208578550131)
XLA Ops:
  0.0 0.0 copy-start.5
  0.0 0.0 copy-start.6
  0.0 0.0 copy-start.3
  0.0 1.0 slice_bitcast_fusion.weight_ref
  1.0 0.0 copy-done.5
  1.0 0.0 copy-done.6
  1.0 0.0 copy-done.3
  1.0 0.6 shard_map.73
  1.6 0.0 copy-start.1
  1.6 28.2 %all_to_all.30 = bf16[64,5,2,128]{3,2,1,0:T(2,128)(2,1)S(1)} all-to-all(bf16[64,5,2,128]{3,2,1,0:T(2,128)(2,1)S(1)} %get-tuple-element.12), channel_id=1, replica_groups=mesh['yh'=2,'z2'=2,'z1'=2,'z0'=2,'x'=4,'yl'=4,'core'=2] {'yl','z1','yh',..., dimensions={0} | all-to-all | bytes 327680 | tf_op jit(solution)/shard_map/all_to_all | solution.py:264
  29.9 4.2 %all-gather = bf16[128,5,2,128]{3,2,1,0:T(2,128)(2,1)S(1)} all-gather(bf16[64,5,2,128]{3,2,1,0:T(2,128)(2,1)S(1)} %all_to_all.30), channel_id=2, replica_groups=mesh['yh'=2,'z2'=2,'z1'=2,'z0'=2,'x'=4,'yl'=4,'core'=2] {'core'}, dimensions={0}, use_global_device_ids=true | all-gather | bytes 491520 | tf_op jit(solution)/shard_map/all_gather | solution.py:265
  34.0 0.0 copy-done.1
  34.0 0.6 shard_map.74
  34.6 0.0 copy-start
  34.6 10.4 %all_to_all.31.right_ref = bf16[4,96,384]{2,1,0:T(8,128)(2,1)S(1)} all-to-all(bf16[4,96,384]{2,1,0:T(8,128)(2,1)S(1)} %get-tuple-element.14), channel_id=1, replica_groups=mesh['yh'=2,'z2'=2,'z1'=2,'z0'=2,'x'=4,'yl'=4,'core'=2] {'x'}, dimensions={0} | all-to-all | bytes 589824 | tf_op jit(solution)/shard_map/all_to_all | solution.py:267
  45.0 0.0 copy-done
  45.0 0.0 copy-start.2
  45.0 0.6 shard_map.75
  45.7 0.0 copy-start.4
  45.7 14.4 %all_to_all.32.arrived_ref = bf16[64,3,2,128]{3,2,1,0:T(2,128)(2,1)S(1)} all-to-all(bf16[64,3,2,128]{3,2,1,0:T(2,128)(2,1)S(1)} %shard_map.75), channel_id=1, replica_groups=mesh['yh'=2,'z2'=2,'z1'=2,'z0'=2,'x'=4,'yl'=4,'core'=2] {'yl','z1','yh',..., dimensions={0} | all-to-all | bytes 196608 | tf_op jit(solution)/shard_map/all_to_all | solution.py:269
  60.1 0.0 copy-done.2
  60.1 0.0 copy-done.4
  60.1 0.9 shard_map.76
  61.0 15.2 %all_to_all.33 = bf16[64,5,2,128]{3,2,1,0:T(2,128)(2,1)S(1)} all-to-all(bf16[64,5,2,128]{3,2,1,0:T(2,128)(2,1)S(1)} %get-tuple-element.16), channel_id=1, replica_groups=mesh['yh'=2,'z2'=2,'z1'=2,'z0'=2,'x'=4,'yl'=4,'core'=2] {'yl','z1','yh',..., dimensions={0} | all-to-all | bytes 327680 | tf_op jit(solution)/shard_map/all_to_all | solution.py:274
  76.2 5.6 %all-gather.1 = bf16[128,5,2,128]{3,2,1,0:T(2,128)(2,1)S(1)} all-gather(bf16[64,5,2,128]{3,2,1,0:T(2,128)(2,1)S(1)} %all_to_all.33), channel_id=3, replica_groups=mesh['yh'=2,'z2'=2,'z1'=2,'z0'=2,'x'=4,'yl'=4,'core'=2] {'core'}, dimensions={0}, use_global_device_ids=true | all-gather | bytes 491520 | tf_op jit(solution)/shard_map/all_gather | solution.py:275
  81.8 0.8 shard_map.77
  82.6 9.0 %all_to_all.34.parts_ref = bf16[4,96,384]{2,1,0:T(8,128)(2,1)S(1)} all-to-all(bf16[4,96,384]{2,1,0:T(8,128)(2,1)S(1)} %shard_map.77), channel_id=1, replica_groups=mesh['yh'=2,'z2'=2,'z1'=2,'z0'=2,'x'=4,'yl'=4,'core'=2] {'x'}, dimensions={0} | all-to-all | bytes 589824 | tf_op jit(solution)/shard_map/all_to_all | solution.py:277
  91.6 0.4 shard_map.78
  92.0 14.3 %all_to_all.35.arrived_ref = bf16[64,3,2,128]{3,2,1,0:T(2,128)(2,1)S(1)} all-to-all(bf16[64,3,2,128]{3,2,1,0:T(2,128)(2,1)S(1)} %shard_map.78), channel_id=1, replica_groups=mesh['yh'=2,'z2'=2,'z1'=2,'z0'=2,'x'=4,'yl'=4,'core'=2] {'yl','z1','yh',..., dimensions={0} | all-to-all | bytes 196608 | tf_op jit(solution)/shard_map/all_to_all | solution.py:279
  106.2 1.0 shard_map.79
  (1 shorter events, 0.0 us)
Async XLA Ops:
  0.0 1.0 copy-start.5
  0.0 1.0 copy-start.6
  0.0 1.0 copy-start.3
  1.6 32.4 %copy-start.1 = (bf16[512,384]{1,0:T(8,128)(2,1)S(1)}, bf16[512,384]{1,0:T(8,128)(2,1)}, u32[]{:S(2)}) copy-start(bf16[512,384]{1,0:T(8,128)(2,1)} %constant.4.clone.squeeze_ref) | copy-start | bytes 1179652
  34.6 10.4 %copy-start = (bf16[384,512]{1,0:T(8,128)(2,1)S(1)}, bf16[384,512]{1,0:T(8,128)(2,1)}, u32[]{:S(2)}) copy-start(bf16[384,512]{1,0:T(8,128)(2,1)} %constant.5.clone.stretch_ref) | copy-start | bytes 1179652
  45.0 15.1 %copy-start.2 = (bf16[2,128,640]{2,1,0:T(8,128)(2,1)S(1)}, bf16[2,128,640]{2,1,0:T(8,128)(2,1)}, u32[]{:S(2)}) copy-start(bf16[2,128,640]{2,1,0:T(8,128)(2,1)} %weight_ref.1) | copy-start | bytes 983044
  45.7 14.4 %copy-start.4 = (bf16[2,128,128]{2,1,0:T(8,128)(2,1)S(1)}, bf16[2,128,128]{2,1,0:T(8,128)(2,1)}, u32[]{:S(2)}) copy-start(bf16[2,128,128]{2,1,0:T(8,128)(2,1)} %out_weight_ref.3) | copy-start | bytes 196612
